TPU v7x, 512 devices: a whole 4x4x16 slice. The times are simulated.
512 devices in a mesh: wide: 64 (over z, y), narrow: 8 (over x, core).
Axes of the slice: x: 4, y: 4, z: 16, core: 2. Of those that a mesh axis runs over, the one named last changes fastest.
Arguments:
- points: float32 [3, 2097152], P(None, ('wide', 'narrow'))
- charges: float32 [2097152], P(('wide', 'narrow')), may hold values from -1.5 to 1.5
- order: int32 [2097152], P(('wide', 'narrow')), may hold values from 0 to 4095, as said below
- source_basis: float32 [32, 2097152], P(None, ('wide', 'narrow')), may hold values from -0.375 to 0.375
- target_basis: float32 [32, 2097152], P(None, ('wide', 'narrow')), may hold values from -1 to 1
- skeleton_points: float32 [3, 262144], P(None, ('wide', 'narrow'))
- transfer: float32 [32, 262144], P(None, ('wide', 'narrow')), may hold values from -3 to 3
- top_points: float32 [3, 2048], P(None, 'wide')
- near_pairs: int32 [2, 32768], P(None, ('wide', 'narrow')), may hold values from 0 to 8191, as said below
- near_count: int32 [512], P(('wide', 'narrow')), may hold values from 16 to 64
- far_pairs: int32 [3, 65536], P(None, ('wide', 'narrow')), may hold values from 0 to 8191, as said below
- far_count: int32 [512], P(('wide', 'narrow')), may hold values from 64 to 128
Outputs:
- potential: float32 [2097152], P(('wide', 'narrow'))
Inputs may be any that keep to these rules, and one draw needn't show every extreme that they name: `order`: within each device's block of 4096 slots, a permutation of 0 to 4095. `near_pairs`: clusters sit on a grid of cells, 8 wide and 16 deep in each group's layer: cluster c has cell (w % 8, w // 8, c // 128) with w = c % 128. Row 0 is a cluster of the device that holds the slot; row 1 is a cluster whose cell is at Chebyshev distance exactly 1 from the target's cell (so it lies in the target's group or the group just before or after it). Only the first near_count slots of a device are used. `far_pairs`: row 0 is a cluster of the device that holds the slot; row 2 is 0 or 1; with 0, row 1 is a cluster of the target's group or of the group just before or after it whose cell is at Chebyshev distance 2 or more from the target's cell; with 1, row 1 is a group two or more groups away from the target's. Only the first far_count slots of a device are used.
All inputs are finite; a program needn't handle non-finite values.
Results may differ from a plain program's by a relative error of at most 0.0003.
Values sent between devices are 32-bit elements; how exact they have to be, the bound alone decides.
No kernel may reach another device: no remote copies, remote signals or barrier semaphores. Data moves between devices by JAX's collectives and lax.ppermute only.
A program may use at most 64 MiB of HBM per device.

v0:
```python
import jax
import jax.numpy as jnp
from jax import lax
from jax.sharding import PartitionSpec as P

C = 256
R = 32


soft_square = 0.01
kernel_scale = 0.07957747154594767
highest = lax.Precision.HIGHEST
pair_block = 8


def padded(x, sides, width):
    for axis, dim in sides:
        count, length = (lax.axis_size(axis), x.shape[dim])
        up = [(i, (i + 1) % count) for i in range(count - 1)]
        down = [(j, i) for i, j in up]
        last = lax.slice_in_dim(x, length - width, length, axis=dim)
        leading = lax.slice_in_dim(x, 0, width, axis=dim)
        before = lax.ppermute(last, axis, up)
        after = lax.ppermute(leading, axis, down)
        x = jnp.concatenate([before, x, after], axis=dim)
    return x


def passed_along(value, axis, steps):
    count = lax.axis_size(axis)
    leading, last = (max(0, -steps), min(count, count - steps))
    return lax.ppermute(value, axis, [(source, source + steps) for source in range(leading, last)])


def kernel_tile(target_xyz, source_xyz):
    offsets = target_xyz[..., :, :, None] - source_xyz[..., :, None, :]
    dist_sq = jnp.sum(offsets * offsets, axis=-3)
    return kernel_scale * lax.rsqrt(dist_sq + soft_square)


def unpack(records):
    xyz_part = records[:, : 3 * C].reshape(-1, 3, C)
    charge_part = records[:, 3 * C : 4 * C]
    skel_part = records[:, 4 * C : 4 * C + 3 * R].reshape(-1, 3, R)
    skel_values = records[:, 4 * C + 3 * R :]
    return (xyz_part, charge_part, skel_part, skel_values)


def local(
    points,
    charges,
    order,
    source_basis,
    target_basis,
    skeleton_points,
    transfer,
    top_points,
    near_pairs,
    near_count,
    far_pairs,
    far_count,
):
    narrow_size = lax.axis_size("narrow")
    wide_index = lax.axis_index("wide")
    narrow_index = lax.axis_index("narrow")
    panel_count = charges.shape[0]
    own_count = panel_count // C
    group_rows = own_count * narrow_size
    device_index = wide_index * narrow_size + narrow_index
    slot_xyz = points[:, order].reshape(3, own_count, C).transpose(1, 0, 2)
    slot_charge = charges[order].reshape(own_count, C)
    skel_xyz = skeleton_points.reshape(3, own_count, R).transpose(1, 0, 2)
    skel_charge = jnp.einsum(
        "rci,ci->cr", source_basis.reshape(R, own_count, C), slot_charge, precision=highest
    )
    records = jnp.concatenate(
        [
            slot_xyz.reshape(own_count, 3 * C),
            slot_charge,
            skel_xyz.reshape(own_count, 3 * R),
            skel_charge,
        ],
        axis=1,
    )
    grouped = lax.all_gather(records, "narrow", axis=0, tiled=True)
    window = padded(grouped, (("wide", 0),), group_rows)
    window_start = (wide_index - 1) * group_rows
    win_xyz, win_charge, win_skel, win_skel_charge = unpack(window)
    last = near_count[0]

    def near_block(block_step, sums):
        positions = block_step * pair_block + jnp.arange(pair_block, dtype=jnp.int32)
        weight = (positions < last).astype(jnp.float32)[:, None]
        slots = jnp.clip(positions, 0, near_pairs.shape[1] - 1)
        target = near_pairs[0, slots] - window_start
        source = near_pairs[1, slots] - window_start
        tiles = kernel_tile(win_xyz[target], win_xyz[source])
        to_target = jnp.einsum("nij,nj->ni", tiles, win_charge[source], precision=highest) * weight
        to_source = jnp.einsum("nij,ni->nj", tiles, win_charge[target], precision=highest) * weight
        return sums.at[target].add(to_target).at[source].add(to_source)

    block_count = (last + pair_block - 1) // pair_block
    window_sums = lax.fori_loop(
        0, block_count, near_block, jnp.zeros((3 * group_rows, C), jnp.float32)
    )
    from_after = passed_along(window_sums[:group_rows], "wide", -1)
    from_before = passed_along(window_sums[2 * group_rows :], "wide", 1)
    middle_rows = window_sums[group_rows : 2 * group_rows] + from_after + from_before
    near_potential = lax.psum_scatter(middle_rows, "narrow", scatter_dimension=0, tiled=True)
    self_tiles = kernel_tile(slot_xyz, slot_xyz)
    self_potential = jnp.einsum("nij,nj->ni", self_tiles, slot_charge, precision=highest)
    partial_value = jnp.sum(
        jnp.einsum("acb,cb->ca", transfer.reshape(R, own_count, R), skel_charge, precision=highest),
        axis=0,
    )
    every = lax.all_gather(partial_value[None, :], ("wide", "narrow"), axis=0, tiled=True)
    group_charge = every.reshape(-1, narrow_size, R).sum(axis=1)
    top_xyz = (
        lax.all_gather(top_points, "wide", axis=1, tiled=True).reshape(3, -1, R).transpose(1, 0, 2)
    )
    far_slots = far_pairs.shape[1]
    far_weight = (jnp.arange(far_slots, dtype=jnp.int32) < far_count[0]).astype(jnp.float32)[
        :, None
    ]
    far_target = far_pairs[0] - device_index * own_count
    leaf_index = jnp.clip(far_pairs[1] - window_start, 0, 3 * group_rows - 1)
    top_index = jnp.clip(far_pairs[1], 0, group_charge.shape[0] - 1)
    is_leaf = far_pairs[2] == 0
    source_xyz = jnp.where(is_leaf[:, None, None], win_skel[leaf_index], top_xyz[top_index])
    source_charge = jnp.where(
        is_leaf[:, None], win_skel_charge[leaf_index], group_charge[top_index]
    )
    coupling = kernel_tile(skel_xyz[jnp.clip(far_target, 0, own_count - 1)], source_xyz)
    middle = jnp.einsum("nab,nb->na", coupling, source_charge, precision=highest) * far_weight
    selector = (far_target[:, None] == jnp.arange(own_count, dtype=jnp.int32)[None, :]).astype(
        jnp.float32
    )
    per_cluster = jnp.dot(selector.T, middle, precision=highest)
    far_potential = jnp.einsum(
        "rci,cr->ci", target_basis.reshape(R, own_count, C), per_cluster, precision=highest
    )
    total = near_potential + self_potential + far_potential
    return jnp.zeros((panel_count,), jnp.float32).at[order].set(total.reshape(-1))


def solution(mesh):
    return jax.shard_map(
        local,
        mesh=mesh,
        in_specs=(
            P(None, ("wide", "narrow")),
            P(("wide", "narrow")),
            P(("wide", "narrow")),
            P(None, ("wide", "narrow")),
            P(None, ("wide", "narrow")),
            P(None, ("wide", "narrow")),
            P(None, ("wide", "narrow")),
            P(None, "wide"),
            P(None, ("wide", "narrow")),
            P(("wide", "narrow")),
            P(None, ("wide", "narrow")),
            P(("wide", "narrow")),
        ),
        out_specs=P(("wide", "narrow")),
        check_vma=False,
    )
```

profile of v0, /device:TPU:8, one launch (start us, length us, event | category | flops | bytes accessed | tf_op | source)
XLA Modules:
  0.0 700.9 jit_solution(17302735869719776494)
XLA Ops:
  9.6 23.0 %gather_fusion.7 = f32[4096]{0:T(1024)S(1)} fusion(f32[4096]{0:T(1024)S(1)} %copy-done, s32[4096]{0:T(1024)S(1)} %get-tuple-element.101), kind=kCustom, calls=%fused_computation.7 | custom fusion | bytes 49152 | tf_op jit(solution)/shard_map/gather | solution.py:71
  32.7 14.1 %gather_fusion.6 = f32[4096,3]{1,0:T(8,128)} fusion(f32[3,4096]{0,1:T(8,128)S(1)} %copy.43, s32[4096]{0:T(1024)S(1)} %get-tuple-element.101), kind=kCustom, calls=%fused_computation.6 | custom fusion | bytes 114688 | tf_op jit(solution)/shard_map/gather | solution.py:70
  46.8 2.2 copy.44
  49.8 13.5 %all_gather.9 = f32[128,1152]{1,0:T(8,128)S(1)} all-gather(f32[16,1152]{1,0:T(8,128)S(1)} %concatenate.12), channel_id=1, replica_groups=mesh['wide'=64,'narrow'=8] {'narrow'}, dimensions={0}, use_global_device_ids=true | all-gather | bytes 663552 | tf_op jit(solution)/shard_map/all_gather | solution.py:85
  63.3 3.5 collective-permute-start
  66.8 5.2 collective-permute-start.1
  73.6 2.2 multiply_reduce_fusion.1
  76.5 4.1 fusion.23
  81.3 103.1 %all-gather.1 = f32[64,32,3]{1,2,0:T(4,128)S(1)} all-gather(f32[1,32,3]{1,2,0:T(4,128)S(1)} %bitcast.142), channel_id=1, replica_groups=mesh['wide'=64,'narrow'=8] {'wide'}, dimensions={0}, use_global_device_ids=true | all-gather | bytes 24960 | tf_op jit(solution)/shard_map/all_gather | solution.py:119
  186.3 328.6 %all-reduce.5.cloned.1.call-done = f32[16384]{0:T(1024)} async-done(((f32[16384]{0:T(1024)}), f32[16384]{0:T(1024)}) %all-reduce.5.cloned.1.call-update) | async-done | bytes 65552
  518.8 2.8 copy.64
  524.3 54.4 %while.10 = (s32[]{:T(128)}, f32[384,256]{1,0:T(8,128)S(1)}, s32[]{:T(128)}, s32[2,64]{1,0:T(2,128)S(1)}, s32[]{:T(128)}, /*index=5*/f32[384,3,256]{2,1,0:T(4,12...) while((s32[]{:T(128)}, f32[384,256]{1,0:T(8,128)S(1)}, s32[]{:T(128)}, s32[2,64]{1,0:T(2,128)S(1)}, ...), condition=%wide.region_4.5_spmd, body=%wide.region_0.4_spmd.sunk | while | flops 18884820 | bytes 7317285 | solution.py:103
  525.7 2.0 gather_fusion.2
  531.3 2.1 fusion.67
  539.3 2.0 gather_fusion.2
  544.9 2.1 fusion.67
  552.9 2.0 gather_fusion.2
  558.5 2.1 fusion.67
  572.1 2.1 fusion.67
  578.7 2.1 collective-permute-start.2
  580.8 4.1 collective-permute-start.3
  585.0 4.9 fusion.50
  591.3 85.3 %reduce-scatter.2.cloned.1.call-done = f32[16,256]{1,0:T(8,128)} async-done(((f32[128,256]{1,0:T(8,128)}), f32[16,256]{1,0:T(8,128)}) %reduce-scatter.2.cloned.1.call-update) | async-done | bytes 16400 | tf_op jit(solution)/shard_map/reduce_scatter | solution.py:109
  677.4 16.1 %scatter_custom_fusion.2 = f32[4096]{0:T(1024)} fusion(s32[4096]{0:T(1024)S(1)} %get-tuple-element.102, f32[4096]{0:T(1024)S(1)} %bitcast.140, f32[]{:T(128)} %constant.38.clone.1), kind=kCustom, calls=%fused_computation.82 | custom fusion | bytes 16388 | tf_op jit(solution)/shard_map/scatter | solution.py:143
  (141 shorter events, 54.6 us)
Async XLA Ops:
  7.4 2.2 copy-start
  7.4 507.5 %all-reduce.5.cloned.1.call-start = ((), (), s32[]{:S(2)}) async-start(), calls=%async_computation.2 | async-start | bytes 131072
  32.6 16.4 %copy-start.6 = (f32[3,512]{1,0:T(4,128)S(1)}, f32[3,512]{1,0:T(4,128)}, u32[]{:S(2)}) copy-start(f32[3,512]{1,0:T(4,128)} %param.19) | copy-start | bytes 18436
  32.6 16.6 %copy-start.2 = (f32[32,4096]{1,0:T(8,128)S(1)}, f32[32,4096]{1,0:T(8,128)}, u32[]{:S(2)}) copy-start(f32[32,4096]{1,0:T(8,128)} %param.17) | copy-start | bytes 1572868
  32.7 39.4 %copy-start.5 = (f32[32,512]{1,0:T(8,128)S(1)}, f32[32,512]{1,0:T(8,128)}, u32[]{:S(2)}) copy-start(f32[32,512]{1,0:T(8,128)} %param.20) | copy-start | bytes 196612
  46.8 26.7 %copy-start.8 = (s32[3,128]{1,0:T(4,128)S(1)}, s32[3,128]{1,0:T(4,128)}, u32[]{:S(2)}) copy-start(s32[3,128]{1,0:T(4,128)} %param.24) | copy-start | bytes 4612
  63.3 453.2 %collective-permute-start = (f32[128,1152]{1,0:T(8,128)S(1)}, f32[128,1152]{1,0:T(8,128)S(1)}, u32[]{:S(2)}, u32[]{:S(2)}) collective-permute-start(f32[128,1152]{1,0:T(8,128)S(1)} %all_gather.9), channel_id=1, source_target_pairs={{0,8},{8,16},{16,24},{24,32},{32,40},{40,48},{48,56},{56,64},{64,7... | collective-permute-start | bytes 1769480 | tf_op jit(solution)/shard_map/ppermute | solution.py:23
  66.8 449.9 %collective-permute-start.1 = (f32[128,1152]{1,0:T(8,128)S(1)}, f32[128,1152]{1,0:T(8,128)S(1)}, u32[]{:S(2)}, u32[]{:S(2)}) collective-permute-start(f32[128,1152]{1,0:T(8,128)S(1)} %all_gather.9), channel_id=1, source_target_pairs={{8,0},{16,8},{24,16},{32,24},{40,32},{48,40},{56,48},{64,56},{72,6... | collective-permute-start | bytes 1769480 | tf_op jit(solution)/shard_map/ppermute | solution.py:24
  72.8 0.6 copy-start.4
  73.4 603.2 %reduce-scatter.2.cloned.1.call-start = ((), (), s32[]{:S(2)}) async-start(), calls=%async_computation.1 | async-start | bytes 147456 | tf_op jit(solution)/shard_map/reduce_scatter | solution.py:109
  76.5 4.8 copy-start.7
  522.7 1.6 copy-start.1
  578.7 12.3 %copy-start.3 = (f32[32,4096]{1,0:T(8,128)S(1)}, f32[32,4096]{1,0:T(8,128)}, u32[]{:S(2)}) copy-start(f32[32,4096]{1,0:T(8,128)} %param.18) | copy-start | bytes 1572868
  578.7 11.2 %collective-permute-start.2 = (f32[128,256]{1,0:T(8,128)S(1)}, f32[128,256]{1,0:T(8,128)S(1)}, u32[]{:S(2)}, u32[]{:S(2)}) collective-permute-start(f32[128,256]{1,0:T(8,128)S(1)} %get-tuple-element.99), channel_id=1, source_target_pairs={{8,0},{16,8},{24,16},{32,24},{40,32},{48,40},{56,48},{64,56},{72,6... | collective-permute-start | bytes 393224 | tf_op jit(solution)/shard_map/ppermute | solution.py:32
  580.8 9.2 %collective-permute-start.3 = (f32[128,256]{1,0:T(8,128)S(1)}, f32[128,256]{1,0:T(8,128)S(1)}, u32[]{:S(2)}, u32[]{:S(2)}) collective-permute-start(f32[128,256]{1,0:T(8,128)S(1)} %get-tuple-element.100), channel_id=1, source_target_pairs={{0,8},{8,16},{16,24},{24,32},{32,40},{40,48},{48,56},{56,64},{64,7... | collective-permute-start | bytes 393224 | tf_op jit(solution)/shard_map/ppermute | solution.py:32
Sparse Core Ops, SparseCore 0:
  73.6 441.2 all-reduce.4
Sparse Core Ops, SparseCore 1:
  590.8 85.8 reduce-scatter.1
where the time goes:
time: 702 us; the launch traced here: 701 us
  waiting for transfers between devices  414 us (59%)
  blocking collectives  117 us (17%)
  local copies, waits for them, and re-layouts  94.5 us (13%)
  matrix products  24.7 us (4%)
  other arithmetic  19.3 us (3%)
  between operations  16.7 us (2%)
  starting transfers between devices  14.9 us (2%)
    unnamed x3, waiting for transfers between devices  329 us
    all_gather x1, blocking collectives, local(): lax.all_gather(top_points, 'wide', axis=1, tiled=True).reshape(3, -1, R)  103 us
    reduce_scatter x1, waiting for transfers between devices, local(): lax.psum_scatter(middle_rows, 'narrow', scatter_dimension=0, tiled=True)  85.3 us
    gather x1, local copies, waits for them, and re-layouts, local(): slot_charge = charges[order].reshape(own_count, C)  23 us
    scatter x1, local copies, waits for them, and re-layouts, local(): jnp.zeros((panel_count,), jnp.float32).at[order].set(total.reshape(-1))  16.1 us
    gather x8, local copies, waits for them, and re-layouts, near_block(): tiles = kernel_tile(win_xyz[target], win_xyz[source])  15.9 us
    gather x1, local copies, waits for them, and re-layouts, local(): slot_xyz = points[:, order].reshape(3, own_count, C).transpose(1, 0, 2)  14.1 us
  transfers between devices with their start and end apart: 6, of which 2 were waited for; matrix products, arithmetic and copies ran while one was open for 2% of the time, Pallas kernels for 0%

commit v1 on v0

v1 whole, which is shorter than its diff:
```python
import functools

import jax
import jax.numpy as jnp
from jax import lax
from jax.experimental import pallas as pl
from jax.experimental.pallas import tpu as pltpu
from jax.sharding import PartitionSpec as P

C = 256
R = 32
LANES = 128
CLUSTERS = 16
ROWS = 32
NARROW = 8
GROUP = 128
WIDTH = 8
STRIP_CLUSTERS = 32
PAIR_ROW = 8 * STRIP_CLUSTERS
SKEL_ROW = PAIR_ROW + 24
STRIP_ROWS = SKEL_ROW + GROUP
SKEL_REC = 24
WINDOW = 3 * STRIP_CLUSTERS
DUMMY = WINDOW
SELF = WINDOW + 1
DEPTH = 48
UNROLL = 2
CHUNK = 64

soft_square = 0.01
kernel_scale = 0.07957747154594767
f32 = jnp.float32
bf16 = jnp.bfloat16
i32 = jnp.int32


def iota(shape, dim):
    return lax.broadcasted_iota(i32, shape, dim)


def split3(x):
    high = x.astype(bf16)
    rest = x - high.astype(f32)
    mid = rest.astype(bf16)
    low = (rest - mid.astype(f32)).astype(bf16)
    return high, mid, low


def parts_dot(x, ones, dims):
    dots = [
        lax.dot_general(part, ones, (dims, ((), ())), preferred_element_type=f32)
        for part in split3(x)
    ]
    return dots[0] + dots[1] + dots[2]


def as_bf16(mask):
    return mask.astype(f32).astype(bf16)


def slots_kernel(
    near_count,
    points,
    charges,
    order,
    source_basis,
    transfer,
    skeleton_points,
    top_points,
    near_pairs,
    own,
    to_down,
    to_up,
    skel_out,
):
    low = order[...] & (LANES - 1)
    high = order[...] >> 7
    sub = iota((8, LANES), 0)
    tables = []
    for row in range(ROWS):
        xyz = points[:, row * LANES : (row + 1) * LANES]
        charge = charges[row : row + 1, :]
        tables.append(jnp.concatenate([xyz, charge, xyz, charge], axis=0))
    tiles = []
    for tile in range(CLUSTERS):
        first = 4 * (tile // 2) + tile % 2
        low_tile = jnp.where(sub < 4, low[first : first + 1], low[first + 2 : first + 3])
        high_tile = jnp.where(sub < 4, high[first : first + 1], high[first + 2 : first + 3])
        values = jnp.zeros((8, LANES), f32)
        for row in range(ROWS):
            found = jnp.take_along_axis(tables[row], low_tile, axis=1)
            values = jnp.where(high_tile == row, found, values)
        own[8 * tile : 8 * tile + 8, :] = values
        if tile < 8:
            to_down[8 * tile : 8 * tile + 8, :] = values
        else:
            to_up[8 * tile - 64 : 8 * tile - 56, :] = values
        tiles.append(values)

    pairs = jnp.where(iota((2, 64), 1) < near_count[0], near_pairs[...] + 1, 0).astype(f32)
    for ref, start in ((own, 128), (to_down, 64), (to_up, 64)):
        ref[start : start + 8, :] = jnp.zeros((8, LANES), f32)
        ref[start : start + 2, 0:64] = pairs

    lane = iota((R, LANES), 1)
    skel = jnp.zeros((R, LANES), f32)
    for cluster in range(CLUSTERS):
        block, place = cluster // 2, 4 * (cluster % 2) + 3
        basis = source_basis[:, cluster * C : (cluster + 1) * C]
        product = (
            basis[:, :LANES] * tiles[2 * block][place : place + 1]
            + basis[:, LANES:] * tiles[2 * block + 1][place : place + 1]
        )
        skel = jnp.where(lane == cluster, jnp.sum(product, axis=1, keepdims=True), skel)
    skel_rows = skel.T[:CLUSTERS, :]
    long_lane = iota((R, CLUSTERS * R), 1)
    repeat = as_bf16(long_lane % R == iota((R, CLUSTERS * R), 0))
    tiled = parts_dot(skel_rows, repeat, ((1,), (0,)))
    mine = iota((CLUSTERS, CLUSTERS * R), 1) // R == iota((CLUSTERS, CLUSTERS * R), 0)
    flat = jnp.sum(jnp.where(mine, tiled, 0.0), axis=0, keepdims=True)
    partial = jnp.sum(transfer[...] * flat, axis=1, keepdims=True)
    skel = jnp.where(lane == CLUSTERS, partial, skel)
    to_charge = as_bf16(lane == iota((R, LANES), 0) + 3 * R)
    record = parts_dot(skel.T[:SKEL_REC, :], to_charge, ((1,), (0,)))
    fold = as_bf16(iota((CLUSTERS * R, LANES), 1) % R == iota((CLUSTERS * R, LANES), 0) % R)
    short_lane = iota((CLUSTERS, LANES), 1) // R
    geometry = jnp.zeros((CLUSTERS, LANES), f32)
    for axis in range(3):
        masked = jnp.where(mine, skeleton_points[axis : axis + 1, :], 0.0)
        folded = parts_dot(masked, fold, ((1,), (0,)))
        geometry = jnp.where(short_lane == axis, folded, geometry)
    spread = as_bf16(lane % R == iota((R, LANES), 0))
    top = parts_dot(top_points[...], spread, ((1,), (0,)))
    top_mine = iota((3, LANES), 1) // R == iota((3, LANES), 0)
    top_row = jnp.sum(jnp.where(top_mine, top, 0.0), axis=0, keepdims=True)
    last = jnp.where(iota((8, LANES), 0) == 1, top_row, 0.0)
    record = record + jnp.concatenate([geometry, last], axis=0)
    for copy in range(NARROW):
        skel_out[copy] = record


def with_norms(halves, origin):
    out = []
    for half in halves:
        sub = iota((8, LANES), 0)
        shifted = jnp.where(sub < 3, half - origin, 0.0)
        norms = jnp.sum(shifted * shifted, axis=0, keepdims=True)
        out.append((shifted, norms))
    return out


def source_features(halves, origin):
    sub = iota((8, LANES), 0)
    columns = []
    for shifted, norms in with_norms(halves, origin):
        rows = jnp.where(sub < 3, shifted, jnp.where(sub == 4, norms, 0.0))
        rows = jnp.where(sub == 5, 1.0, rows)
        high, mid, low = [part.astype(f32) for part in split3(rows)]
        columns.append(jnp.concatenate([high, mid, high, mid, low, high], axis=0).astype(bf16))
    return jnp.concatenate(columns, axis=1)


def target_features(halves, origin):
    sub = iota((8, LANES), 0)
    columns = []
    for shifted, norms in with_norms(halves, origin):
        rows = jnp.where(sub < 3, -2.0 * shifted, jnp.where(sub == 5, norms + soft_square, 0.0))
        rows = jnp.where(sub == 4, 1.0, rows)
        high, mid, low = [part.astype(f32) for part in split3(rows)]
        stacked = jnp.concatenate([high, high, mid, mid, high, low], axis=0)
        columns.append(stacked.T.astype(bf16))
    return jnp.concatenate(columns, axis=0)


def near_kernel(
    place,
    before,
    strip,
    after,
    near,
    features,
    charge,
    lhs,
    entries_vmem,
    entries,
    semaphore,
    *sums,
):
    wide_index = place[0]
    narrow_index = place[1]
    sub = iota((8, LANES), 0)

    def cluster_halves(ref, block, odd):
        halves = []
        for half in range(2):
            tile = ref[pl.ds(pl.multiple_of(16 * block + 8 * half, 8), 8), :]
            halves.append(pltpu.roll(tile, 4, 0) if odd else tile)
        return halves

    def put_source(slot, halves, origin):
        features[slot] = source_features(halves, origin)
        for half in range(2):
            row = halves[half][3:4]
            charge[slot, :, half * LANES : (half + 1) * LANES] = jnp.broadcast_to(row, (8, LANES))

    base = (wide_index * GROUP + narrow_index * CLUSTERS + 1).astype(f32)
    targets, sources = [], []
    for ref in (before, strip, after):
        for block in range(3):
            start = PAIR_ROW + 8 * block
            targets.append(ref[start : start + 1, :])
            sources.append(ref[start : start + 1 + 1, :][1:2])
    nothing = jnp.zeros((6, LANES), f32)
    own_ids = jnp.concatenate(sources + [targets[4]] + [nothing], axis=0)
    other_ids = jnp.concatenate(targets + [sources[4]] + [nothing], axis=0)
    local = own_ids - base
    used = (local >= 0.0) & (local < CLUSTERS) & (own_ids > 0.0)
    count = used.astype(f32)
    upto = as_bf16(iota((LANES, LANES), 0) <= iota((LANES, LANES), 1))
    inclusive = jnp.dot(count.astype(bf16), upto, preferred_element_type=f32)
    totals = jnp.sum(count, axis=1, keepdims=True)
    row_of = iota((16, LANES), 0)
    offset = jnp.zeros((16, LANES), f32)
    for row in range(10):
        offset = jnp.where(row_of > row, offset + totals[row : row + 1], offset)
    spot = inclusive - count + offset
    other = other_ids - 1.0
    group = jnp.floor(other * (1.0 / GROUP))
    rest = other - GROUP * group
    depth = jnp.floor(rest * (1.0 / WIDTH))
    column = rest - WIDTH * depth
    group_step = group - (wide_index - 1).astype(f32)
    depth_step = depth - (2 * narrow_index - 1).astype(f32)
    window = group_step * STRIP_CLUSTERS + depth_step * WIDTH + column
    window = jnp.where(used, window, 0.0)
    local = jnp.where(used, local, 0.0)
    spot = jnp.where(used, spot, -1.0)
    spot_high = jnp.floor(spot * (1.0 / LANES))
    spot_low = spot - LANES * spot_high
    listed = jnp.zeros((16, LANES), f32)
    eight = iota((8, LANES), 0).astype(f32)
    tall = iota((LANES, LANES), 0).astype(f32)
    for row in range(10):
        here = eight == spot_high[row : row + 1]
        values = jnp.concatenate(
            [
                jnp.where(here, local[row : row + 1], 0.0),
                jnp.where(here, window[row : row + 1], 0.0),
            ],
            axis=0,
        ).astype(bf16)
        hot = as_bf16(tall == spot_low[row : row + 1])
        listed = listed + lax.dot_general(
            values, hot, (((1,), (1,)), ((), ())), preferred_element_type=f32
        )
    coded = listed[:8] * float(GROUP) + listed[8:]
    coded = jnp.where(eight == 7.0, jnp.sum(totals), coded)
    entries_vmem[...] = coded.astype(i32)
    copy = pltpu.make_async_copy(entries_vmem, entries, semaphore)
    copy.start()

    whole = jnp.zeros((8, LANES), f32)
    for block in range(8):
        for half in range(2):
            start = 64 + 16 * block + 8 * half
            whole = whole + strip[start : start + 8, :]
    mean = jnp.sum(whole, axis=1, keepdims=True) * (1.0 / (CLUSTERS * C))
    mean = jnp.broadcast_to(mean, (8, LANES))
    origin = jnp.where(sub < 3, mean + pltpu.roll(mean, 4, 0), 0.0)

    def own_block(block, carry):
        for odd in range(2):
            cluster = 2 * block + odd
            halves = cluster_halves(strip, block + 4, odd)
            lhs[cluster] = target_features(halves, origin)
            centre = jnp.sum(halves[0] + halves[1], axis=1, keepdims=True) * (1.0 / C)
            lhs[CLUSTERS + cluster] = target_features(halves, centre)
            put_source(SELF + cluster, halves, centre)
        return carry

    lax.fori_loop(0, CLUSTERS // 2, own_block, 0)

    def window_block(block, carry):
        for part, ref in enumerate((before, strip, after)):
            for odd in range(2):
                put_source(
                    part * STRIP_CLUSTERS + 2 * block + odd, cluster_halves(ref, block, odd), origin
                )
        return carry

    lax.fori_loop(0, STRIP_CLUSTERS // 2, window_block, 0)
    features[DUMMY] = jnp.zeros((DEPTH, C), bf16)
    charge[DUMMY] = jnp.zeros((8, C), f32)

    def interact(left, slot, first):
        rhs = features[slot]
        charge_low = charge[slot, 0:1, 0:LANES]
        charge_high = charge[slot, 0:1, LANES:C]
        for start in range(0, C, CHUNK):
            square = jnp.dot(
                lhs[left, start : start + CHUNK, :], rhs, preferred_element_type=f32
            )
            inverse = lax.rsqrt(jnp.maximum(square, soft_square))
            first(start, inverse[:, :LANES] * charge_low + inverse[:, LANES:] * charge_high)

    def self_step(step, carry):
        for turn in range(UNROLL):
            cluster = step * UNROLL + turn

            def store(start, value):
                for other_turn in range(UNROLL):
                    sums[other_turn][cluster, start : start + CHUNK, :] = (
                        value if other_turn == turn else jnp.zeros_like(value)
                    )

            interact(CLUSTERS + cluster, SELF + cluster, store)
        return carry

    lax.fori_loop(0, CLUSTERS // UNROLL, self_step, 0)
    copy.wait()
    pair_total = entries[7, 0]

    def pair_step(step, carry):
        for turn in range(UNROLL):
            index = step * UNROLL + turn
            code = entries[index >> 7, index & (LANES - 1)]
            live = index < pair_total
            cluster = jnp.where(live, code >> 7, 0)
            slot = jnp.where(live, code & (LANES - 1), DUMMY)

            def add(start, value):
                sums[turn][cluster, start : start + CHUNK, :] += value

            interact(cluster, slot, add)
        return carry

    lax.fori_loop(0, (pair_total + UNROLL - 1) // UNROLL, pair_step, 0)

    for cluster in range(CLUSTERS):
        for half in range(2):
            rows = slice(half * LANES, (half + 1) * LANES)
            total = sums[0][cluster, rows, :]
            for turn in range(1, UNROLL):
                total = total + sums[turn][cluster, rows, :]
            row = 2 * cluster + half
            near[row : row + 1, :] = kernel_scale * jnp.sum(total.T, axis=0, keepdims=True)


def far_kernel(
    place,
    far_count,
    before,
    strip,
    after,
    own_skel,
    top,
    far_pairs,
    near,
    order,
    target_basis,
    potential,
    total,
):
    wide_index = place[0]
    narrow_index = place[1]
    first = wide_index * GROUP + narrow_index * CLUSTERS
    target = far_pairs[0:1, :] - first
    source = far_pairs[1:2, :]
    is_leaf = far_pairs[2:3, :] == 0
    live = iota((1, LANES), 1) < far_count[0]
    index = jnp.where(is_leaf, source - (wide_index - 1) * GROUP, source + 3 * GROUP)
    skel = slice(SKEL_ROW, SKEL_ROW + GROUP)
    table = jnp.concatenate([before[skel, :], strip[skel, :], after[skel, :], top[...]], axis=0)
    chosen = as_bf16(iota((table.shape[0], LANES), 0) == index)
    over_rows = ((0,), (0,))
    sources = parts_dot(table, chosen, over_rows)
    own_chosen = as_bf16(iota((CLUSTERS, LANES), 0) == target)
    targets = parts_dot(own_skel[0, :CLUSTERS, :], own_chosen, over_rows)
    rows = []
    for a in range(R):
        square = soft_square
        for axis in range(3):
            offset = sources[axis * R : (axis + 1) * R] - targets[axis * R + a : axis * R + a + 1]
            square = square + offset * offset
        product = lax.rsqrt(square) * sources[3 * R :]
        rows.append(jnp.sum(product, axis=0, keepdims=True))
    middle = jnp.where(live, jnp.concatenate(rows, axis=0) * kernel_scale, 0.0)
    for cluster in range(CLUSTERS):
        column = jnp.sum(jnp.where(target == cluster, middle, 0.0), axis=1, keepdims=True)
        spread = jnp.sum(
            target_basis[:, cluster * C : (cluster + 1) * C] * column, axis=0, keepdims=True
        )
        for half in range(2):
            row = 2 * cluster + half
            total[row : row + 1, :] = (
                near[row : row + 1, :] + spread[:, half * LANES : (half + 1) * LANES]
            )
    low = order[...] & (LANES - 1)
    high = order[...] >> 7
    out = jnp.zeros((ROWS, LANES), f32)
    tall = iota((LANES, LANES), 0)
    wide = iota((ROWS, LANES), 0)
    for row in range(ROWS):
        here = wide == high[row : row + 1]
        value = jnp.where(here, total[row : row + 1, :], 0.0)
        out = out + parts_dot(value, as_bf16(tall == low[row : row + 1]), ((1,), (1,)))
    potential[...] = out


def smem():
    return pl.BlockSpec(memory_space=pltpu.SMEM)


def vmem():
    return pl.BlockSpec(memory_space=pltpu.VMEM)


params = pltpu.CompilerParams(vmem_limit_bytes=50 * 1024 * 1024)


def local(
    points,
    charges,
    order,
    source_basis,
    target_basis,
    skeleton_points,
    transfer,
    top_points,
    near_pairs,
    near_count,
    far_pairs,
    far_count,
):
    wide_size = lax.axis_size("wide")
    narrow_size = lax.axis_size("narrow")
    place = jnp.stack([lax.axis_index("wide"), lax.axis_index("narrow")]).astype(i32)
    order = order.reshape(ROWS, LANES)
    shape = jax.ShapeDtypeStruct
    with jax.named_scope("slots"):
        own, to_down, to_up, skel = pl.pallas_call(
            slots_kernel,
            out_shape=(
                shape((136, LANES), f32),
                shape((72, LANES), f32),
                shape((72, LANES), f32),
                shape((NARROW, SKEL_REC, LANES), f32),
            ),
            in_specs=[smem()] + [vmem()] * 8,
            out_specs=[vmem()] * 4,
            compiler_params=params,
        )(
            near_count,
            points,
            charges.reshape(ROWS, LANES),
            order,
            source_basis,
            transfer,
            skeleton_points,
            top_points,
            near_pairs,
        )
    upward = [(i, i + 1) for i in range(narrow_size - 1)]
    downward = [(i + 1, i) for i in range(narrow_size - 1)]
    from_down = lax.ppermute(to_up, "narrow", upward)
    from_up = lax.ppermute(to_down, "narrow", downward)
    skels = lax.all_to_all(skel, "narrow", 0, 0, tiled=True)
    message = jnp.sum(skels[:, CLUSTERS, :], axis=0) + skels[0, CLUSTERS + 1, :]
    tops = lax.all_to_all(
        jnp.broadcast_to(message[None, None, :], (wide_size, 1, LANES)), "wide", 0, 0, tiled=True
    )
    strip = jnp.concatenate(
        [
            from_down[:64],
            own[:128],
            from_up[:64],
            from_down[64:],
            own[128:],
            from_up[64:],
            skels[:, :CLUSTERS, :].reshape(GROUP, LANES),
        ],
        axis=0,
    )
    before = lax.ppermute(strip, "wide", [(i, i + 1) for i in range(wide_size - 1)])
    after = lax.ppermute(strip, "wide", [(i + 1, i) for i in range(wide_size - 1)])
    with jax.named_scope("near"):
        near = pl.pallas_call(
            near_kernel,
            out_shape=shape((ROWS, LANES), f32),
            in_specs=[smem()] + [vmem()] * 3,
            out_specs=vmem(),
            scratch_shapes=[
                pltpu.VMEM((SELF + CLUSTERS, DEPTH, C), bf16),
                pltpu.VMEM((SELF + CLUSTERS, 8, C), f32),
                pltpu.VMEM((2 * CLUSTERS, C, DEPTH), bf16),
                pltpu.VMEM((8, LANES), i32),
                pltpu.SMEM((8, LANES), i32),
                pltpu.SemaphoreType.DMA(()),
            ]
            + [pltpu.VMEM((CLUSTERS, C, LANES), f32)] * UNROLL,
            compiler_params=params,
        )(place, before, strip, after)
    with jax.named_scope("far"):
        potential = pl.pallas_call(
            far_kernel,
            out_shape=shape((ROWS, LANES), f32),
            in_specs=[smem(), smem()] + [vmem()] * 9,
            out_specs=vmem(),
            scratch_shapes=[pltpu.VMEM((ROWS, LANES), f32)],
            compiler_params=params,
        )(
            place,
            far_count,
            before,
            strip,
            after,
            skel,
            tops.reshape(wide_size, LANES),
            far_pairs,
            near,
            order,
            target_basis,
        )
    return potential.reshape(-1)


def solution(mesh):
    both = ("wide", "narrow")
    split = P(None, both)
    return jax.shard_map(
        local,
        mesh=mesh,
        in_specs=(
            split,
            P(both),
            P(both),
            split,
            split,
            split,
            split,
            P(None, "wide"),
            split,
            P(both),
            split,
            P(both),
        ),
        out_specs=P(both),
        check_vma=False,
    )
```

time: 702 us -> 70.8 us (0.10)
  waiting for transfers between devices: 414 us -> 4.45 us
  blocking collectives: 117 us -> 0 us
  local copies, waits for them, and re-layouts: 94.5 us -> 6.2 us
  matrix products: 24.7 us -> 0 us
  Pallas kernels: 0 us -> 23 us
  starting transfers between devices: 14.9 us -> 34.9 us
  other arithmetic: 19.3 us -> 0.11 us
  between operations: 16.7 us -> 1.47 us
    unnamed x3 -> x0, waiting for transfers between devices: 329 us -> none
    all_gather x2 -> x0, blocking collectives: 117 us -> none  [the longest x1 103 us: local(): lax.all_gather(top_points, 'wide', axis=1, tiled=True).reshape(3, -1, R)]
    reduce_scatter x1 -> x0, waiting for transfers between devices: 85.3 us -> none  [local(): lax.psum_scatter(middle_rows, 'narrow', scatter_dimension=0, tiled=True)]
    gather x32 -> x0, local copies, waits for them, and re-layouts: 66.4 us -> none  [the longest x1 23 us: local(): slot_charge = charges[order].reshape(own_count, C)]
    all_to_all x0 -> x2, starting transfers between devices: none -> 24.8 us  [the longest x1 19.4 us: local(): lax.all_to_all(jnp.broadcast_to(message[None, None, :], (wide_size, 1, LA...]
    dot_general x14 -> x0, matrix products: 24.7 us -> none  [the longest x4 8.41 us: near_block(): jnp.einsum('nij,nj->ni', tiles, win_charge[source], precision=highest)]
    pallas_call x0 -> x3, Pallas kernels: none -> 23 us  [the longest x1 16.4 us: local(): pl.pallas_call(near_kernel, out_shape=shape((ROWS, LANES), f32), in_specs...]
    scatter x1 -> x0, local copies, waits for them, and re-layouts: 16.1 us -> none  [local(): jnp.zeros((panel_count,), jnp.float32).at[order].set(total.reshape(-1))]
  transfers between devices with their start and end apart: 6 -> 6, of which waited for: 2 -> 2; matrix products, arithmetic and copies ran while one was open for 2% -> 1% of each run, Pallas kernels for 0% -> 23%
where the time goes in v1:
time: 70.8 us; the launch traced here: 70.1 us
  starting transfers between devices  34.9 us (49%)
  Pallas kernels  23 us (32%)
  local copies, waits for them, and re-layouts  6.2 us (9%)
  waiting for transfers between devices  4.45 us (6%)
  between operations  1.47 us (2%)
    all_to_all x1, starting transfers between devices, local(): lax.all_to_all(jnp.broadcast_to(message[None, None, :], (wide_size, 1, LA...  19.4 us
    pallas_call x1, Pallas kernels, local(): pl.pallas_call(near_kernel, out_shape=shape((ROWS, LANES), f32), in_specs...  16.4 us
    unnamed x28, local copies, waits for them, and re-layouts  5.57 us
    all_to_all x1, starting transfers between devices, local(): skels = lax.all_to_all(skel, 'narrow', 0, 0, tiled=True)  5.4 us
    ppermute x1, starting transfers between devices, local(): lax.ppermute(strip, 'wide', [(i + 1, i) for i in range(wide_size - 1)])  5.18 us
    pallas_call x1, Pallas kernels, local(): pl.pallas_call(far_kernel, out_shape=shape((ROWS, LANES), f32), in_specs=...  4.07 us
    all_to_all x1, waiting for transfers between devices, local(): skels = lax.all_to_all(skel, 'narrow', 0, 0, tiled=True)  2.66 us
    pallas_call x1, Pallas kernels, local(): pl.pallas_call(slots_kernel, out_shape=(shape((136, LANES), f32), shape((...  2.45 us
  transfers between devices with their start and end apart: 6, of which 2 were waited for; matrix products, arithmetic and copies ran while one was open for 1% of the time, Pallas kernels for 23%

profile of v1, /device:TPU:8, one launch (start us, length us, event | category | flops | bytes accessed | tf_op | source)
XLA Modules:
  0.0 70.1 jit_solution(18295064504710888562)
XLA Ops:
  0.7 0.7 copy-done.8
  1.3 0.0 copy-done.10
  1.4 1.0 %copy-done = f32[32,4096]{1,0:T(8,128)S(1)} copy-done((f32[32,4096]{1,0:T(8,128)S(1)}, f32[32,4096]{1,0:T(8,128)}, u32[]{:S(2)}) %copy-start) | copy-done | bytes 524312
  2.4 0.7 %copy-done.2 = s32[4096]{0:T(1024)S(1)} copy-done((s32[4096]{0:T(1024)S(1)}, s32[4096]{0:T(1024)}, u32[]{:S(2)}) %copy-start.2) | copy-done | bytes 16408
  3.1 0.8 %copy-done.4 = f32[3,4096]{1,0:T(4,128)S(1)} copy-done((f32[3,4096]{1,0:T(4,128)S(1)}, f32[3,4096]{1,0:T(4,128)}, u32[]{:S(2)}) %copy-start.4) | copy-done | bytes 49176
  4.0 0.8 %copy-done.5 = f32[32,512]{1,0:T(8,128)S(1)} copy-done((f32[32,512]{1,0:T(8,128)S(1)}, f32[32,512]{1,0:T(8,128)}, u32[]{:S(2)}) %copy-start.5) | copy-done | bytes 65560
  4.8 0.7 %copy-done.6 = f32[4096]{0:T(1024)S(1)} copy-done((f32[4096]{0:T(1024)S(1)}, f32[4096]{0:T(1024)}, u32[]{:S(2)}) %copy-start.6) | copy-done | bytes 16408
  5.5 0.7 copy-done.7
  6.2 2.5 %slots.1 = (f32[136,128]{1,0:T(8,128)S(1)}, f32[72,128]{1,0:T(8,128)S(1)}, f32[72,128]{1,0:T(8,128)S(1)}, f32[8,24,128]{2,1,0:T(8,128)}) custom-call(s32[1]{0:T(128)S(6)} %copy.19.near_count, f32[3,4096]{1,0:T(4,128)S(1)} %copy-done.4, f32[32,128]{1,0:T(8,128)S(1)} %bitcast.14, s32[32,128]{1,0:T(8,128)S(1)} %bitcast.12, f32[32,4096]{1,0:T(8,128)S(1)} %copy-done, ...), custom_call_target="tpu_custom_call" | custom-call | tf_op jit(solution)/shard_map/slots/pallas_call | solution.py:441
  8.7 1.7 %collective-permute-start = (f32[72,128]{1,0:T(8,128)S(1)}, f32[72,128]{1,0:T(8,128)S(1)}, u32[]{:S(2)}, u32[]{:S(2)}) collective-permute-start(f32[72,128]{1,0:T(8,128)S(1)} %get-tuple-element.9), channel_id=1, source_target_pairs={{0,1},{1,2},{2,3},{3,4},{4,5},{5,6},{6,7},{8,9},{9,10},{10,11},{11... | collective-permute-start | bytes 110600 | tf_op jit(solution)/shard_map/ppermute | solution.py:465
  10.4 5.4 %all-to-all-start = ((f32[8,24,128]{2,1,0:T(8,128)}), f32[8,24,128]{2,1,0:T(8,128)S(1)}, u32[]{:S(2)}, u32[]{:S(2)}) async-start(f32[8,24,128]{2,1,0:T(8,128)} %get-tuple-element.12.own_skel), calls=%async_computation | async-start | bytes 196608 | tf_op jit(solution)/shard_map/all_to_all | solution.py:467
  15.8 1.3 %collective-permute-start.1 = (f32[72,128]{1,0:T(8,128)S(1)}, f32[72,128]{1,0:T(8,128)S(1)}, u32[]{:S(2)}, u32[]{:S(2)}) collective-permute-start(f32[72,128]{1,0:T(8,128)S(1)} %get-tuple-element.11), channel_id=1, source_target_pairs={{1,0},{2,1},{3,2},{4,3},{5,4},{6,5},{7,6},{9,8},{10,9},{11,10},{12... | collective-permute-start | bytes 110600 | tf_op jit(solution)/shard_map/ppermute | solution.py:466
  17.1 0.0 collective-permute-done
  17.1 1.8 %collective-permute-done.1 = f32[72,128]{1,0:T(8,128)S(1)} collective-permute-done((f32[72,128]{1,0:T(8,128)S(1)}, f32[72,128]{1,0:T(8,128)S(1)}, u32[]{:S(2)}, u32[]{:S(2)}) %collective-permute-start.1) | collective-permute-done | bytes 36896 | tf_op jit(solution)/shard_map/ppermute | solution.py:466
  18.9 2.7 %all-to-all-done = f32[8,24,128]{2,1,0:T(8,128)S(1)} async-done(((f32[8,24,128]{2,1,0:T(8,128)}), f32[8,24,128]{2,1,0:T(8,128)S(1)}, u32[]{:S(2)}, u32[]{:S(2)}) %all-to-all-start) | async-done | bytes 98336 | tf_op jit(solution)/shard_map/all_to_all | solution.py:467
  21.6 5.2 %collective-permute-start.3 = (f32[408,128]{1,0:T(8,128)S(1)}, f32[408,128]{1,0:T(8,128)S(1)}, u32[]{:S(2)}, u32[]{:S(2)}) collective-permute-start(f32[408,128]{1,0:T(8,128)S(1)} %constant_dynamic-update-slice_fusion.strip), channel_id=1, source_target_pairs={{8,0},{16,8},{24,16},{32,24},{40,32},{48,40},{56,48},{64,56},{72,6... | collective-permute-start | bytes 626696 | tf_op jit(solution)/shard_map/ppermute | solution.py:485
  26.8 1.9 %collective-permute-start.2 = (f32[408,128]{1,0:T(8,128)S(1)}, f32[408,128]{1,0:T(8,128)S(1)}, u32[]{:S(2)}, u32[]{:S(2)}) collective-permute-start(f32[408,128]{1,0:T(8,128)S(1)} %constant_dynamic-update-slice_fusion.strip), channel_id=1, source_target_pairs={{0,8},{8,16},{16,24},{24,32},{32,40},{40,48},{48,56},{56,64},{64,7... | collective-permute-start | bytes 626696 | tf_op jit(solution)/shard_map/ppermute | solution.py:484
  28.8 0.6 broadcast_in_dim.9
  29.4 19.4 %all-to-all-start.1 = ((f32[64,1,128]{2,1,0:T(1,128)}), f32[64,1,128]{2,1,0:T(1,128)S(1)}, u32[]{:S(2)}, u32[]{:S(2)}) async-start(f32[64,1,128]{2,1,0:T(1,128)} %broadcast_in_dim.9), calls=%async_computation.1 | async-start | bytes 65536 | tf_op jit(solution)/shard_map/all_to_all | solution.py:469
  49.4 0.1 pad_add_fusion.place
  49.5 0.0 collective-permute-done.3.after
  49.5 0.0 copy-start.9
  49.5 16.4 %near.1 = f32[32,128]{1,0:T(8,128)S(1)} custom-call(s32[2]{0:T(128)S(1)} %pad_add_fusion.place, f32[408,128]{1,0:T(8,128)S(1)} %collective-permute-done.2.before, f32[408,128]{1,0:T(8,128)S(1)} %constant_dynamic-update-slice_fusion.strip, f32[408,128]{1,0:T(8,128)S(1)} %collective-permute-done.3.after), custom_call_target="tpu_custom_call" | custom-call | tf_op jit(solution)/shard_map/near/pallas_call | solution.py:487
  66.0 4.1 %far.1 = f32[32,128]{1,0:T(8,128)} custom-call(s32[2]{0:T(128)S(1)} %pad_add_fusion.place, s32[1]{0:T(128)S(6)} %copy.20.far_count, f32[408,128]{1,0:T(8,128)S(1)} %collective-permute-done.2.before, f32[408,128]{1,0:T(8,128)S(1)} %constant_dynamic-update-slice_fusion.strip, f32[408,128]{1,0:T(8,128)S(1)} %collective-permute-done.3.after, ...), custom_call_target="tpu_custom_call" | custom-call | tf_op jit(solution)/shard_map/far/pallas_call | solution.py:504
  (25 shorter events, 0.1 us)
Async XLA Ops:
  0.7 0.7 copy-start.8
  0.7 0.7 copy-start.10
  1.3 1.0 %copy-start = (f32[32,4096]{1,0:T(8,128)S(1)}, f32[32,4096]{1,0:T(8,128)}, u32[]{:S(2)}) copy-start(f32[32,4096]{1,0:T(8,128)} %source_basis.1) | copy-start | bytes 1572868
  2.4 0.7 %copy-start.2 = (s32[4096]{0:T(1024)S(1)}, s32[4096]{0:T(1024)}, u32[]{:S(2)}) copy-start(s32[4096]{0:T(1024)} %param.14) | copy-start | bytes 49156
  3.1 0.8 %copy-start.4 = (f32[3,4096]{1,0:T(4,128)S(1)}, f32[3,4096]{1,0:T(4,128)}, u32[]{:S(2)}) copy-start(f32[3,4096]{1,0:T(4,128)} %points.1) | copy-start | bytes 147460
  3.9 0.8 %copy-start.5 = (f32[32,512]{1,0:T(8,128)S(1)}, f32[32,512]{1,0:T(8,128)}, u32[]{:S(2)}) copy-start(f32[32,512]{1,0:T(8,128)} %transfer.1) | copy-start | bytes 196612
  4.8 0.7 %copy-start.6 = (f32[4096]{0:T(1024)S(1)}, f32[4096]{0:T(1024)}, u32[]{:S(2)}) copy-start(f32[4096]{0:T(1024)} %param.13) | copy-start | bytes 49156
  5.5 0.7 copy-start.7
  8.7 8.4 %collective-permute-start = (f32[72,128]{1,0:T(8,128)S(1)}, f32[72,128]{1,0:T(8,128)S(1)}, u32[]{:S(2)}, u32[]{:S(2)}) collective-permute-start(f32[72,128]{1,0:T(8,128)S(1)} %get-tuple-element.9), channel_id=1, source_target_pairs={{0,1},{1,2},{2,3},{3,4},{4,5},{5,6},{6,7},{8,9},{9,10},{10,11},{11... | collective-permute-start | bytes 110600 | tf_op jit(solution)/shard_map/ppermute | solution.py:465
  10.4 11.2 %all-to-all-start = ((f32[8,24,128]{2,1,0:T(8,128)}), f32[8,24,128]{2,1,0:T(8,128)S(1)}, u32[]{:S(2)}, u32[]{:S(2)}) async-start(f32[8,24,128]{2,1,0:T(8,128)} %get-tuple-element.12.own_skel), calls=%async_computation | async-start | bytes 196608 | tf_op jit(solution)/shard_map/all_to_all | solution.py:467
  15.8 3.1 %collective-permute-start.1 = (f32[72,128]{1,0:T(8,128)S(1)}, f32[72,128]{1,0:T(8,128)S(1)}, u32[]{:S(2)}, u32[]{:S(2)}) collective-permute-start(f32[72,128]{1,0:T(8,128)S(1)} %get-tuple-element.11), channel_id=1, source_target_pairs={{1,0},{2,1},{3,2},{4,3},{5,4},{6,5},{7,6},{9,8},{10,9},{11,10},{12... | collective-permute-start | bytes 110600 | tf_op jit(solution)/shard_map/ppermute | solution.py:466
  18.9 47.1 %copy-start.1 = (f32[32,4096]{1,0:T(8,128)S(1)}, f32[32,4096]{1,0:T(8,128)}, u32[]{:S(2)}) copy-start(f32[32,4096]{1,0:T(8,128)} %target_basis.1) | copy-start | bytes 1572868
  21.6 27.9 %collective-permute-start.3 = (f32[408,128]{1,0:T(8,128)S(1)}, f32[408,128]{1,0:T(8,128)S(1)}, u32[]{:S(2)}, u32[]{:S(2)}) collective-permute-start(f32[408,128]{1,0:T(8,128)S(1)} %constant_dynamic-update-slice_fusion.strip), channel_id=1, source_target_pairs={{8,0},{16,8},{24,16},{32,24},{40,32},{48,40},{56,48},{64,56},{72,6... | collective-permute-start | bytes 626696 | tf_op jit(solution)/shard_map/ppermute | solution.py:485
  26.8 22.7 %collective-permute-start.2 = (f32[408,128]{1,0:T(8,128)S(1)}, f32[408,128]{1,0:T(8,128)S(1)}, u32[]{:S(2)}, u32[]{:S(2)}) collective-permute-start(f32[408,128]{1,0:T(8,128)S(1)} %constant_dynamic-update-slice_fusion.strip), channel_id=1, source_target_pairs={{0,8},{8,16},{16,24},{24,32},{32,40},{40,48},{48,56},{56,64},{64,7... | collective-permute-start | bytes 626696 | tf_op jit(solution)/shard_map/ppermute | solution.py:484
  29.4 36.6 %all-to-all-start.1 = ((f32[64,1,128]{2,1,0:T(1,128)}), f32[64,1,128]{2,1,0:T(1,128)S(1)}, u32[]{:S(2)}, u32[]{:S(2)}) async-start(f32[64,1,128]{2,1,0:T(1,128)} %broadcast_in_dim.9), calls=%async_computation.1 | async-start | bytes 65536 | tf_op jit(solution)/shard_map/all_to_all | solution.py:469
  49.5 16.5 %copy-start.3 = (s32[4096]{0:T(1024)S(1)}, s32[4096]{0:T(1024)}, u32[]{:S(2)}) copy-start(s32[4096]{0:T(1024)} %param.14) | copy-start | bytes 49156
  49.5 16.5 %copy-start.9 = (s32[3,128]{1,0:T(4,128)S(1)}, s32[3,128]{1,0:T(4,128)}, u32[]{:S(2)}) copy-start(s32[3,128]{1,0:T(4,128)} %far_pairs.1) | copy-start | bytes 4612

commit v2 on v1

--- a/solution.py
+++ b/solution.py
@@ -1,5 +1,3 @@
-import functools
-
 import jax
 import jax.numpy as jnp
 from jax import lax
@@ -20,11 +18,12 @@
 SKEL_ROW = PAIR_ROW + 24
 STRIP_ROWS = SKEL_ROW + GROUP
 SKEL_REC = 24
+MESSAGE_ROWS = 72 + SKEL_REC
 WINDOW = 3 * STRIP_CLUSTERS
 DUMMY = WINDOW
-SELF = WINDOW + 1
 DEPTH = 48
-UNROLL = 2
+UNROLL = 8
+SUMS = 4
 CHUNK = 64
 
 soft_square = 0.01
@@ -58,21 +57,20 @@
     return mask.astype(f32).astype(bf16)
 
 
-def slots_kernel(
-    near_count,
-    points,
-    charges,
-    order,
-    source_basis,
-    transfer,
-    skeleton_points,
-    top_points,
-    near_pairs,
-    own,
-    to_down,
-    to_up,
-    skel_out,
-):
+def slots_kernel(near_count, place, *refs):
+    count = 8
+    held = refs[count + 2 : 2 * count + 2]
+    semaphores = refs[2 * count + 2]
+    own, message = refs[count : count + 2]
+    copies = [
+        pltpu.make_async_copy(refs[i], held[i], semaphores.at[i]) for i in range(count)
+    ]
+    for copy in copies:
+        copy.start()
+    order, points, charges, near_pairs, source_basis, transfer, skeleton_points, top_points = held
+    narrow_index = place[1]
+    for copy in copies[:4]:
+        copy.wait()
     low = order[...] & (LANES - 1)
     high = order[...] >> 7
     sub = iota((8, LANES), 0)
@@ -91,16 +89,13 @@
             found = jnp.take_along_axis(tables[row], low_tile, axis=1)
             values = jnp.where(high_tile == row, found, values)
         own[8 * tile : 8 * tile + 8, :] = values
-        if tile < 8:
-            to_down[8 * tile : 8 * tile + 8, :] = values
-        else:
-            to_up[8 * tile - 64 : 8 * tile - 56, :] = values
         tiles.append(values)
 
     pairs = jnp.where(iota((2, 64), 1) < near_count[0], near_pairs[...] + 1, 0).astype(f32)
-    for ref, start in ((own, 128), (to_down, 64), (to_up, 64)):
-        ref[start : start + 8, :] = jnp.zeros((8, LANES), f32)
-        ref[start : start + 2, 0:64] = pairs
+    own[128:136, :] = jnp.zeros((8, LANES), f32)
+    own[128:130, 0:64] = pairs
+    for copy in copies[4:]:
+        copy.wait()
 
     lane = iota((R, LANES), 1)
     skel = jnp.zeros((R, LANES), f32)
@@ -135,8 +130,34 @@
     top_row = jnp.sum(jnp.where(top_mine, top, 0.0), axis=0, keepdims=True)
     last = jnp.where(iota((8, LANES), 0) == 1, top_row, 0.0)
     record = record + jnp.concatenate([geometry, last], axis=0)
-    for copy in range(NARROW):
-        skel_out[copy] = record
+    pair_block = own[128:136, :]
+    for device in range(NARROW):
+        for tile in range(8):
+            message[device, 8 * tile : 8 * tile + 8, :] = jnp.where(
+                narrow_index < device, tiles[8 + tile], tiles[tile]
+            )
+        message[device, 64:72, :] = jnp.where(narrow_index == device, 0.0, pair_block)
+        message[device, 72:, :] = record
+
+
+def strip_kernel(place, received, own, strip, top_message):
+    narrow_index = place[1]
+    down = jnp.maximum(narrow_index - 1, 0)
+    up = jnp.minimum(narrow_index + 1, NARROW - 1)
+    strip[0:64, :] = received[down, 0:64, :]
+    strip[64:192, :] = own[0:128, :]
+    strip[192:256, :] = received[up, 0:64, :]
+    strip[PAIR_ROW : PAIR_ROW + 8, :] = received[down, 64:72, :]
+    strip[PAIR_ROW + 8 : PAIR_ROW + 16, :] = own[128:136, :]
+    strip[PAIR_ROW + 16 : PAIR_ROW + 24, :] = received[up, 64:72, :]
+    last = received[0, 88:96, :]
+    row = last[0:1] + last[1:2]
+    for device in range(NARROW):
+        start = SKEL_ROW + device * CLUSTERS
+        strip[start : start + CLUSTERS, :] = received[device, 72:88, :]
+        if device > 0:
+            row = row + received[device, 88:96, :][0:1]
+    top_message[...] = jnp.broadcast_to(row, top_message.shape)
 
 
 def with_norms(halves, origin):
@@ -172,15 +193,70 @@
     return jnp.concatenate(columns, axis=0)
 
 
+def cluster_halves(ref, block, odd):
+    halves = []
+    for half in range(2):
+        tile = ref[pl.ds(pl.multiple_of(16 * block + 8 * half, 8), 8), :]
+        halves.append(pltpu.roll(tile, 4, 0) if odd else tile)
+    return halves
+
+
+def own_origin(ref, start):
+    whole = jnp.zeros((8, LANES), f32)
+    for tile in range(CLUSTERS):
+        whole = whole + ref[start + 8 * tile : start + 8 * tile + 8, :]
+    mean = jnp.sum(whole, axis=1, keepdims=True) * (1.0 / (CLUSTERS * C))
+    mean = jnp.broadcast_to(mean, (8, LANES))
+    return jnp.where(iota((8, LANES), 0) < 3, mean + pltpu.roll(mean, 4, 0), 0.0)
+
+
+def weighted(left, right, charge_low, charge_high, store):
+    for start in range(0, C, CHUNK):
+        square = jnp.dot(left(start), right, preferred_element_type=f32)
+        inverse = lax.rsqrt(jnp.maximum(square, soft_square))
+        store(start, inverse[:, :LANES] * charge_low + inverse[:, LANES:] * charge_high)
+
+
+def self_kernel(own, lhs, near, held):
+    origin = own_origin(own, 0)
+
+    def block_step(block, carry):
+        for odd in range(2):
+            halves = cluster_halves(own, block, odd)
+            lhs[2 * block + odd] = target_features(halves, origin)
+            centre = jnp.sum(halves[0] + halves[1], axis=1, keepdims=True) * (1.0 / C)
+            left = target_features(halves, centre)
+
+            def store(start, value):
+                held[odd, start : start + CHUNK, :] = value
+
+            weighted(
+                lambda start: left[start : start + CHUNK],
+                source_features(halves, centre),
+                halves[0][3:4],
+                halves[1][3:4],
+                store,
+            )
+            for half in range(2):
+                part = held[odd, half * LANES : (half + 1) * LANES, :]
+                near[pl.ds(2 * (2 * block + odd) + half, 1), :] = kernel_scale * jnp.sum(
+                    part.T, axis=0, keepdims=True
+                )
+        return carry
+
+    lax.fori_loop(0, CLUSTERS // 2, block_step, 0)
+
+
 def near_kernel(
     place,
     before,
     strip,
     after,
+    lhs,
+    self_rows,
     near,
     features,
     charge,
-    lhs,
     entries_vmem,
     entries,
     semaphore,
@@ -188,14 +264,6 @@
 ):
     wide_index = place[0]
     narrow_index = place[1]
-    sub = iota((8, LANES), 0)
-
-    def cluster_halves(ref, block, odd):
-        halves = []
-        for half in range(2):
-            tile = ref[pl.ds(pl.multiple_of(16 * block + 8 * half, 8), 8), :]
-            halves.append(pltpu.roll(tile, 4, 0) if odd else tile)
-        return halves
 
     def put_source(slot, halves, origin):
         features[slot] = source_features(halves, origin)
@@ -259,26 +327,9 @@
     copy = pltpu.make_async_copy(entries_vmem, entries, semaphore)
     copy.start()
 
-    whole = jnp.zeros((8, LANES), f32)
-    for block in range(8):
-        for half in range(2):
-            start = 64 + 16 * block + 8 * half
-            whole = whole + strip[start : start + 8, :]
-    mean = jnp.sum(whole, axis=1, keepdims=True) * (1.0 / (CLUSTERS * C))
-    mean = jnp.broadcast_to(mean, (8, LANES))
-    origin = jnp.where(sub < 3, mean + pltpu.roll(mean, 4, 0), 0.0)
-
-    def own_block(block, carry):
-        for odd in range(2):
-            cluster = 2 * block + odd
-            halves = cluster_halves(strip, block + 4, odd)
-            lhs[cluster] = target_features(halves, origin)
-            centre = jnp.sum(halves[0] + halves[1], axis=1, keepdims=True) * (1.0 / C)
-            lhs[CLUSTERS + cluster] = target_features(halves, centre)
-            put_source(SELF + cluster, halves, centre)
-        return carry
-
-    lax.fori_loop(0, CLUSTERS // 2, own_block, 0)
+    for total in sums:
+        total[...] = jnp.zeros(total.shape, f32)
+    origin = own_origin(strip, 64)
 
     def window_block(block, carry):
         for part, ref in enumerate((before, strip, after)):
@@ -292,31 +343,6 @@
     features[DUMMY] = jnp.zeros((DEPTH, C), bf16)
     charge[DUMMY] = jnp.zeros((8, C), f32)
 
-    def interact(left, slot, first):
-        rhs = features[slot]
-        charge_low = charge[slot, 0:1, 0:LANES]
-        charge_high = charge[slot, 0:1, LANES:C]
-        for start in range(0, C, CHUNK):
-            square = jnp.dot(
-                lhs[left, start : start + CHUNK, :], rhs, preferred_element_type=f32
-            )
-            inverse = lax.rsqrt(jnp.maximum(square, soft_square))
-            first(start, inverse[:, :LANES] * charge_low + inverse[:, LANES:] * charge_high)
-
-    def self_step(step, carry):
-        for turn in range(UNROLL):
-            cluster = step * UNROLL + turn
-
-            def store(start, value):
-                for other_turn in range(UNROLL):
-                    sums[other_turn][cluster, start : start + CHUNK, :] = (
-                        value if other_turn == turn else jnp.zeros_like(value)
-                    )
-
-            interact(CLUSTERS + cluster, SELF + cluster, store)
-        return carry
-
-    lax.fori_loop(0, CLUSTERS // UNROLL, self_step, 0)
     copy.wait()
     pair_total = entries[7, 0]
 
@@ -329,9 +355,15 @@
             slot = jnp.where(live, code & (LANES - 1), DUMMY)
 
             def add(start, value):
-                sums[turn][cluster, start : start + CHUNK, :] += value
-
-            interact(cluster, slot, add)
+                sums[turn % SUMS][cluster, start : start + CHUNK, :] += value
+
+            weighted(
+                lambda start: lhs[cluster, start : start + CHUNK, :],
+                features[slot],
+                charge[slot, 0:1, 0:LANES],
+                charge[slot, 0:1, LANES:C],
+                add,
+            )
         return carry
 
     lax.fori_loop(0, (pair_total + UNROLL - 1) // UNROLL, pair_step, 0)
@@ -340,10 +372,12 @@
         for half in range(2):
             rows = slice(half * LANES, (half + 1) * LANES)
             total = sums[0][cluster, rows, :]
-            for turn in range(1, UNROLL):
+            for turn in range(1, SUMS):
                 total = total + sums[turn][cluster, rows, :]
             row = 2 * cluster + half
-            near[row : row + 1, :] = kernel_scale * jnp.sum(total.T, axis=0, keepdims=True)
+            near[row : row + 1, :] = self_rows[row : row + 1, :] + kernel_scale * jnp.sum(
+                total.T, axis=0, keepdims=True
+            )
 
 
 def far_kernel(
@@ -352,15 +386,21 @@
     before,
     strip,
     after,
-    own_skel,
     top,
     far_pairs,
     near,
+    order_in,
+    target_basis_in,
+    potential,
+    total,
     order,
     target_basis,
-    potential,
-    total,
+    semaphores,
 ):
+    order_copy = pltpu.make_async_copy(order_in, order, semaphores.at[0])
+    basis_copy = pltpu.make_async_copy(target_basis_in, target_basis, semaphores.at[1])
+    order_copy.start()
+    basis_copy.start()
     wide_index = place[0]
     narrow_index = place[1]
     first = wide_index * GROUP + narrow_index * CLUSTERS
@@ -374,8 +414,10 @@
     chosen = as_bf16(iota((table.shape[0], LANES), 0) == index)
     over_rows = ((0,), (0,))
     sources = parts_dot(table, chosen, over_rows)
+    own_start = pl.multiple_of(SKEL_ROW + narrow_index * CLUSTERS, 8)
+    own_skel = strip[pl.ds(own_start, CLUSTERS), :]
     own_chosen = as_bf16(iota((CLUSTERS, LANES), 0) == target)
-    targets = parts_dot(own_skel[0, :CLUSTERS, :], own_chosen, over_rows)
+    targets = parts_dot(own_skel, own_chosen, over_rows)
     rows = []
     for a in range(R):
         square = soft_square
@@ -385,6 +427,7 @@
         product = lax.rsqrt(square) * sources[3 * R :]
         rows.append(jnp.sum(product, axis=0, keepdims=True))
     middle = jnp.where(live, jnp.concatenate(rows, axis=0) * kernel_scale, 0.0)
+    basis_copy.wait()
     for cluster in range(CLUSTERS):
         column = jnp.sum(jnp.where(target == cluster, middle, 0.0), axis=1, keepdims=True)
         spread = jnp.sum(
@@ -395,6 +438,7 @@
             total[row : row + 1, :] = (
                 near[row : row + 1, :] + spread[:, half * LANES : (half + 1) * LANES]
             )
+    order_copy.wait()
     low = order[...] & (LANES - 1)
     high = order[...] >> 7
     out = jnp.zeros((ROWS, LANES), f32)
@@ -409,6 +453,10 @@
 
 def smem():
     return pl.BlockSpec(memory_space=pltpu.SMEM)
+
+
+def anywhere():
+    return pl.BlockSpec(memory_space=pl.ANY)
 
 
 def vmem():
@@ -433,94 +481,83 @@
     far_count,
 ):
     wide_size = lax.axis_size("wide")
-    narrow_size = lax.axis_size("narrow")
     place = jnp.stack([lax.axis_index("wide"), lax.axis_index("narrow")]).astype(i32)
     order = order.reshape(ROWS, LANES)
     shape = jax.ShapeDtypeStruct
+    inputs = (
+        order,
+        points,
+        charges.reshape(ROWS, LANES),
+        near_pairs,
+        source_basis,
+        transfer,
+        skeleton_points,
+        top_points,
+    )
     with jax.named_scope("slots"):
-        own, to_down, to_up, skel = pl.pallas_call(
+        own, message = pl.pallas_call(
             slots_kernel,
             out_shape=(
                 shape((136, LANES), f32),
-                shape((72, LANES), f32),
-                shape((72, LANES), f32),
-                shape((NARROW, SKEL_REC, LANES), f32),
+                shape((NARROW, MESSAGE_ROWS, LANES), f32),
             ),
-            in_specs=[smem()] + [vmem()] * 8,
-            out_specs=[vmem()] * 4,
+            in_specs=[smem(), smem()] + [anywhere()] * len(inputs),
+            out_specs=[vmem()] * 2,
+            scratch_shapes=[pltpu.VMEM(x.shape, x.dtype) for x in inputs]
+            + [pltpu.SemaphoreType.DMA((len(inputs),))],
             compiler_params=params,
-        )(
-            near_count,
-            points,
-            charges.reshape(ROWS, LANES),
-            order,
-            source_basis,
-            transfer,
-            skeleton_points,
-            top_points,
-            near_pairs,
-        )
-    upward = [(i, i + 1) for i in range(narrow_size - 1)]
-    downward = [(i + 1, i) for i in range(narrow_size - 1)]
-    from_down = lax.ppermute(to_up, "narrow", upward)
-    from_up = lax.ppermute(to_down, "narrow", downward)
-    skels = lax.all_to_all(skel, "narrow", 0, 0, tiled=True)
-    message = jnp.sum(skels[:, CLUSTERS, :], axis=0) + skels[0, CLUSTERS + 1, :]
-    tops = lax.all_to_all(
-        jnp.broadcast_to(message[None, None, :], (wide_size, 1, LANES)), "wide", 0, 0, tiled=True
-    )
-    strip = jnp.concatenate(
-        [
-            from_down[:64],
-            own[:128],
-            from_up[:64],
-            from_down[64:],
-            own[128:],
-            from_up[64:],
-            skels[:, :CLUSTERS, :].reshape(GROUP, LANES),
-        ],
-        axis=0,
-    )
+        )(near_count, place, *inputs)
+    received = lax.all_to_all(message, "narrow", 0, 0, tiled=True)
+    with jax.named_scope("self"):
+        lhs, self_rows = pl.pallas_call(
+            self_kernel,
+            out_shape=(shape((CLUSTERS, C, DEPTH), bf16), shape((ROWS, LANES), f32)),
+            in_specs=[vmem()],
+            out_specs=[vmem()] * 2,
+            scratch_shapes=[pltpu.VMEM((2, C, LANES), f32)],
+            compiler_params=params,
+        )(own)
+    with jax.named_scope("strip"):
+        strip, top_message = pl.pallas_call(
+            strip_kernel,
+            out_shape=(shape((STRIP_ROWS, LANES), f32), shape((wide_size, LANES), f32)),
+            in_specs=[smem()] + [vmem()] * 2,
+            out_specs=[vmem()] * 2,
+            compiler_params=params,
+        )(place, received, own)
     before = lax.ppermute(strip, "wide", [(i, i + 1) for i in range(wide_size - 1)])
     after = lax.ppermute(strip, "wide", [(i + 1, i) for i in range(wide_size - 1)])
+    tops = lax.all_to_all(top_message, "wide", 0, 0, tiled=True)
     with jax.named_scope("near"):
         near = pl.pallas_call(
             near_kernel,
             out_shape=shape((ROWS, LANES), f32),
-            in_specs=[smem()] + [vmem()] * 3,
+            in_specs=[smem()] + [vmem()] * 5,
             out_specs=vmem(),
             scratch_shapes=[
-                pltpu.VMEM((SELF + CLUSTERS, DEPTH, C), bf16),
-                pltpu.VMEM((SELF + CLUSTERS, 8, C), f32),
-                pltpu.VMEM((2 * CLUSTERS, C, DEPTH), bf16),
+                pltpu.VMEM((WINDOW + 1, DEPTH, C), bf16),
+                pltpu.VMEM((WINDOW + 1, 8, C), f32),
                 pltpu.VMEM((8, LANES), i32),
                 pltpu.SMEM((8, LANES), i32),
                 pltpu.SemaphoreType.DMA(()),
             ]
-            + [pltpu.VMEM((CLUSTERS, C, LANES), f32)] * UNROLL,
+            + [pltpu.VMEM((CLUSTERS, C, LANES), f32)] * SUMS,
             compiler_params=params,
-        )(place, before, strip, after)
+        )(place, before, strip, after, lhs, self_rows)
     with jax.named_scope("far"):
         potential = pl.pallas_call(
             far_kernel,
             out_shape=shape((ROWS, LANES), f32),
-            in_specs=[smem(), smem()] + [vmem()] * 9,
+            in_specs=[smem(), smem()] + [vmem()] * 6 + [anywhere()] * 2,
             out_specs=vmem(),
-            scratch_shapes=[pltpu.VMEM((ROWS, LANES), f32)],
+            scratch_shapes=[
+                pltpu.VMEM((ROWS, LANES), f32),
+                pltpu.VMEM((ROWS, LANES), i32),
+                pltpu.VMEM(target_basis.shape, f32),
+                pltpu.SemaphoreType.DMA((2,)),
+            ],
             compiler_params=params,
-        )(
-            place,
-            far_count,
-            before,
-            strip,
-            after,
-            skel,
-            tops.reshape(wide_size, LANES),
-            far_pairs,
-            near,
-            order,
-            target_basis,
-        )
+        )(place, far_count, before, strip, after, tops, far_pairs, near, order, target_basis)
     return potential.reshape(-1)
 
 

time: 70.8 us -> 65.7 us (0.928)
  the two profiles are of different devices: /device:TPU:8 before, /device:TPU:2 now
where the time goes in v2:
time: 65.7 us; the launch traced here: 65.2 us
  starting transfers between devices  21.6 us (33%)
  Pallas kernels  17.1 us (26%)
  blocking collectives  15.8 us (24%)
  local copies, waits for them, and re-layouts  4.84 us (7%)
  waiting for transfers between devices  4.35 us (7%)
  between operations  1.4 us (2%)
    all_to_all x1, starting transfers between devices, local(): tops = lax.all_to_all(top_message, 'wide', 0, 0, tiled=True)  19 us
    all_to_all x1, blocking collectives, local(): received = lax.all_to_all(message, 'narrow', 0, 0, tiled=True)  15.8 us
    pallas_call x1, Pallas kernels, local(): pl.pallas_call(near_kernel, out_shape=shape((ROWS, LANES), f32), in_specs...  5.86 us
    unnamed x20, local copies, waits for them, and re-layouts  4.84 us
    all_to_all x1, waiting for transfers between devices, local(): tops = lax.all_to_all(top_message, 'wide', 0, 0, tiled=True)  4.35 us
    pallas_call x1, Pallas kernels, local(): pl.pallas_call(far_kernel, out_shape=shape((ROWS, LANES), f32), in_specs=...  3.87 us
    pallas_call x1, Pallas kernels, local(): pl.pallas_call(self_kernel, out_shape=(shape((CLUSTERS, C, DEPTH), bf16),...  3.86 us
    pallas_call x1, Pallas kernels, local(): pl.pallas_call(slots_kernel, out_shape=(shape((136, LANES), f32), shape((...  2.36 us
  transfers between devices with their start and end apart: 3, of which 1 were waited for; matrix products, arithmetic and copies ran while one was open for 0% of the time, Pallas kernels for 15%

profile of v2, /device:TPU:2, one launch (start us, length us, event | category | flops | bytes accessed | tf_op | source)
XLA Modules:
  0.0 65.2 jit_solution(16577826734967586157)
XLA Ops:
  0.7 0.1 pad_add_fusion.place
  0.7 0.0 copy-done.2
  0.7 0.7 %copy-done.7 = f32[3,32]{1,0:T(4,128)S(1)} copy-done((f32[3,32]{1,0:T(4,128)S(1)}, f32[3,32]{1,0:T(4,128)}, u32[]{:S(2)}) %copy-start.7) | copy-done | bytes 408
  1.4 0.0 copy-done.9
  1.4 1.0 %copy-done = f32[32,4096]{1,0:T(8,128)S(1)} copy-done((f32[32,4096]{1,0:T(8,128)S(1)}, f32[32,4096]{1,0:T(8,128)}, u32[]{:S(2)}) %copy-start) | copy-done | bytes 524312
  2.5 0.8 %copy-done.3 = f32[3,4096]{1,0:T(4,128)S(1)} copy-done((f32[3,4096]{1,0:T(4,128)S(1)}, f32[3,4096]{1,0:T(4,128)}, u32[]{:S(2)}) %copy-start.3) | copy-done | bytes 49176
  3.3 0.8 %copy-done.4 = f32[32,512]{1,0:T(8,128)S(1)} copy-done((f32[32,512]{1,0:T(8,128)S(1)}, f32[32,512]{1,0:T(8,128)}, u32[]{:S(2)}) %copy-start.4) | copy-done | bytes 65560
  4.2 0.7 %copy-done.5 = f32[4096]{0:T(1024)S(1)} copy-done((f32[4096]{0:T(1024)S(1)}, f32[4096]{0:T(1024)}, u32[]{:S(2)}) %copy-start.5) | copy-done | bytes 16408
  4.9 0.7 %copy-done.6 = f32[3,512]{1,0:T(4,128)S(1)} copy-done((f32[3,512]{1,0:T(4,128)S(1)}, f32[3,512]{1,0:T(4,128)}, u32[]{:S(2)}) %copy-start.6) | copy-done | bytes 6168
  5.6 2.4 %slots.1 = (f32[136,128]{1,0:T(8,128)S(1)}, f32[8,96,128]{2,1,0:T(8,128)S(1)}) custom-call(s32[1]{0:T(128)S(6)} %copy.14.near_count, s32[2]{0:T(128)S(1)} %pad_add_fusion.place, s32[32,128]{1,0:T(8,128)S(1)} %bitcast.10, f32[3,4096]{1,0:T(4,128)S(1)} %copy-done.3, f32[32,128]{1,0:T(8,128)S(1)} %bitcast.12, s32[2,64]{1,0:T(2,128)S(1)} %copy-done.9, ...), custom_call_target="tpu_custom_call" | custom-call | tf_op jit(solution)/shard_map/slots/pallas_call | solution.py:498
  7.9 15.8 %all_to_all.16.received = f32[8,96,128]{2,1,0:T(8,128)S(1)} all-to-all(f32[8,96,128]{2,1,0:T(8,128)S(1)} %get-tuple-element.11), channel_id=1, replica_groups=mesh['wide'=64,'narrow'=8] {'narrow'}, dimensions={0} | all-to-all | bytes 786432 | tf_op jit(solution)/shard_map/all_to_all | solution.py:510
  23.7 1.2 %strip.1 = (f32[408,128]{1,0:T(8,128)S(1)}, f32[64,128]{1,0:T(8,128)}) custom-call(s32[2]{0:T(128)S(1)} %pad_add_fusion.place, f32[8,96,128]{2,1,0:T(8,128)S(1)} %all_to_all.16.received, f32[136,128]{1,0:T(8,128)S(1)} %get-tuple-element.12.own), custom_call_target="tpu_custom_call" | custom-call | tf_op jit(solution)/shard_map/strip/pallas_call | solution.py:521
  24.9 1.3 %collective-permute-start = (f32[408,128]{1,0:T(8,128)S(1)}, f32[408,128]{1,0:T(8,128)S(1)}, u32[]{:S(2)}, u32[]{:S(2)}) collective-permute-start(f32[408,128]{1,0:T(8,128)S(1)} %get-tuple-element.13.strip), channel_id=1, source_target_pairs={{0,8},{8,16},{16,24},{24,32},{32,40},{40,48},{48,56},{56,64},{64,7... | collective-permute-start | bytes 626696 | tf_op jit(solution)/shard_map/ppermute | solution.py:528
  26.2 1.3 %collective-permute-start.1 = (f32[408,128]{1,0:T(8,128)S(1)}, f32[408,128]{1,0:T(8,128)S(1)}, u32[]{:S(2)}, u32[]{:S(2)}) collective-permute-start(f32[408,128]{1,0:T(8,128)S(1)} %get-tuple-element.13.strip), channel_id=1, source_target_pairs={{8,0},{16,8},{24,16},{32,24},{40,32},{48,40},{56,48},{64,56},{72,6... | collective-permute-start | bytes 626696 | tf_op jit(solution)/shard_map/ppermute | solution.py:529
  27.5 19.0 %all-to-all-start.1 = ((f32[64,1,128]{2,1,0:T(1,128)}), f32[64,1,128]{2,1,0:T(1,128)S(1)}, u32[]{:S(2)}, u32[]{:S(2)}) async-start(f32[64,1,128]{2,1,0:T(1,128)} %bitcast.5), calls=%async_computation.1 | async-start | bytes 65536 | tf_op jit(solution)/shard_map/all_to_all | solution.py:530
  46.5 3.9 %self.1 = (bf16[16,256,48]{2,1,0:T(8,128)(2,1)S(1)}, f32[32,128]{1,0:T(8,128)S(1)}) custom-call(f32[136,128]{1,0:T(8,128)S(1)} %get-tuple-element.12.own), custom_call_target="tpu_custom_call" | custom-call | tf_op jit(solution)/shard_map/self/pallas_call | solution.py:512
  51.0 0.0 collective-permute-done.before
  51.0 0.0 collective-permute-done.1.after
  51.0 0.0 copy-start.1
  51.1 0.0 copy-start.8
  51.1 5.9 %near.1 = f32[32,128]{1,0:T(8,128)S(1)} custom-call(s32[2]{0:T(128)S(1)} %pad_add_fusion.place, f32[408,128]{1,0:T(8,128)S(1)} %collective-permute-done.before, f32[408,128]{1,0:T(8,128)S(1)} %get-tuple-element.13.strip, f32[408,128]{1,0:T(8,128)S(1)} %collective-permute-done.1.after, bf16[16,256,48]{2,1,0:T(8,128)(2,1)S(1)} %get-tuple-element.15.lhs, ...), custom_call_target="tpu_custom_call" | custom-call | tf_op jit(solution)/shard_map/near/pallas_call | solution.py:532
  56.9 4.3 %all-to-all-done.1 = f32[64,1,128]{2,1,0:T(1,128)S(1)} async-done(((f32[64,1,128]{2,1,0:T(1,128)}), f32[64,1,128]{2,1,0:T(1,128)S(1)}, u32[]{:S(2)}, u32[]{:S(2)}) %all-to-all-start.1) | async-done | bytes 32800 | tf_op jit(solution)/shard_map/all_to_all | solution.py:530
  61.3 0.0 copy-done.8
  61.3 3.9 %far.1 = f32[32,128]{1,0:T(8,128)} custom-call(s32[2]{0:T(128)S(1)} %pad_add_fusion.place, s32[1]{0:T(128)S(6)} %copy.15.far_count, f32[408,128]{1,0:T(8,128)S(1)} %collective-permute-done.before, f32[408,128]{1,0:T(8,128)S(1)} %get-tuple-element.13.strip, f32[408,128]{1,0:T(8,128)S(1)} %collective-permute-done.1.after, f32[64,128]{1,0:T(8,128)S(1)} %bitcast.9, ...), custom_call_target="tpu_custom_call" | custom-call | tf_op jit(solution)/shard_map/far/pallas_call | solution.py:548
  (9 shorter events, 0.0 us)
Async XLA Ops:
  0.0 0.7 %copy-start.2 = (s32[4096]{0:T(1024)S(1)}, s32[4096]{0:T(1024)}, u32[]{:S(2)}) copy-start(s32[4096]{0:T(1024)} %param.14) | copy-start | bytes 49156
  0.7 0.7 %copy-start.7 = (f32[3,32]{1,0:T(4,128)S(1)}, f32[3,32]{1,0:T(4,128)}, u32[]{:S(2)}) copy-start(f32[3,32]{1,0:T(4,128)} %refs_7_.1) | copy-start | bytes 1156
  0.7 0.7 %copy-start.9 = (s32[2,64]{1,0:T(2,128)S(1)}, s32[2,64]{1,0:T(2,128)}, u32[]{:S(2)}) copy-start(s32[2,64]{1,0:T(2,128)} %refs_3_.1) | copy-start | bytes 1540
  1.4 1.0 %copy-start = (f32[32,4096]{1,0:T(8,128)S(1)}, f32[32,4096]{1,0:T(8,128)}, u32[]{:S(2)}) copy-start(f32[32,4096]{1,0:T(8,128)} %refs_4_.1) | copy-start | bytes 1572868
  2.5 0.8 %copy-start.3 = (f32[3,4096]{1,0:T(4,128)S(1)}, f32[3,4096]{1,0:T(4,128)}, u32[]{:S(2)}) copy-start(f32[3,4096]{1,0:T(4,128)} %refs_1_.1) | copy-start | bytes 147460
  3.3 0.8 %copy-start.4 = (f32[32,512]{1,0:T(8,128)S(1)}, f32[32,512]{1,0:T(8,128)}, u32[]{:S(2)}) copy-start(f32[32,512]{1,0:T(8,128)} %refs_5_.1) | copy-start | bytes 196612
  4.2 0.7 %copy-start.5 = (f32[4096]{0:T(1024)S(1)}, f32[4096]{0:T(1024)}, u32[]{:S(2)}) copy-start(f32[4096]{0:T(1024)} %param.13) | copy-start | bytes 49156
  4.9 0.7 %copy-start.6 = (f32[3,512]{1,0:T(4,128)S(1)}, f32[3,512]{1,0:T(4,128)}, u32[]{:S(2)}) copy-start(f32[3,512]{1,0:T(4,128)} %refs_6_.1) | copy-start | bytes 18436
  24.9 26.1 %collective-permute-start = (f32[408,128]{1,0:T(8,128)S(1)}, f32[408,128]{1,0:T(8,128)S(1)}, u32[]{:S(2)}, u32[]{:S(2)}) collective-permute-start(f32[408,128]{1,0:T(8,128)S(1)} %get-tuple-element.13.strip), channel_id=1, source_target_pairs={{0,8},{8,16},{16,24},{24,32},{32,40},{40,48},{48,56},{56,64},{64,7... | collective-permute-start | bytes 626696 | tf_op jit(solution)/shard_map/ppermute | solution.py:528
  26.2 24.8 %collective-permute-start.1 = (f32[408,128]{1,0:T(8,128)S(1)}, f32[408,128]{1,0:T(8,128)S(1)}, u32[]{:S(2)}, u32[]{:S(2)}) collective-permute-start(f32[408,128]{1,0:T(8,128)S(1)} %get-tuple-element.13.strip), channel_id=1, source_target_pairs={{8,0},{16,8},{24,16},{32,24},{40,32},{48,40},{56,48},{64,56},{72,6... | collective-permute-start | bytes 626696 | tf_op jit(solution)/shard_map/ppermute | solution.py:529
  27.5 33.8 %all-to-all-start.1 = ((f32[64,1,128]{2,1,0:T(1,128)}), f32[64,1,128]{2,1,0:T(1,128)S(1)}, u32[]{:S(2)}, u32[]{:S(2)}) async-start(f32[64,1,128]{2,1,0:T(1,128)} %bitcast.5), calls=%async_computation.1 | async-start | bytes 65536 | tf_op jit(solution)/shard_map/all_to_all | solution.py:530
  51.0 10.2 %copy-start.1 = (f32[32,4096]{1,0:T(8,128)S(1)}, f32[32,4096]{1,0:T(8,128)}, u32[]{:S(2)}) copy-start(f32[32,4096]{1,0:T(8,128)} %target_basis_in.1) | copy-start | bytes 1572868
  51.1 10.2 %copy-start.8 = (s32[3,128]{1,0:T(4,128)S(1)}, s32[3,128]{1,0:T(4,128)}, u32[]{:S(2)}) copy-start(s32[3,128]{1,0:T(4,128)} %far_pairs.1) | copy-start | bytes 4612

commit v3 on v2

--- a/solution.py
+++ b/solution.py
@@ -140,7 +140,8 @@
         message[device, 72:, :] = record
 
 
-def strip_kernel(place, received, own, strip, top_message):
+def strip_kernel(place, received, own, self_rows, strip, top_message):
+    del self_rows
     narrow_index = place[1]
     down = jnp.maximum(narrow_index - 1, 0)
     up = jnp.minimum(narrow_index + 1, NARROW - 1)
@@ -389,18 +390,11 @@
     top,
     far_pairs,
     near,
-    order_in,
-    target_basis_in,
+    order,
+    target_basis,
     potential,
     total,
-    order,
-    target_basis,
-    semaphores,
 ):
-    order_copy = pltpu.make_async_copy(order_in, order, semaphores.at[0])
-    basis_copy = pltpu.make_async_copy(target_basis_in, target_basis, semaphores.at[1])
-    order_copy.start()
-    basis_copy.start()
     wide_index = place[0]
     narrow_index = place[1]
     first = wide_index * GROUP + narrow_index * CLUSTERS
@@ -427,7 +421,6 @@
         product = lax.rsqrt(square) * sources[3 * R :]
         rows.append(jnp.sum(product, axis=0, keepdims=True))
     middle = jnp.where(live, jnp.concatenate(rows, axis=0) * kernel_scale, 0.0)
-    basis_copy.wait()
     for cluster in range(CLUSTERS):
         column = jnp.sum(jnp.where(target == cluster, middle, 0.0), axis=1, keepdims=True)
         spread = jnp.sum(
@@ -438,16 +431,24 @@
             total[row : row + 1, :] = (
                 near[row : row + 1, :] + spread[:, half * LANES : (half + 1) * LANES]
             )
-    order_copy.wait()
     low = order[...] & (LANES - 1)
     high = order[...] >> 7
-    out = jnp.zeros((ROWS, LANES), f32)
     tall = iota((LANES, LANES), 0)
     wide = iota((ROWS, LANES), 0)
+    whole = [part.astype(f32) for part in split3(total[...])]
+    values, places = [], []
     for row in range(ROWS):
         here = wide == high[row : row + 1]
-        value = jnp.where(here, total[row : row + 1, :], 0.0)
-        out = out + parts_dot(value, as_bf16(tall == low[row : row + 1]), ((1,), (1,)))
+        parts = [jnp.where(here, part[row : row + 1, :], 0.0) for part in whole]
+        values.append(jnp.concatenate(parts, axis=0).astype(bf16))
+        places.append(as_bf16(tall == low[row : row + 1]))
+    placed = lax.dot_general(
+        jnp.concatenate(values, axis=1),
+        jnp.concatenate(places, axis=1),
+        (((1,), (1,)), ((), ())),
+        preferred_element_type=f32,
+    )
+    out = placed[:ROWS] + placed[ROWS : 2 * ROWS] + placed[2 * ROWS :]
     potential[...] = out
 
 
@@ -455,8 +456,8 @@
     return pl.BlockSpec(memory_space=pltpu.SMEM)
 
 
-def anywhere():
-    return pl.BlockSpec(memory_space=pl.ANY)
+def in_hbm():
+    return pl.BlockSpec(memory_space=pltpu.HBM)
 
 
 def vmem():
@@ -464,6 +465,7 @@
 
 
 params = pltpu.CompilerParams(vmem_limit_bytes=50 * 1024 * 1024)
+first_params = pltpu.CompilerParams(vmem_limit_bytes=127 * 512 * 1024)
 
 
 def local(
@@ -501,11 +503,11 @@
                 shape((136, LANES), f32),
                 shape((NARROW, MESSAGE_ROWS, LANES), f32),
             ),
-            in_specs=[smem(), smem()] + [anywhere()] * len(inputs),
+            in_specs=[smem(), smem()] + [in_hbm()] * len(inputs),
             out_specs=[vmem()] * 2,
             scratch_shapes=[pltpu.VMEM(x.shape, x.dtype) for x in inputs]
             + [pltpu.SemaphoreType.DMA((len(inputs),))],
-            compiler_params=params,
+            compiler_params=first_params,
         )(near_count, place, *inputs)
     received = lax.all_to_all(message, "narrow", 0, 0, tiled=True)
     with jax.named_scope("self"):
@@ -521,10 +523,10 @@
         strip, top_message = pl.pallas_call(
             strip_kernel,
             out_shape=(shape((STRIP_ROWS, LANES), f32), shape((wide_size, LANES), f32)),
-            in_specs=[smem()] + [vmem()] * 2,
+            in_specs=[smem()] + [vmem()] * 3,
             out_specs=[vmem()] * 2,
             compiler_params=params,
-        )(place, received, own)
+        )(place, received, own, self_rows)
     before = lax.ppermute(strip, "wide", [(i, i + 1) for i in range(wide_size - 1)])
     after = lax.ppermute(strip, "wide", [(i + 1, i) for i in range(wide_size - 1)])
     tops = lax.all_to_all(top_message, "wide", 0, 0, tiled=True)
@@ -548,14 +550,9 @@
         potential = pl.pallas_call(
             far_kernel,
             out_shape=shape((ROWS, LANES), f32),
-            in_specs=[smem(), smem()] + [vmem()] * 6 + [anywhere()] * 2,
+            in_specs=[smem(), smem()] + [vmem()] * 8,
             out_specs=vmem(),
-            scratch_shapes=[
-                pltpu.VMEM((ROWS, LANES), f32),
-                pltpu.VMEM((ROWS, LANES), i32),
-                pltpu.VMEM(target_basis.shape, f32),
-                pltpu.SemaphoreType.DMA((2,)),
-            ],
+            scratch_shapes=[pltpu.VMEM((ROWS, LANES), f32)],
             compiler_params=params,
         )(place, far_count, before, strip, after, tops, far_pairs, near, order, target_basis)
     return potential.reshape(-1)

time: 65.7 us -> 62.8 us (0.956)
  blocking collectives: 15.8 us -> 0 us
  starting transfers between devices: 21.6 us -> 31.5 us
  waiting for transfers between devices: 4.35 us -> 10.1 us
  local copies, waits for them, and re-layouts: 4.84 us -> 0.03 us
  Pallas kernels: 17.1 us -> 18.8 us
    all_to_all x1 -> x0, blocking collectives: 15.8 us -> none  [local(): received = lax.all_to_all(message, 'narrow', 0, 0, tiled=True)]
    all_to_all x0 -> x1, starting transfers between devices: none -> 9.41 us  [local(): received = lax.all_to_all(message, 'narrow', 0, 0, tiled=True)]
    unnamed x20 -> x10, local copies, waits for them, and re-layouts: 4.84 us -> 0.03 us
    all_to_all x0 -> x1, waiting for transfers between devices: none -> 3.64 us  [local(): received = lax.all_to_all(message, 'narrow', 0, 0, tiled=True)]
    ppermute x1, starting transfers between devices: 1.29 us -> 4.56 us  [local(): lax.ppermute(strip, 'wide', [(i, i + 1) for i in range(wide_size - 1)])]
    all_to_all x1, starting transfers between devices: 19 us -> 16.2 us  [local(): tops = lax.all_to_all(top_message, 'wide', 0, 0, tiled=True)]
    all_to_all x1, waiting for transfers between devices: 4.35 us -> 6.51 us  [local(): tops = lax.all_to_all(top_message, 'wide', 0, 0, tiled=True)]
    pallas_call x1, Pallas kernels: 5.86 us -> 7.53 us  [local(): pl.pallas_call(near_kernel, out_shape=shape((ROWS, LANES), f32), in_specs...]
  transfers between devices with their start and end apart: 3 -> 4, of which waited for: 1 -> 2; matrix products, arithmetic and copies ran while one was open for 0% -> 0% of each run, Pallas kernels for 15% -> 18%
where the time goes in v3:
time: 62.8 us; the launch traced here: 62.5 us
  starting transfers between devices  31.5 us (50%)
  Pallas kernels  18.8 us (30%)
  waiting for transfers between devices  10.1 us (16%)
  between operations  1.41 us (2%)
    all_to_all x1, starting transfers between devices, local(): tops = lax.all_to_all(top_message, 'wide', 0, 0, tiled=True)  16.2 us
    all_to_all x1, starting transfers between devices, local(): received = lax.all_to_all(message, 'narrow', 0, 0, tiled=True)  9.41 us
    pallas_call x1, Pallas kernels, local(): pl.pallas_call(near_kernel, out_shape=shape((ROWS, LANES), f32), in_specs...  7.53 us
    all_to_all x1, waiting for transfers between devices, local(): tops = lax.all_to_all(top_message, 'wide', 0, 0, tiled=True)  6.51 us
    ppermute x1, starting transfers between devices, local(): lax.ppermute(strip, 'wide', [(i, i + 1) for i in range(wide_size - 1)])  4.56 us
    pallas_call x1, Pallas kernels, local(): pl.pallas_call(self_kernel, out_shape=(shape((CLUSTERS, C, DEPTH), bf16),...  3.85 us
    pallas_call x1, Pallas kernels, local(): pl.pallas_call(slots_kernel, out_shape=(shape((136, LANES), f32), shape((...  3.81 us
    all_to_all x1, waiting for transfers between devices, local(): received = lax.all_to_all(message, 'narrow', 0, 0, tiled=True)  3.64 us
  transfers between devices with their start and end apart: 4, of which 2 were waited for; matrix products, arithmetic and copies ran while one was open for 0% of the time, Pallas kernels for 18%

profile of v3, /device:TPU:2, one launch (start us, length us, event | category | flops | bytes accessed | tf_op | source)
XLA Modules:
  0.0 62.5 jit_solution(10541022792219334257)
XLA Ops:
  0.7 0.6 pad_add_fusion.place
  1.2 3.8 %slots.1 = (f32[136,128]{1,0:T(8,128)}, f32[8,96,128]{2,1,0:T(8,128)}) custom-call(s32[1]{0:T(128)S(6)} %copy.14.near_count, s32[2]{0:T(128)} %pad_add_fusion.place, s32[32,128]{1,0:T(8,128)} %bitcast.10, f32[3,4096]{1,0:T(4,128)} %refs_1_.1, f32[32,128]{1,0:T(8,128)} %bitcast.12, s32[2,64]{1,0:T(2,128)} %refs_3_.1, f32[32,4096]{1,0:T(8,128)} %refs_4_.1, ...), custom_call_target="tpu_custom_call" | custom-call | tf_op jit(solution)/shard_map/slots/pallas_call | solution.py:500
  5.1 0.0 copy-start.1
  5.1 9.4 %all-to-all-start = ((f32[8,96,128]{2,1,0:T(8,128)}), f32[8,96,128]{2,1,0:T(8,128)S(1)}, u32[]{:S(2)}, u32[]{:S(2)}) async-start(f32[8,96,128]{2,1,0:T(8,128)} %get-tuple-element.11), calls=%async_computation | async-start | bytes 786432 | tf_op jit(solution)/shard_map/all_to_all | solution.py:512
  14.5 0.0 copy-done.1
  14.5 3.9 %self.1 = (bf16[16,256,48]{2,1,0:T(8,128)(2,1)S(1)}, f32[32,128]{1,0:T(8,128)S(1)}) custom-call(f32[136,128]{1,0:T(8,128)S(1)} %copy-done.1), custom_call_target="tpu_custom_call" | custom-call | tf_op jit(solution)/shard_map/self/pallas_call | solution.py:514
  18.4 0.0 copy-start.3
  18.4 3.6 %all-to-all-done.received = f32[8,96,128]{2,1,0:T(8,128)S(1)} async-done(((f32[8,96,128]{2,1,0:T(8,128)}), f32[8,96,128]{2,1,0:T(8,128)S(1)}, u32[]{:S(2)}, u32[]{:S(2)}) %all-to-all-start) | async-done | bytes 393248 | tf_op jit(solution)/shard_map/all_to_all | solution.py:512
  22.0 0.0 copy-done.3
  22.0 1.2 %strip.1 = (f32[408,128]{1,0:T(8,128)S(1)}, f32[64,128]{1,0:T(8,128)}) custom-call(s32[2]{0:T(128)S(1)} %copy-done.3, f32[8,96,128]{2,1,0:T(8,128)S(1)} %all-to-all-done.received, f32[136,128]{1,0:T(8,128)S(1)} %copy-done.1, f32[32,128]{1,0:T(8,128)S(1)} %get-tuple-element.13.self_rows), custom_call_target="tpu_custom_call" | custom-call | tf_op jit(solution)/shard_map/strip/pallas_call | solution.py:523
  23.2 1.3 %collective-permute-start.1 = (f32[408,128]{1,0:T(8,128)S(1)}, f32[408,128]{1,0:T(8,128)S(1)}, u32[]{:S(2)}, u32[]{:S(2)}) collective-permute-start(f32[408,128]{1,0:T(8,128)S(1)} %get-tuple-element.14.strip), channel_id=1, source_target_pairs={{8,0},{16,8},{24,16},{32,24},{40,32},{48,40},{56,48},{64,56},{72,6... | collective-permute-start | bytes 626696 | tf_op jit(solution)/shard_map/ppermute | solution.py:531
  24.5 4.6 %collective-permute-start = (f32[408,128]{1,0:T(8,128)S(1)}, f32[408,128]{1,0:T(8,128)S(1)}, u32[]{:S(2)}, u32[]{:S(2)}) collective-permute-start(f32[408,128]{1,0:T(8,128)S(1)} %get-tuple-element.14.strip), channel_id=1, source_target_pairs={{0,8},{8,16},{16,24},{24,32},{32,40},{40,48},{48,56},{56,64},{64,7... | collective-permute-start | bytes 626696 | tf_op jit(solution)/shard_map/ppermute | solution.py:530
  29.0 16.2 %all-to-all-start.1 = ((f32[64,1,128]{2,1,0:T(1,128)}), f32[64,1,128]{2,1,0:T(1,128)S(1)}, u32[]{:S(2)}, u32[]{:S(2)}) async-start(f32[64,1,128]{2,1,0:T(1,128)} %bitcast.5), calls=%async_computation.1 | async-start | bytes 65536 | tf_op jit(solution)/shard_map/all_to_all | solution.py:532
  45.9 0.0 collective-permute-done.1.after
  45.9 0.0 collective-permute-done.before
  45.9 0.0 copy-start
  45.9 0.0 copy-start.2
  45.9 0.0 copy-start.4
  45.9 7.5 %near.1 = f32[32,128]{1,0:T(8,128)S(1)} custom-call(s32[2]{0:T(128)S(1)} %copy-done.3, f32[408,128]{1,0:T(8,128)S(1)} %collective-permute-done.before, f32[408,128]{1,0:T(8,128)S(1)} %get-tuple-element.14.strip, f32[408,128]{1,0:T(8,128)S(1)} %collective-permute-done.1.after, bf16[16,256,48]{2,1,0:T(8,128)(2,1)S(1)} %get-tuple-element.16.lhs, ...), custom_call_target="tpu_custom_call" | custom-call | tf_op jit(solution)/shard_map/near/pallas_call | solution.py:534
  53.5 6.5 %all-to-all-done.1 = f32[64,1,128]{2,1,0:T(1,128)S(1)} async-done(((f32[64,1,128]{2,1,0:T(1,128)}), f32[64,1,128]{2,1,0:T(1,128)S(1)}, u32[]{:S(2)}, u32[]{:S(2)}) %all-to-all-start.1) | async-done | bytes 32800 | tf_op jit(solution)/shard_map/all_to_all | solution.py:532
  60.0 0.0 copy-done
  60.0 0.0 copy-done.2
  60.0 0.0 copy-done.4
  60.0 2.5 %far.1 = f32[32,128]{1,0:T(8,128)} custom-call(s32[2]{0:T(128)S(1)} %copy-done.3, s32[1]{0:T(128)S(6)} %copy.15.far_count, f32[408,128]{1,0:T(8,128)S(1)} %collective-permute-done.before, f32[408,128]{1,0:T(8,128)S(1)} %get-tuple-element.14.strip, f32[408,128]{1,0:T(8,128)S(1)} %collective-permute-done.1.after, f32[64,128]{1,0:T(8,128)S(1)} %bitcast.9, ...), custom_call_target="tpu_custom_call" | custom-call | tf_op jit(solution)/shard_map/far/pallas_call | solution.py:550
Async XLA Ops:
  5.1 9.4 %copy-start.1 = (f32[136,128]{1,0:T(8,128)S(1)}, f32[136,128]{1,0:T(8,128)}, u32[]{:S(2)}) copy-start(f32[136,128]{1,0:T(8,128)} %get-tuple-element.12.own) | copy-start | bytes 208900
  5.1 16.9 %all-to-all-start = ((f32[8,96,128]{2,1,0:T(8,128)}), f32[8,96,128]{2,1,0:T(8,128)S(1)}, u32[]{:S(2)}, u32[]{:S(2)}) async-start(f32[8,96,128]{2,1,0:T(8,128)} %get-tuple-element.11), calls=%async_computation | async-start | bytes 786432 | tf_op jit(solution)/shard_map/all_to_all | solution.py:512
  18.4 3.7 %copy-start.3 = (s32[2]{0:T(128)S(1)}, s32[2]{0:T(128)}, u32[]{:S(2)}) copy-start(s32[2]{0:T(128)} %pad_add_fusion.place) | copy-start | bytes 28
  23.2 22.7 %collective-permute-start.1 = (f32[408,128]{1,0:T(8,128)S(1)}, f32[408,128]{1,0:T(8,128)S(1)}, u32[]{:S(2)}, u32[]{:S(2)}) collective-permute-start(f32[408,128]{1,0:T(8,128)S(1)} %get-tuple-element.14.strip), channel_id=1, source_target_pairs={{8,0},{16,8},{24,16},{32,24},{40,32},{48,40},{56,48},{64,56},{72,6... | collective-permute-start | bytes 626696 | tf_op jit(solution)/shard_map/ppermute | solution.py:531
  24.5 21.4 %collective-permute-start = (f32[408,128]{1,0:T(8,128)S(1)}, f32[408,128]{1,0:T(8,128)S(1)}, u32[]{:S(2)}, u32[]{:S(2)}) collective-permute-start(f32[408,128]{1,0:T(8,128)S(1)} %get-tuple-element.14.strip), channel_id=1, source_target_pairs={{0,8},{8,16},{16,24},{24,32},{32,40},{40,48},{48,56},{56,64},{64,7... | collective-permute-start | bytes 626696 | tf_op jit(solution)/shard_map/ppermute | solution.py:530
  29.0 31.0 %all-to-all-start.1 = ((f32[64,1,128]{2,1,0:T(1,128)}), f32[64,1,128]{2,1,0:T(1,128)S(1)}, u32[]{:S(2)}, u32[]{:S(2)}) async-start(f32[64,1,128]{2,1,0:T(1,128)} %bitcast.5), calls=%async_computation.1 | async-start | bytes 65536 | tf_op jit(solution)/shard_map/all_to_all | solution.py:532
  45.9 14.1 %copy-start = (f32[32,4096]{1,0:T(8,128)S(1)}, f32[32,4096]{1,0:T(8,128)}, u32[]{:S(2)}) copy-start(f32[32,4096]{1,0:T(8,128)} %target_basis.1) | copy-start | bytes 1572868
  45.9 14.1 %copy-start.2 = (s32[4096]{0:T(1024)S(1)}, s32[4096]{0:T(1024)}, u32[]{:S(2)}) copy-start(s32[4096]{0:T(1024)} %param.14) | copy-start | bytes 49156
  45.9 14.1 %copy-start.4 = (s32[3,128]{1,0:T(4,128)S(1)}, s32[3,128]{1,0:T(4,128)}, u32[]{:S(2)}) copy-start(s32[3,128]{1,0:T(4,128)} %far_pairs.1) | copy-start | bytes 4612

commit v4 on v3

--- a/solution.py
+++ b/solution.py
@@ -19,6 +19,7 @@
 STRIP_ROWS = SKEL_ROW + GROUP
 SKEL_REC = 24
 MESSAGE_ROWS = 72 + SKEL_REC
+TOP_ROWS = 2
 WINDOW = 3 * STRIP_CLUSTERS
 DUMMY = WINDOW
 DEPTH = 48
@@ -140,8 +141,17 @@
         message[device, 72:, :] = record
 
 
-def strip_kernel(place, received, own, self_rows, strip, top_message):
+def top_kernel(received, self_rows, top_message):
     del self_rows
+    last = received[0, 88:96, :]
+    row = last[0:1] + last[1:2]
+    for device in range(1, NARROW):
+        row = row + received[device, 88:96, :][0:1]
+    top_message[...] = jnp.broadcast_to(row, top_message.shape)
+
+
+def strip_kernel(place, received, own, top_message, strip):
+    del top_message
     narrow_index = place[1]
     down = jnp.maximum(narrow_index - 1, 0)
     up = jnp.minimum(narrow_index + 1, NARROW - 1)
@@ -151,14 +161,9 @@
     strip[PAIR_ROW : PAIR_ROW + 8, :] = received[down, 64:72, :]
     strip[PAIR_ROW + 8 : PAIR_ROW + 16, :] = own[128:136, :]
     strip[PAIR_ROW + 16 : PAIR_ROW + 24, :] = received[up, 64:72, :]
-    last = received[0, 88:96, :]
-    row = last[0:1] + last[1:2]
     for device in range(NARROW):
         start = SKEL_ROW + device * CLUSTERS
         strip[start : start + CLUSTERS, :] = received[device, 72:88, :]
-        if device > 0:
-            row = row + received[device, 88:96, :][0:1]
-    top_message[...] = jnp.broadcast_to(row, top_message.shape)
 
 
 def with_norms(halves, origin):
@@ -404,7 +409,8 @@
     live = iota((1, LANES), 1) < far_count[0]
     index = jnp.where(is_leaf, source - (wide_index - 1) * GROUP, source + 3 * GROUP)
     skel = slice(SKEL_ROW, SKEL_ROW + GROUP)
-    table = jnp.concatenate([before[skel, :], strip[skel, :], after[skel, :], top[...]], axis=0)
+    tops = top[pl.ds(0, top.shape[0] // TOP_ROWS, stride=TOP_ROWS), :]
+    table = jnp.concatenate([before[skel, :], strip[skel, :], after[skel, :], tops], axis=0)
     chosen = as_bf16(iota((table.shape[0], LANES), 0) == index)
     over_rows = ((0,), (0,))
     sources = parts_dot(table, chosen, over_rows)
@@ -519,17 +525,25 @@
             scratch_shapes=[pltpu.VMEM((2, C, LANES), f32)],
             compiler_params=params,
         )(own)
+    with jax.named_scope("top"):
+        top_message = pl.pallas_call(
+            top_kernel,
+            out_shape=shape((TOP_ROWS * wide_size, LANES), f32),
+            in_specs=[vmem()] * 2,
+            out_specs=vmem(),
+            compiler_params=params,
+        )(received, self_rows)
+    tops = lax.all_to_all(top_message, "wide", 0, 0, tiled=True)
     with jax.named_scope("strip"):
-        strip, top_message = pl.pallas_call(
+        strip = pl.pallas_call(
             strip_kernel,
-            out_shape=(shape((STRIP_ROWS, LANES), f32), shape((wide_size, LANES), f32)),
+            out_shape=shape((STRIP_ROWS, LANES), f32),
             in_specs=[smem()] + [vmem()] * 3,
-            out_specs=[vmem()] * 2,
+            out_specs=vmem(),
             compiler_params=params,
-        )(place, received, own, self_rows)
+        )(place, received, own, top_message)
     before = lax.ppermute(strip, "wide", [(i, i + 1) for i in range(wide_size - 1)])
     after = lax.ppermute(strip, "wide", [(i + 1, i) for i in range(wide_size - 1)])
-    tops = lax.all_to_all(top_message, "wide", 0, 0, tiled=True)
     with jax.named_scope("near"):
         near = pl.pallas_call(
             near_kernel,

time: 62.8 us -> 62.9 us (level)
  the two profiles are of different devices: /device:TPU:2 before, /device:TPU:130 now
where the time goes in v4:
time: 62.9 us; the launch traced here: 62.5 us
  starting transfers between devices  28.6 us (45%)
  Pallas kernels  19.7 us (31%)
  waiting for transfers between devices  12.1 us (19%)
  between operations  1.41 us (2%)
    all_to_all x1, starting transfers between devices, local(): tops = lax.all_to_all(top_message, 'wide', 0, 0, tiled=True)  17.2 us
    pallas_call x1, Pallas kernels, local(): pl.pallas_call(near_kernel, out_shape=shape((ROWS, LANES), f32), in_specs...  7.98 us
    ppermute x1, waiting for transfers between devices, local(): lax.ppermute(strip, 'wide', [(i, i + 1) for i in range(wide_size - 1)])  6.87 us
    all_to_all x1, starting transfers between devices, local(): received = lax.all_to_all(message, 'narrow', 0, 0, tiled=True)  4.97 us
    ppermute x1, starting transfers between devices, local(): lax.ppermute(strip, 'wide', [(i + 1, i) for i in range(wide_size - 1)])  4.58 us
    pallas_call x1, Pallas kernels, local(): pl.pallas_call(self_kernel, out_shape=(shape((CLUSTERS, C, DEPTH), bf16),...  3.85 us
    pallas_call x1, Pallas kernels, local(): pl.pallas_call(slots_kernel, out_shape=(shape((136, LANES), f32), shape((...  3.81 us
    all_to_all x1, waiting for transfers between devices, local(): received = lax.all_to_all(message, 'narrow', 0, 0, tiled=True)  3.62 us
  transfers between devices with their start and end apart: 4, of which 3 were waited for; matrix products, arithmetic and copies ran while one was open for 0% of the time, Pallas kernels for 20%

profile of v4, /device:TPU:130, one launch (start us, length us, event | category | flops | bytes accessed | tf_op | source)
XLA Modules:
  0.0 62.5 jit_solution(13531848707029974338)
XLA Ops:
  0.7 0.6 pad_add_fusion.place
  1.3 3.8 %slots.1 = (f32[136,128]{1,0:T(8,128)}, f32[8,96,128]{2,1,0:T(8,128)}) custom-call(s32[1]{0:T(128)S(6)} %copy.13.near_count, s32[2]{0:T(128)} %pad_add_fusion.place, s32[32,128]{1,0:T(8,128)} %bitcast.8, f32[3,4096]{1,0:T(4,128)} %refs_1_.1, f32[32,128]{1,0:T(8,128)} %bitcast.10, s32[2,64]{1,0:T(2,128)} %refs_3_.1, f32[32,4096]{1,0:T(8,128)} %refs_4_.1, ...), custom_call_target="tpu_custom_call" | custom-call | tf_op jit(solution)/shard_map/slots/pallas_call | solution.py:506
  5.1 0.0 copy-start.1
  5.1 5.0 %all-to-all-start = ((f32[8,96,128]{2,1,0:T(8,128)}), f32[8,96,128]{2,1,0:T(8,128)S(1)}, u32[]{:S(2)}, u32[]{:S(2)}) async-start(f32[8,96,128]{2,1,0:T(8,128)} %get-tuple-element.9), calls=%async_computation | async-start | bytes 786432 | tf_op jit(solution)/shard_map/all_to_all | solution.py:518
  10.1 0.0 copy-done.1
  10.1 3.9 %self.1 = (bf16[16,256,48]{2,1,0:T(8,128)(2,1)S(1)}, f32[32,128]{1,0:T(8,128)S(1)}) custom-call(f32[136,128]{1,0:T(8,128)S(1)} %copy-done.1), custom_call_target="tpu_custom_call" | custom-call | tf_op jit(solution)/shard_map/self/pallas_call | solution.py:520
  13.9 3.6 %all-to-all-done.received = f32[8,96,128]{2,1,0:T(8,128)S(1)} async-done(((f32[8,96,128]{2,1,0:T(8,128)}), f32[8,96,128]{2,1,0:T(8,128)S(1)}, u32[]{:S(2)}, u32[]{:S(2)}) %all-to-all-start) | async-done | bytes 393248 | tf_op jit(solution)/shard_map/all_to_all | solution.py:518
  17.6 0.6 %top.1.top_message = f32[128,128]{1,0:T(8,128)} custom-call(f32[8,96,128]{2,1,0:T(8,128)S(1)} %all-to-all-done.received, f32[32,128]{1,0:T(8,128)S(1)} %get-tuple-element.11.self_rows), custom_call_target="tpu_custom_call" | custom-call | tf_op jit(solution)/shard_map/top/pallas_call | solution.py:529
  18.2 0.0 copy-start.3
  18.2 17.2 %all-to-all-start.1 = ((f32[64,2,128]{2,1,0:T(2,128)}), f32[64,2,128]{2,1,0:T(2,128)S(1)}, u32[]{:S(2)}, u32[]{:S(2)}) async-start(f32[64,2,128]{2,1,0:T(2,128)} %bitcast.4), calls=%async_computation.1 | async-start | bytes 131072 | tf_op jit(solution)/shard_map/all_to_all | solution.py:536
  35.4 0.0 copy-done.3
  35.4 0.9 %strip.1 = f32[408,128]{1,0:T(8,128)S(1)} custom-call(s32[2]{0:T(128)S(1)} %copy-done.3, f32[8,96,128]{2,1,0:T(8,128)S(1)} %all-to-all-done.received, f32[136,128]{1,0:T(8,128)S(1)} %copy-done.1, f32[128,128]{1,0:T(8,128)} %top.1.top_message), custom_call_target="tpu_custom_call" | custom-call | tf_op jit(solution)/shard_map/strip/pallas_call | solution.py:538
  36.3 4.6 %collective-permute-start.1 = (f32[408,128]{1,0:T(8,128)S(1)}, f32[408,128]{1,0:T(8,128)S(1)}, u32[]{:S(2)}, u32[]{:S(2)}) collective-permute-start(f32[408,128]{1,0:T(8,128)S(1)} %strip.1), channel_id=1, source_target_pairs={{8,0},{16,8},{24,16},{32,24},{40,32},{48,40},{56,48},{64,56},{72,6... | collective-permute-start | bytes 626696 | tf_op jit(solution)/shard_map/ppermute | solution.py:546
  40.9 1.9 %collective-permute-start = (f32[408,128]{1,0:T(8,128)S(1)}, f32[408,128]{1,0:T(8,128)S(1)}, u32[]{:S(2)}, u32[]{:S(2)}) collective-permute-start(f32[408,128]{1,0:T(8,128)S(1)} %strip.1), channel_id=1, source_target_pairs={{0,8},{8,16},{16,24},{24,32},{32,40},{40,48},{48,56},{56,64},{64,7... | collective-permute-start | bytes 626696 | tf_op jit(solution)/shard_map/ppermute | solution.py:545
  43.5 1.6 %collective-permute-done.1.after = f32[408,128]{1,0:T(8,128)S(1)} collective-permute-done((f32[408,128]{1,0:T(8,128)S(1)}, f32[408,128]{1,0:T(8,128)S(1)}, u32[]{:S(2)}, u32[]{:S(2)}) %collective-permute-start.1) | collective-permute-done | bytes 208928 | tf_op jit(solution)/shard_map/ppermute | solution.py:546
  45.1 6.9 %collective-permute-done.before = f32[408,128]{1,0:T(8,128)S(1)} collective-permute-done((f32[408,128]{1,0:T(8,128)S(1)}, f32[408,128]{1,0:T(8,128)S(1)}, u32[]{:S(2)}, u32[]{:S(2)}) %collective-permute-start) | collective-permute-done | bytes 208928 | tf_op jit(solution)/shard_map/ppermute | solution.py:545
  52.0 0.0 copy-start
  52.0 0.0 copy-start.2
  52.0 8.0 %near.1 = f32[32,128]{1,0:T(8,128)S(1)} custom-call(s32[2]{0:T(128)S(1)} %copy-done.3, f32[408,128]{1,0:T(8,128)S(1)} %collective-permute-done.before, f32[408,128]{1,0:T(8,128)S(1)} %strip.1, f32[408,128]{1,0:T(8,128)S(1)} %collective-permute-done.1.after, bf16[16,256,48]{2,1,0:T(8,128)(2,1)S(1)} %get-tuple-element.12.lhs, ...), custom_call_target="tpu_custom_call" | custom-call | tf_op jit(solution)/shard_map/near/pallas_call | solution.py:548
  60.0 0.0 all-to-all-done.1
  60.0 0.0 copy-done
  60.0 0.0 copy-done.2
  60.0 0.0 copy-done.4
  60.0 2.5 %far.1 = f32[32,128]{1,0:T(8,128)} custom-call(s32[2]{0:T(128)S(1)} %copy-done.3, s32[1]{0:T(128)S(6)} %copy.14.far_count, f32[408,128]{1,0:T(8,128)S(1)} %collective-permute-done.before, f32[408,128]{1,0:T(8,128)S(1)} %strip.1, f32[408,128]{1,0:T(8,128)S(1)} %collective-permute-done.1.after, f32[128,128]{1,0:T(8,128)S(1)} %bitcast.7, ...), custom_call_target="tpu_custom_call" | custom-call | tf_op jit(solution)/shard_map/far/pallas_call | solution.py:564
  (1 shorter events, 0.0 us)
Async XLA Ops:
  5.1 5.0 %copy-start.1 = (f32[136,128]{1,0:T(8,128)S(1)}, f32[136,128]{1,0:T(8,128)}, u32[]{:S(2)}) copy-start(f32[136,128]{1,0:T(8,128)} %get-tuple-element.10.own) | copy-start | bytes 208900
  5.1 12.5 %all-to-all-start = ((f32[8,96,128]{2,1,0:T(8,128)}), f32[8,96,128]{2,1,0:T(8,128)S(1)}, u32[]{:S(2)}, u32[]{:S(2)}) async-start(f32[8,96,128]{2,1,0:T(8,128)} %get-tuple-element.9), calls=%async_computation | async-start | bytes 786432 | tf_op jit(solution)/shard_map/all_to_all | solution.py:518
  18.2 17.2 %copy-start.3 = (s32[2]{0:T(128)S(1)}, s32[2]{0:T(128)}, u32[]{:S(2)}) copy-start(s32[2]{0:T(128)} %pad_add_fusion.place) | copy-start | bytes 28
  18.2 41.8 %all-to-all-start.1 = ((f32[64,2,128]{2,1,0:T(2,128)}), f32[64,2,128]{2,1,0:T(2,128)S(1)}, u32[]{:S(2)}, u32[]{:S(2)}) async-start(f32[64,2,128]{2,1,0:T(2,128)} %bitcast.4), calls=%async_computation.1 | async-start | bytes 131072 | tf_op jit(solution)/shard_map/all_to_all | solution.py:536
  36.3 8.8 %collective-permute-start.1 = (f32[408,128]{1,0:T(8,128)S(1)}, f32[408,128]{1,0:T(8,128)S(1)}, u32[]{:S(2)}, u32[]{:S(2)}) collective-permute-start(f32[408,128]{1,0:T(8,128)S(1)} %strip.1), channel_id=1, source_target_pairs={{8,0},{16,8},{24,16},{32,24},{40,32},{48,40},{56,48},{64,56},{72,6... | collective-permute-start | bytes 626696 | tf_op jit(solution)/shard_map/ppermute | solution.py:546
  40.9 11.1 %collective-permute-start = (f32[408,128]{1,0:T(8,128)S(1)}, f32[408,128]{1,0:T(8,128)S(1)}, u32[]{:S(2)}, u32[]{:S(2)}) collective-permute-start(f32[408,128]{1,0:T(8,128)S(1)} %strip.1), channel_id=1, source_target_pairs={{0,8},{8,16},{16,24},{24,32},{32,40},{40,48},{48,56},{56,64},{64,7... | collective-permute-start | bytes 626696 | tf_op jit(solution)/shard_map/ppermute | solution.py:545
  52.0 8.0 %copy-start = (f32[32,4096]{1,0:T(8,128)S(1)}, f32[32,4096]{1,0:T(8,128)}, u32[]{:S(2)}) copy-start(f32[32,4096]{1,0:T(8,128)} %target_basis.1) | copy-start | bytes 1572868
  52.0 8.0 %copy-start.2 = (s32[4096]{0:T(1024)S(1)}, s32[4096]{0:T(1024)}, u32[]{:S(2)}) copy-start(s32[4096]{0:T(1024)} %param.14) | copy-start | bytes 49156
  52.0 8.0 %copy-start.4 = (s32[3,128]{1,0:T(4,128)S(1)}, s32[3,128]{1,0:T(4,128)}, u32[]{:S(2)}) copy-start(s32[3,128]{1,0:T(4,128)} %far_pairs.1) | copy-start | bytes 4612

commit v5 on v4

--- a/solution.py
+++ b/solution.py
@@ -18,13 +18,12 @@
 SKEL_ROW = PAIR_ROW + 24
 STRIP_ROWS = SKEL_ROW + GROUP
 SKEL_REC = 24
-MESSAGE_ROWS = 72 + SKEL_REC
 TOP_ROWS = 2
 WINDOW = 3 * STRIP_CLUSTERS
 DUMMY = WINDOW
 DEPTH = 48
 UNROLL = 8
-SUMS = 4
+SUMS = 2
 CHUNK = 64
 
 soft_square = 0.01
@@ -58,18 +57,17 @@
     return mask.astype(f32).astype(bf16)
 
 
-def slots_kernel(near_count, place, *refs):
+def slots_kernel(near_count, *refs):
     count = 8
+    own, skel_out = refs[count : count + 2]
     held = refs[count + 2 : 2 * count + 2]
     semaphores = refs[2 * count + 2]
-    own, message = refs[count : count + 2]
     copies = [
         pltpu.make_async_copy(refs[i], held[i], semaphores.at[i]) for i in range(count)
     ]
     for copy in copies:
         copy.start()
     order, points, charges, near_pairs, source_basis, transfer, skeleton_points, top_points = held
-    narrow_index = place[1]
     for copy in copies[:4]:
         copy.wait()
     low = order[...] & (LANES - 1)
@@ -131,39 +129,29 @@
     top_row = jnp.sum(jnp.where(top_mine, top, 0.0), axis=0, keepdims=True)
     last = jnp.where(iota((8, LANES), 0) == 1, top_row, 0.0)
     record = record + jnp.concatenate([geometry, last], axis=0)
-    pair_block = own[128:136, :]
     for device in range(NARROW):
-        for tile in range(8):
-            message[device, 8 * tile : 8 * tile + 8, :] = jnp.where(
-                narrow_index < device, tiles[8 + tile], tiles[tile]
-            )
-        message[device, 64:72, :] = jnp.where(narrow_index == device, 0.0, pair_block)
-        message[device, 72:, :] = record
-
-
-def top_kernel(received, self_rows, top_message):
-    del self_rows
-    last = received[0, 88:96, :]
+        skel_out[device] = record
+
+
+def top_kernel(skels, top_message):
+    last = skels[0, CLUSTERS:SKEL_REC, :]
     row = last[0:1] + last[1:2]
     for device in range(1, NARROW):
-        row = row + received[device, 88:96, :][0:1]
+        row = row + skels[device, CLUSTERS:SKEL_REC, :][0:1]
     top_message[...] = jnp.broadcast_to(row, top_message.shape)
 
 
-def strip_kernel(place, received, own, top_message, strip):
+def strip_kernel(skels, from_down, own, from_up, top_message, strip):
     del top_message
-    narrow_index = place[1]
-    down = jnp.maximum(narrow_index - 1, 0)
-    up = jnp.minimum(narrow_index + 1, NARROW - 1)
-    strip[0:64, :] = received[down, 0:64, :]
+    strip[0:64, :] = from_down[64:128, :]
     strip[64:192, :] = own[0:128, :]
-    strip[192:256, :] = received[up, 0:64, :]
-    strip[PAIR_ROW : PAIR_ROW + 8, :] = received[down, 64:72, :]
+    strip[192:256, :] = from_up[0:64, :]
+    strip[PAIR_ROW : PAIR_ROW + 8, :] = from_down[128:136, :]
     strip[PAIR_ROW + 8 : PAIR_ROW + 16, :] = own[128:136, :]
-    strip[PAIR_ROW + 16 : PAIR_ROW + 24, :] = received[up, 64:72, :]
+    strip[PAIR_ROW + 16 : PAIR_ROW + 24, :] = from_up[128:136, :]
     for device in range(NARROW):
         start = SKEL_ROW + device * CLUSTERS
-        strip[start : start + CLUSTERS, :] = received[device, 72:88, :]
+        strip[start : start + CLUSTERS, :] = skels[device, :CLUSTERS, :]
 
 
 def with_norms(halves, origin):
@@ -223,12 +211,12 @@
         store(start, inverse[:, :LANES] * charge_low + inverse[:, LANES:] * charge_high)
 
 
-def self_kernel(own, lhs, near, held):
-    origin = own_origin(own, 0)
+def self_kernel(strip, lhs, near, held):
+    origin = own_origin(strip, 64)
 
     def block_step(block, carry):
         for odd in range(2):
-            halves = cluster_halves(own, block, odd)
+            halves = cluster_halves(strip, block + 4, odd)
             lhs[2 * block + odd] = target_features(halves, origin)
             centre = jnp.sum(halves[0] + halves[1], axis=1, keepdims=True) * (1.0 / C)
             left = target_features(halves, centre)
@@ -352,9 +340,9 @@
     copy.wait()
     pair_total = entries[7, 0]
 
-    def pair_step(step, carry):
-        for turn in range(UNROLL):
-            index = step * UNROLL + turn
+    def pair_steps(first, turns, carry):
+        for turn in range(turns):
+            index = first + turn
             code = entries[index >> 7, index & (LANES - 1)]
             live = index < pair_total
             cluster = jnp.where(live, code >> 7, 0)
@@ -372,7 +360,13 @@
             )
         return carry
 
-    lax.fori_loop(0, (pair_total + UNROLL - 1) // UNROLL, pair_step, 0)
+    steps = (pair_total + UNROLL - 1) // UNROLL
+    lax.fori_loop(
+        0, steps // 2, lambda step, carry: pair_steps(2 * UNROLL * step, 2 * UNROLL, carry), 0
+    )
+    lax.fori_loop(
+        2 * (steps // 2), steps, lambda step, carry: pair_steps(UNROLL * step, UNROLL, carry), 0
+    )
 
     for cluster in range(CLUSTERS):
         for half in range(2):
@@ -489,6 +483,7 @@
     far_count,
 ):
     wide_size = lax.axis_size("wide")
+    narrow_size = lax.axis_size("narrow")
     place = jnp.stack([lax.axis_index("wide"), lax.axis_index("narrow")]).astype(i32)
     order = order.reshape(ROWS, LANES)
     shape = jax.ShapeDtypeStruct
@@ -503,19 +498,40 @@
         top_points,
     )
     with jax.named_scope("slots"):
-        own, message = pl.pallas_call(
+        own, skel = pl.pallas_call(
             slots_kernel,
             out_shape=(
                 shape((136, LANES), f32),
-                shape((NARROW, MESSAGE_ROWS, LANES), f32),
+                shape((NARROW, SKEL_REC, LANES), f32),
             ),
-            in_specs=[smem(), smem()] + [in_hbm()] * len(inputs),
+            in_specs=[smem()] + [in_hbm()] * len(inputs),
             out_specs=[vmem()] * 2,
             scratch_shapes=[pltpu.VMEM(x.shape, x.dtype) for x in inputs]
             + [pltpu.SemaphoreType.DMA((len(inputs),))],
             compiler_params=first_params,
-        )(near_count, place, *inputs)
-    received = lax.all_to_all(message, "narrow", 0, 0, tiled=True)
+        )(near_count, *inputs)
+    skels = lax.all_to_all(skel, "narrow", 0, 0, tiled=True)
+    from_down = lax.ppermute(own, "narrow", [(i, i + 1) for i in range(narrow_size - 1)])
+    from_up = lax.ppermute(own, "narrow", [(i + 1, i) for i in range(narrow_size - 1)])
+    with jax.named_scope("top"):
+        top_message = pl.pallas_call(
+            top_kernel,
+            out_shape=shape((TOP_ROWS * wide_size, LANES), f32),
+            in_specs=[vmem()],
+            out_specs=vmem(),
+            compiler_params=params,
+        )(skels)
+    tops = lax.all_to_all(top_message, "wide", 0, 0, tiled=True)
+    with jax.named_scope("strip"):
+        strip = pl.pallas_call(
+            strip_kernel,
+            out_shape=shape((STRIP_ROWS, LANES), f32),
+            in_specs=[vmem()] * 5,
+            out_specs=vmem(),
+            compiler_params=params,
+        )(skels, from_down, own, from_up, top_message)
+    before = lax.ppermute(strip, "wide", [(i, i + 1) for i in range(wide_size - 1)])
+    after = lax.ppermute(strip, "wide", [(i + 1, i) for i in range(wide_size - 1)])
     with jax.named_scope("self"):
         lhs, self_rows = pl.pallas_call(
             self_kernel,
@@ -524,26 +540,7 @@
             out_specs=[vmem()] * 2,
             scratch_shapes=[pltpu.VMEM((2, C, LANES), f32)],
             compiler_params=params,
-        )(own)
-    with jax.named_scope("top"):
-        top_message = pl.pallas_call(
-            top_kernel,
-            out_shape=shape((TOP_ROWS * wide_size, LANES), f32),
-            in_specs=[vmem()] * 2,
-            out_specs=vmem(),
-            compiler_params=params,
-        )(received, self_rows)
-    tops = lax.all_to_all(top_message, "wide", 0, 0, tiled=True)
-    with jax.named_scope("strip"):
-        strip = pl.pallas_call(
-            strip_kernel,
-            out_shape=shape((STRIP_ROWS, LANES), f32),
-            in_specs=[smem()] + [vmem()] * 3,
-            out_specs=vmem(),
-            compiler_params=params,
-        )(place, received, own, top_message)
-    before = lax.ppermute(strip, "wide", [(i, i + 1) for i in range(wide_size - 1)])
-    after = lax.ppermute(strip, "wide", [(i + 1, i) for i in range(wide_size - 1)])
+        )(strip)
     with jax.named_scope("near"):
         near = pl.pallas_call(
             near_kernel,

time: 62.9 us -> 58.4 us (0.928)
  the two profiles are of different devices: /device:TPU:130 before, /device:TPU:120 now
where the time goes in v5:
time: 58.4 us; the launch traced here: 58 us
  starting transfers between devices  31.8 us (54%)
  Pallas kernels  17.5 us (30%)
  waiting for transfers between devices  7.2 us (12%)
  between operations  1.44 us (2%)
    all_to_all x1, starting transfers between devices, local(): tops = lax.all_to_all(top_message, 'wide', 0, 0, tiled=True)  17.1 us
    pallas_call x1, Pallas kernels, local(): pl.pallas_call(near_kernel, out_shape=shape((ROWS, LANES), f32), in_specs...  6.56 us
    ppermute x1, waiting for transfers between devices, local(): lax.ppermute(strip, 'wide', [(i + 1, i) for i in range(wide_size - 1)])  5.1 us
    ppermute x1, starting transfers between devices, local(): lax.ppermute(strip, 'wide', [(i, i + 1) for i in range(wide_size - 1)])  4.58 us
    all_to_all x1, starting transfers between devices, local(): skels = lax.all_to_all(skel, 'narrow', 0, 0, tiled=True)  4.44 us
    pallas_call x1, Pallas kernels, local(): pl.pallas_call(self_kernel, out_shape=(shape((CLUSTERS, C, DEPTH), bf16),...  3.85 us
    pallas_call x1, Pallas kernels, local(): pl.pallas_call(slots_kernel, out_shape=(shape((136, LANES), f32), shape((...  3.03 us
    pallas_call x1, Pallas kernels, local(): pl.pallas_call(far_kernel, out_shape=shape((ROWS, LANES), f32), in_specs=...  2.49 us
  transfers between devices with their start and end apart: 6, of which 2 were waited for; matrix products, arithmetic and copies ran while one was open for 0% of the time, Pallas kernels for 21%

profile of v5, /device:TPU:120, one launch (start us, length us, event | category | flops | bytes accessed | tf_op | source)
XLA Modules:
  0.0 58.0 jit_solution(5379675478883945528)
XLA Ops:
  0.7 3.0 %slots.1 = (f32[136,128]{1,0:T(8,128)}, f32[8,24,128]{2,1,0:T(8,128)}) custom-call(s32[1]{0:T(128)S(6)} %copy.13.near_count, s32[32,128]{1,0:T(8,128)} %bitcast.8, f32[3,4096]{1,0:T(4,128)} %refs_1_.1, f32[32,128]{1,0:T(8,128)} %bitcast.10, s32[2,64]{1,0:T(2,128)} %refs_3_.1, f32[32,4096]{1,0:T(8,128)} %refs_4_.1, f32[32,512]{1,0:T(8,128)} %refs_5_.1, ...), custom_call_target="tpu_custom_call" | custom-call | tf_op jit(solution)/shard_map/slots/pallas_call | solution.py:501
  3.7 0.0 copy-start.1
  3.7 4.4 %all-to-all-start = ((f32[8,24,128]{2,1,0:T(8,128)}), f32[8,24,128]{2,1,0:T(8,128)S(1)}, u32[]{:S(2)}, u32[]{:S(2)}) async-start(f32[8,24,128]{2,1,0:T(8,128)} %get-tuple-element.9), calls=%async_computation | async-start | bytes 196608 | tf_op jit(solution)/shard_map/all_to_all | solution.py:513
  8.1 0.0 copy-done.1
  8.2 2.4 %collective-permute-start = (f32[136,128]{1,0:T(8,128)S(1)}, f32[136,128]{1,0:T(8,128)S(1)}, u32[]{:S(2)}, u32[]{:S(2)}) collective-permute-start(f32[136,128]{1,0:T(8,128)S(1)} %copy-done.1), channel_id=1, source_target_pairs={{0,1},{1,2},{2,3},{3,4},{4,5},{5,6},{6,7},{8,9},{9,10},{10,11},{11... | collective-permute-start | bytes 208904 | tf_op jit(solution)/shard_map/ppermute | solution.py:514
  10.6 1.3 %collective-permute-start.1 = (f32[136,128]{1,0:T(8,128)S(1)}, f32[136,128]{1,0:T(8,128)S(1)}, u32[]{:S(2)}, u32[]{:S(2)}) collective-permute-start(f32[136,128]{1,0:T(8,128)S(1)} %copy-done.1), channel_id=1, source_target_pairs={{1,0},{2,1},{3,2},{4,3},{5,4},{6,5},{7,6},{9,8},{10,9},{11,10},{12... | collective-permute-start | bytes 208904 | tf_op jit(solution)/shard_map/ppermute | solution.py:515
  11.9 2.1 %all-to-all-done.skels = f32[8,24,128]{2,1,0:T(8,128)S(1)} async-done(((f32[8,24,128]{2,1,0:T(8,128)}), f32[8,24,128]{2,1,0:T(8,128)S(1)}, u32[]{:S(2)}, u32[]{:S(2)}) %all-to-all-start) | async-done | bytes 98336 | tf_op jit(solution)/shard_map/all_to_all | solution.py:513
  13.9 0.6 %top.1.top_message = f32[128,128]{1,0:T(8,128)} custom-call(f32[8,24,128]{2,1,0:T(8,128)S(1)} %all-to-all-done.skels), custom_call_target="tpu_custom_call" | custom-call | tf_op jit(solution)/shard_map/top/pallas_call | solution.py:517
  14.6 17.1 %all-to-all-start.1 = ((f32[64,2,128]{2,1,0:T(2,128)}), f32[64,2,128]{2,1,0:T(2,128)S(1)}, u32[]{:S(2)}, u32[]{:S(2)}) async-start(f32[64,2,128]{2,1,0:T(2,128)} %bitcast.4), calls=%async_computation.1 | async-start | bytes 131072 | tf_op jit(solution)/shard_map/all_to_all | solution.py:524
  31.7 0.0 collective-permute-done.from_down
  31.7 0.0 collective-permute-done.1.from_up
  31.8 0.9 %strip.1 = f32[408,128]{1,0:T(8,128)S(1)} custom-call(f32[8,24,128]{2,1,0:T(8,128)S(1)} %all-to-all-done.skels, f32[136,128]{1,0:T(8,128)S(1)} %collective-permute-done.from_down, f32[136,128]{1,0:T(8,128)S(1)} %copy-done.1, f32[136,128]{1,0:T(8,128)S(1)} %collective-permute-done.1.from_up, f32[128,128]{1,0:T(8,128)} %top.1.top_message), custom_call_target="tpu_custom_call" | custom-call | tf_op jit(solution)/shard_map/strip/pallas_call | solution.py:526
  32.6 4.6 %collective-permute-start.2 = (f32[408,128]{1,0:T(8,128)S(1)}, f32[408,128]{1,0:T(8,128)S(1)}, u32[]{:S(2)}, u32[]{:S(2)}) collective-permute-start(f32[408,128]{1,0:T(8,128)S(1)} %strip.1), channel_id=1, source_target_pairs={{0,8},{8,16},{16,24},{24,32},{32,40},{40,48},{48,56},{56,64},{64,7... | collective-permute-start | bytes 626696 | tf_op jit(solution)/shard_map/ppermute | solution.py:533
  37.2 1.9 %collective-permute-start.3 = (f32[408,128]{1,0:T(8,128)S(1)}, f32[408,128]{1,0:T(8,128)S(1)}, u32[]{:S(2)}, u32[]{:S(2)}) collective-permute-start(f32[408,128]{1,0:T(8,128)S(1)} %strip.1), channel_id=1, source_target_pairs={{8,0},{16,8},{24,16},{32,24},{40,32},{48,40},{56,48},{64,56},{72,6... | collective-permute-start | bytes 626696 | tf_op jit(solution)/shard_map/ppermute | solution.py:534
  39.8 0.1 pad_add_fusion.place
  39.9 3.9 %self.1 = (bf16[16,256,48]{2,1,0:T(8,128)(2,1)S(1)}, f32[32,128]{1,0:T(8,128)S(1)}) custom-call(f32[408,128]{1,0:T(8,128)S(1)} %strip.1), custom_call_target="tpu_custom_call" | custom-call | tf_op jit(solution)/shard_map/self/pallas_call | solution.py:536
  43.8 0.0 collective-permute-done.2.before
  43.8 5.1 %collective-permute-done.3.after = f32[408,128]{1,0:T(8,128)S(1)} collective-permute-done((f32[408,128]{1,0:T(8,128)S(1)}, f32[408,128]{1,0:T(8,128)S(1)}, u32[]{:S(2)}, u32[]{:S(2)}) %collective-permute-start.3) | collective-permute-done | bytes 208928 | tf_op jit(solution)/shard_map/ppermute | solution.py:534
  48.9 6.6 %near.1 = f32[32,128]{1,0:T(8,128)S(1)} custom-call(s32[2]{0:T(128)S(1)} %pad_add_fusion.place, f32[408,128]{1,0:T(8,128)S(1)} %collective-permute-done.2.before, f32[408,128]{1,0:T(8,128)S(1)} %strip.1, f32[408,128]{1,0:T(8,128)S(1)} %collective-permute-done.3.after, bf16[16,256,48]{2,1,0:T(8,128)(2,1)S(1)} %get-tuple-element.11.lhs, ...), custom_call_target="tpu_custom_call" | custom-call | tf_op jit(solution)/shard_map/near/pallas_call | solution.py:545
  55.4 0.0 all-to-all-done.1
  55.5 0.0 copy-done
  55.5 0.0 copy-done.2
  55.5 0.0 copy-done.3
  55.5 2.5 %far.1 = f32[32,128]{1,0:T(8,128)} custom-call(s32[2]{0:T(128)S(1)} %pad_add_fusion.place, s32[1]{0:T(128)S(6)} %copy.14.far_count, f32[408,128]{1,0:T(8,128)S(1)} %collective-permute-done.2.before, f32[408,128]{1,0:T(8,128)S(1)} %strip.1, f32[408,128]{1,0:T(8,128)S(1)} %collective-permute-done.3.after, f32[128,128]{1,0:T(8,128)S(1)} %bitcast.7, ...), custom_call_target="tpu_custom_call" | custom-call | tf_op jit(solution)/shard_map/far/pallas_call | solution.py:561
  (3 shorter events, 0.0 us)
Async XLA Ops:
  3.7 4.5 %copy-start.1 = (f32[136,128]{1,0:T(8,128)S(1)}, f32[136,128]{1,0:T(8,128)}, u32[]{:S(2)}) copy-start(f32[136,128]{1,0:T(8,128)} %get-tuple-element.10.own) | copy-start | bytes 208900
  3.7 10.2 %all-to-all-start = ((f32[8,24,128]{2,1,0:T(8,128)}), f32[8,24,128]{2,1,0:T(8,128)S(1)}, u32[]{:S(2)}, u32[]{:S(2)}) async-start(f32[8,24,128]{2,1,0:T(8,128)} %get-tuple-element.9), calls=%async_computation | async-start | bytes 196608 | tf_op jit(solution)/shard_map/all_to_all | solution.py:513
  8.2 23.6 %collective-permute-start = (f32[136,128]{1,0:T(8,128)S(1)}, f32[136,128]{1,0:T(8,128)S(1)}, u32[]{:S(2)}, u32[]{:S(2)}) collective-permute-start(f32[136,128]{1,0:T(8,128)S(1)} %copy-done.1), channel_id=1, source_target_pairs={{0,1},{1,2},{2,3},{3,4},{4,5},{5,6},{6,7},{8,9},{9,10},{10,11},{11... | collective-permute-start | bytes 208904 | tf_op jit(solution)/shard_map/ppermute | solution.py:514
  10.6 21.2 %collective-permute-start.1 = (f32[136,128]{1,0:T(8,128)S(1)}, f32[136,128]{1,0:T(8,128)S(1)}, u32[]{:S(2)}, u32[]{:S(2)}) collective-permute-start(f32[136,128]{1,0:T(8,128)S(1)} %copy-done.1), channel_id=1, source_target_pairs={{1,0},{2,1},{3,2},{4,3},{5,4},{6,5},{7,6},{9,8},{10,9},{11,10},{12... | collective-permute-start | bytes 208904 | tf_op jit(solution)/shard_map/ppermute | solution.py:515
  14.6 40.9 %all-to-all-start.1 = ((f32[64,2,128]{2,1,0:T(2,128)}), f32[64,2,128]{2,1,0:T(2,128)S(1)}, u32[]{:S(2)}, u32[]{:S(2)}) async-start(f32[64,2,128]{2,1,0:T(2,128)} %bitcast.4), calls=%async_computation.1 | async-start | bytes 131072 | tf_op jit(solution)/shard_map/all_to_all | solution.py:524
  32.6 11.1 %collective-permute-start.2 = (f32[408,128]{1,0:T(8,128)S(1)}, f32[408,128]{1,0:T(8,128)S(1)}, u32[]{:S(2)}, u32[]{:S(2)}) collective-permute-start(f32[408,128]{1,0:T(8,128)S(1)} %strip.1), channel_id=1, source_target_pairs={{0,8},{8,16},{16,24},{24,32},{32,40},{40,48},{48,56},{56,64},{64,7... | collective-permute-start | bytes 626696 | tf_op jit(solution)/shard_map/ppermute | solution.py:533
  37.2 11.6 %collective-permute-start.3 = (f32[408,128]{1,0:T(8,128)S(1)}, f32[408,128]{1,0:T(8,128)S(1)}, u32[]{:S(2)}, u32[]{:S(2)}) collective-permute-start(f32[408,128]{1,0:T(8,128)S(1)} %strip.1), channel_id=1, source_target_pairs={{8,0},{16,8},{24,16},{32,24},{40,32},{48,40},{56,48},{64,56},{72,6... | collective-permute-start | bytes 626696 | tf_op jit(solution)/shard_map/ppermute | solution.py:534
  48.9 6.6 %copy-start = (f32[32,4096]{1,0:T(8,128)S(1)}, f32[32,4096]{1,0:T(8,128)}, u32[]{:S(2)}) copy-start(f32[32,4096]{1,0:T(8,128)} %target_basis.1) | copy-start | bytes 1572868
  48.9 6.6 %copy-start.2 = (s32[4096]{0:T(1024)S(1)}, s32[4096]{0:T(1024)}, u32[]{:S(2)}) copy-start(s32[4096]{0:T(1024)} %param.14) | copy-start | bytes 49156
  48.9 6.6 %copy-start.3 = (s32[3,128]{1,0:T(4,128)S(1)}, s32[3,128]{1,0:T(4,128)}, u32[]{:S(2)}) copy-start(s32[3,128]{1,0:T(4,128)} %far_pairs.1) | copy-start | bytes 4612

commit v6 on v5

--- a/solution.py
+++ b/solution.py
@@ -19,8 +19,8 @@
 STRIP_ROWS = SKEL_ROW + GROUP
 SKEL_REC = 24
 TOP_ROWS = 2
-WINDOW = 3 * STRIP_CLUSTERS
-DUMMY = WINDOW
+OUTER = 2 * STRIP_CLUSTERS
+SELF = STRIP_CLUSTERS + 1
 DEPTH = 48
 UNROLL = 8
 SUMS = 2
@@ -182,9 +182,8 @@
         rows = jnp.where(sub < 3, -2.0 * shifted, jnp.where(sub == 5, norms + soft_square, 0.0))
         rows = jnp.where(sub == 4, 1.0, rows)
         high, mid, low = [part.astype(f32) for part in split3(rows)]
-        stacked = jnp.concatenate([high, high, mid, mid, high, low], axis=0)
-        columns.append(stacked.T.astype(bf16))
-    return jnp.concatenate(columns, axis=0)
+        columns.append(jnp.concatenate([high, high, mid, mid, high, low], axis=0))
+    return columns
 
 
 def cluster_halves(ref, block, odd):
@@ -204,88 +203,37 @@
     return jnp.where(iota((8, LANES), 0) < 3, mean + pltpu.roll(mean, 4, 0), 0.0)
 
 
-def weighted(left, right, charge_low, charge_high, store):
-    for start in range(0, C, CHUNK):
-        square = jnp.dot(left(start), right, preferred_element_type=f32)
-        inverse = lax.rsqrt(jnp.maximum(square, soft_square))
-        store(start, inverse[:, :LANES] * charge_low + inverse[:, LANES:] * charge_high)
-
-
-def self_kernel(strip, lhs, near, held):
-    origin = own_origin(strip, 64)
-
-    def block_step(block, carry):
-        for odd in range(2):
-            halves = cluster_halves(strip, block + 4, odd)
-            lhs[2 * block + odd] = target_features(halves, origin)
-            centre = jnp.sum(halves[0] + halves[1], axis=1, keepdims=True) * (1.0 / C)
-            left = target_features(halves, centre)
-
-            def store(start, value):
-                held[odd, start : start + CHUNK, :] = value
-
-            weighted(
-                lambda start: left[start : start + CHUNK],
-                source_features(halves, centre),
-                halves[0][3:4],
-                halves[1][3:4],
-                store,
-            )
-            for half in range(2):
-                part = held[odd, half * LANES : (half + 1) * LANES, :]
-                near[pl.ds(2 * (2 * block + odd) + half, 1), :] = kernel_scale * jnp.sum(
-                    part.T, axis=0, keepdims=True
-                )
-        return carry
-
-    lax.fori_loop(0, CLUSTERS // 2, block_step, 0)
-
-
-def near_kernel(
-    place,
-    before,
-    strip,
-    after,
-    lhs,
-    self_rows,
-    near,
-    features,
-    charge,
-    entries_vmem,
-    entries,
-    semaphore,
-    *sums,
-):
-    wide_index = place[0]
-    narrow_index = place[1]
-
-    def put_source(slot, halves, origin):
-        features[slot] = source_features(halves, origin)
-        for half in range(2):
-            row = halves[half][3:4]
-            charge[slot, :, half * LANES : (half + 1) * LANES] = jnp.broadcast_to(row, (8, LANES))
-
-    base = (wide_index * GROUP + narrow_index * CLUSTERS + 1).astype(f32)
+def kernel_sums(square, charge_low, charge_high):
+    inverse = lax.rsqrt(jnp.maximum(square, soft_square))
+    return inverse[:, :LANES] * charge_low + inverse[:, LANES:] * charge_high
+
+
+def put_source(features, charge, slot, halves, origin):
+    features[slot] = source_features(halves, origin)
+    for half in range(2):
+        row = halves[half][3:4]
+        charge[slot, :, half * LANES : (half + 1) * LANES] = jnp.broadcast_to(row, (8, LANES))
+
+
+def pair_rows(refs):
     targets, sources = [], []
-    for ref in (before, strip, after):
+    for ref in refs:
         for block in range(3):
             start = PAIR_ROW + 8 * block
             targets.append(ref[start : start + 1, :])
-            sources.append(ref[start : start + 1 + 1, :][1:2])
-    nothing = jnp.zeros((6, LANES), f32)
-    own_ids = jnp.concatenate(sources + [targets[4]] + [nothing], axis=0)
-    other_ids = jnp.concatenate(targets + [sources[4]] + [nothing], axis=0)
+            sources.append(ref[start + 1 : start + 2, :])
+    return targets, sources
+
+
+def list_entries(place, own_rows, other_rows, inner, out):
+    wide_index = place[0]
+    narrow_index = place[1]
+    count_rows = len(own_rows)
+    base = (wide_index * GROUP + narrow_index * CLUSTERS + 1).astype(f32)
+    nothing = [jnp.zeros((16 - count_rows, LANES), f32)]
+    own_ids = jnp.concatenate(own_rows + nothing, axis=0)
+    other_ids = jnp.concatenate(other_rows + nothing, axis=0)
     local = own_ids - base
-    used = (local >= 0.0) & (local < CLUSTERS) & (own_ids > 0.0)
-    count = used.astype(f32)
-    upto = as_bf16(iota((LANES, LANES), 0) <= iota((LANES, LANES), 1))
-    inclusive = jnp.dot(count.astype(bf16), upto, preferred_element_type=f32)
-    totals = jnp.sum(count, axis=1, keepdims=True)
-    row_of = iota((16, LANES), 0)
-    offset = jnp.zeros((16, LANES), f32)
-    for row in range(10):
-        offset = jnp.where(row_of > row, offset + totals[row : row + 1], offset)
-    spot = inclusive - count + offset
     other = other_ids - 1.0
     group = jnp.floor(other * (1.0 / GROUP))
     rest = other - GROUP * group
@@ -293,21 +241,35 @@
     column = rest - WIDTH * depth
     group_step = group - (wide_index - 1).astype(f32)
     depth_step = depth - (2 * narrow_index - 1).astype(f32)
-    window = group_step * STRIP_CLUSTERS + depth_step * WIDTH + column
-    window = jnp.where(used, window, 0.0)
+    slot = depth_step * WIDTH + column
+    if inner:
+        wanted = group_step == 1.0
+    else:
+        wanted = group_step != 1.0
+        slot = jnp.where(group_step > 1.0, slot + STRIP_CLUSTERS, slot)
+    used = wanted & (local >= 0.0) & (local < CLUSTERS) & (own_ids > 0.0)
+    count = used.astype(f32)
+    upto = as_bf16(iota((LANES, LANES), 0) <= iota((LANES, LANES), 1))
+    inclusive = jnp.dot(count.astype(bf16), upto, preferred_element_type=f32)
+    totals = jnp.sum(count, axis=1, keepdims=True)
+    row_of = iota((16, LANES), 0)
+    offset = jnp.zeros((16, LANES), f32)
+    for row in range(count_rows):
+        offset = jnp.where(row_of > row, offset + totals[row : row + 1], offset)
+    spot = jnp.where(used, inclusive - count + offset, -1.0)
+    slot = jnp.where(used, slot, 0.0)
     local = jnp.where(used, local, 0.0)
-    spot = jnp.where(used, spot, -1.0)
     spot_high = jnp.floor(spot * (1.0 / LANES))
     spot_low = spot - LANES * spot_high
     listed = jnp.zeros((16, LANES), f32)
     eight = iota((8, LANES), 0).astype(f32)
     tall = iota((LANES, LANES), 0).astype(f32)
-    for row in range(10):
+    for row in range(count_rows):
         here = eight == spot_high[row : row + 1]
         values = jnp.concatenate(
             [
                 jnp.where(here, local[row : row + 1], 0.0),
-                jnp.where(here, window[row : row + 1], 0.0),
+                jnp.where(here, slot[row : row + 1], 0.0),
             ],
             axis=0,
         ).astype(bf16)
@@ -316,28 +278,10 @@
             values, hot, (((1,), (1,)), ((), ())), preferred_element_type=f32
         )
     coded = listed[:8] * float(GROUP) + listed[8:]
-    coded = jnp.where(eight == 7.0, jnp.sum(totals), coded)
-    entries_vmem[...] = coded.astype(i32)
-    copy = pltpu.make_async_copy(entries_vmem, entries, semaphore)
-    copy.start()
-
-    for total in sums:
-        total[...] = jnp.zeros(total.shape, f32)
-    origin = own_origin(strip, 64)
-
-    def window_block(block, carry):
-        for part, ref in enumerate((before, strip, after)):
-            for odd in range(2):
-                put_source(
-                    part * STRIP_CLUSTERS + 2 * block + odd, cluster_halves(ref, block, odd), origin
-                )
-        return carry
-
-    lax.fori_loop(0, STRIP_CLUSTERS // 2, window_block, 0)
-    features[DUMMY] = jnp.zeros((DEPTH, C), bf16)
-    charge[DUMMY] = jnp.zeros((8, C), f32)
-
-    copy.wait()
+    out[...] = jnp.where(eight == 7.0, jnp.sum(totals), coded).astype(i32)
+
+
+def add_pairs(entries, lhs, features, charge, dummy, sums):
     pair_total = entries[7, 0]
 
     def pair_steps(first, turns, carry):
@@ -346,18 +290,17 @@
             code = entries[index >> 7, index & (LANES - 1)]
             live = index < pair_total
             cluster = jnp.where(live, code >> 7, 0)
-            slot = jnp.where(live, code & (LANES - 1), DUMMY)
-
-            def add(start, value):
-                sums[turn % SUMS][cluster, start : start + CHUNK, :] += value
-
-            weighted(
-                lambda start: lhs[cluster, start : start + CHUNK, :],
-                features[slot],
-                charge[slot, 0:1, 0:LANES],
-                charge[slot, 0:1, LANES:C],
-                add,
-            )
+            slot = jnp.where(live, code & (LANES - 1), dummy)
+            right = features[slot]
+            charge_low = charge[slot, 0:1, 0:LANES]
+            charge_high = charge[slot, 0:1, LANES:C]
+            for start in range(0, C, CHUNK):
+                square = jnp.dot(
+                    lhs[cluster, start : start + CHUNK, :], right, preferred_element_type=f32
+                )
+                sums[turn % SUMS][cluster, start : start + CHUNK, :] += kernel_sums(
+                    square, charge_low, charge_high
+                )
         return carry
 
     steps = (pair_total + UNROLL - 1) // UNROLL
@@ -368,16 +311,114 @@
         2 * (steps // 2), steps, lambda step, carry: pair_steps(UNROLL * step, UNROLL, carry), 0
     )
 
+
+def summed_row(sums, cluster, half):
+    rows = slice(half * LANES, (half + 1) * LANES)
+    total = sums[0][cluster, rows, :] + sums[1][cluster, rows, :]
+    return kernel_scale * jnp.sum(total.T, axis=0, keepdims=True)
+
+
+def inner_kernel(
+    place, strip, lhs, near, features, charge, listed, entries, semaphore, *rest
+):
+    first_sum, second_sum, own_lhs = rest
+    targets, sources = pair_rows((strip,))
+    list_entries(place, sources + [targets[1]], targets + [sources[1]], True, listed)
+    copy = pltpu.make_async_copy(listed, entries, semaphore)
+    copy.start()
+    origin = own_origin(strip, 64)
+
+    def own_step(block, carry):
+        for odd in range(2):
+            cluster = 2 * block + odd
+            halves = cluster_halves(strip, block + 4, odd)
+            for half, column in enumerate(target_features(halves, origin)):
+                lhs[cluster, half * LANES : (half + 1) * LANES, :] = column.T.astype(bf16)
+            centre = jnp.sum(halves[0] + halves[1], axis=1, keepdims=True) * (1.0 / C)
+            for half, column in enumerate(target_features(halves, centre)):
+                own_lhs[cluster, :, half * LANES : (half + 1) * LANES] = column.astype(bf16)
+            put_source(features, charge, SELF + cluster, halves, centre)
+        return carry
+
+    lax.fori_loop(0, CLUSTERS // 2, own_step, 0, unroll=4)
+
+    def strip_step(block, carry):
+        for odd in range(2):
+            put_source(features, charge, 2 * block + odd, cluster_halves(strip, block, odd), origin)
+        return carry
+
+    lax.fori_loop(0, STRIP_CLUSTERS // 2, strip_step, 0, unroll=2)
+    features[STRIP_CLUSTERS] = jnp.zeros((DEPTH, C), bf16)
+    charge[STRIP_CLUSTERS] = jnp.zeros((8, C), f32)
+
+    def self_step(step, carry):
+        for turn in range(UNROLL):
+            cluster = step * UNROLL + turn
+            square = lax.dot_general(
+                own_lhs[cluster],
+                features[SELF + cluster],
+                (((0,), (0,)), ((), ())),
+                preferred_element_type=f32,
+            )
+            first_sum[cluster] = kernel_sums(
+                square,
+                charge[SELF + cluster, 0:1, 0:LANES],
+                charge[SELF + cluster, 0:1, LANES:C],
+            )
+            second_sum[cluster] = jnp.zeros((C, LANES), f32)
+        return carry
+
+    lax.fori_loop(0, CLUSTERS // UNROLL, self_step, 0)
+    copy.wait()
+    add_pairs(entries, lhs, features, charge, STRIP_CLUSTERS, (first_sum, second_sum))
     for cluster in range(CLUSTERS):
         for half in range(2):
-            rows = slice(half * LANES, (half + 1) * LANES)
-            total = sums[0][cluster, rows, :]
-            for turn in range(1, SUMS):
-                total = total + sums[turn][cluster, rows, :]
             row = 2 * cluster + half
-            near[row : row + 1, :] = self_rows[row : row + 1, :] + kernel_scale * jnp.sum(
-                total.T, axis=0, keepdims=True
-            )
+            near[row : row + 1, :] = summed_row((first_sum, second_sum), cluster, half)
+
+
+def outer_kernel(
+    place,
+    before,
+    strip,
+    after,
+    lhs,
+    inner,
+    near,
+    features,
+    charge,
+    listed,
+    entries,
+    semaphore,
+    *sums,
+):
+    targets, sources = pair_rows((before, after))
+    own_targets, own_sources = pair_rows((strip,))
+    list_entries(
+        place, sources + [own_targets[1]], targets + [own_sources[1]], False, listed
+    )
+    copy = pltpu.make_async_copy(listed, entries, semaphore)
+    copy.start()
+    for total in sums:
+        total[...] = jnp.zeros(total.shape, f32)
+    origin = own_origin(strip, 64)
+
+    def window_step(block, carry):
+        for part, ref in enumerate((before, after)):
+            for odd in range(2):
+                slot = part * STRIP_CLUSTERS + 2 * block + odd
+                put_source(features, charge, slot, cluster_halves(ref, block, odd), origin)
+        return carry
+
+    lax.fori_loop(0, STRIP_CLUSTERS // 2, window_step, 0, unroll=2)
+    features[OUTER] = jnp.zeros((DEPTH, C), bf16)
+    charge[OUTER] = jnp.zeros((8, C), f32)
+    copy.wait()
+    add_pairs(entries, lhs, features, charge, OUTER, sums)
+    for cluster in range(CLUSTERS):
+        for half in range(2):
+            row = 2 * cluster + half
+            near[row : row + 1, :] = inner[row : row + 1, :] + summed_row(sums, cluster, half)
 
 
 def far_kernel(
@@ -532,31 +573,34 @@
         )(skels, from_down, own, from_up, top_message)
     before = lax.ppermute(strip, "wide", [(i, i + 1) for i in range(wide_size - 1)])
     after = lax.ppermute(strip, "wide", [(i + 1, i) for i in range(wide_size - 1)])
-    with jax.named_scope("self"):
-        lhs, self_rows = pl.pallas_call(
-            self_kernel,
+    def near_scratch(slots):
+        return [
+            pltpu.VMEM((slots, DEPTH, C), bf16),
+            pltpu.VMEM((slots, 8, C), f32),
+            pltpu.VMEM((8, LANES), i32),
+            pltpu.SMEM((8, LANES), i32),
+            pltpu.SemaphoreType.DMA(()),
+        ] + [pltpu.VMEM((CLUSTERS, C, LANES), f32)] * SUMS
+
+    with jax.named_scope("inner"):
+        lhs, inner = pl.pallas_call(
+            inner_kernel,
             out_shape=(shape((CLUSTERS, C, DEPTH), bf16), shape((ROWS, LANES), f32)),
-            in_specs=[vmem()],
+            in_specs=[smem(), vmem()],
             out_specs=[vmem()] * 2,
-            scratch_shapes=[pltpu.VMEM((2, C, LANES), f32)],
+            scratch_shapes=near_scratch(SELF + CLUSTERS)
+            + [pltpu.VMEM((CLUSTERS, DEPTH, C), bf16)],
             compiler_params=params,
-        )(strip)
-    with jax.named_scope("near"):
+        )(place, strip)
+    with jax.named_scope("outer"):
         near = pl.pallas_call(
-            near_kernel,
+            outer_kernel,
             out_shape=shape((ROWS, LANES), f32),
             in_specs=[smem()] + [vmem()] * 5,
             out_specs=vmem(),
-            scratch_shapes=[
-                pltpu.VMEM((WINDOW + 1, DEPTH, C), bf16),
-                pltpu.VMEM((WINDOW + 1, 8, C), f32),
-                pltpu.VMEM((8, LANES), i32),
-                pltpu.SMEM((8, LANES), i32),
-                pltpu.SemaphoreType.DMA(()),
-            ]
-            + [pltpu.VMEM((CLUSTERS, C, LANES), f32)] * SUMS,
+            scratch_shapes=near_scratch(OUTER + 1),
             compiler_params=params,
-        )(place, before, strip, after, lhs, self_rows)
+        )(place, before, strip, after, lhs, inner)
     with jax.named_scope("far"):
         potential = pl.pallas_call(
             far_kernel,

time: 58.4 us -> 56.7 us (0.971)
  the two profiles are of different devices: /device:TPU:120 before, /device:TPU:66 now
where the time goes in v6:
time: 56.7 us; the launch traced here: 56.3 us
  starting transfers between devices  36.4 us (64%)
  Pallas kernels  18.3 us (32%)
  between operations  1.47 us (3%)
    all_to_all x1, starting transfers between devices, local(): tops = lax.all_to_all(top_message, 'wide', 0, 0, tiled=True)  17.9 us
    pallas_call x1, Pallas kernels, local(): pl.pallas_call(outer_kernel, out_shape=shape((ROWS, LANES), f32), in_spec...  6.02 us
    pallas_call x1, Pallas kernels, local(): pl.pallas_call(inner_kernel, out_shape=(shape((CLUSTERS, C, DEPTH), bf16)...  5.2 us
    all_to_all x1, starting transfers between devices, local(): skels = lax.all_to_all(skel, 'narrow', 0, 0, tiled=True)  4.97 us
    ppermute x1, starting transfers between devices, local(): lax.ppermute(strip, 'wide', [(i + 1, i) for i in range(wide_size - 1)])  4.58 us
    ppermute x1, starting transfers between devices, local(): lax.ppermute(own, 'narrow', [(i + 1, i) for i in range(narrow_size - 1)])  3.51 us
    ppermute x1, starting transfers between devices, local(): lax.ppermute(strip, 'wide', [(i, i + 1) for i in range(wide_size - 1)])  3.37 us
    pallas_call x1, Pallas kernels, local(): pl.pallas_call(slots_kernel, out_shape=(shape((136, LANES), f32), shape((...  3.03 us
  transfers between devices with their start and end apart: 6, of which 0 were waited for; matrix products, arithmetic and copies ran while one was open for 0% of the time, Pallas kernels for 23%

profile of v6, /device:TPU:66, one launch (start us, length us, event | category | flops | bytes accessed | tf_op | source)
XLA Modules:
  0.0 56.3 jit_solution(13525834363785490596)
XLA Ops:
  0.7 3.0 %slots.1 = (f32[136,128]{1,0:T(8,128)}, f32[8,24,128]{2,1,0:T(8,128)}) custom-call(s32[1]{0:T(128)S(6)} %copy.13.near_count, s32[32,128]{1,0:T(8,128)} %bitcast.8, f32[3,4096]{1,0:T(4,128)} %refs_1_.1, f32[32,128]{1,0:T(8,128)} %bitcast.10, s32[2,64]{1,0:T(2,128)} %refs_3_.1, f32[32,4096]{1,0:T(8,128)} %refs_4_.1, f32[32,512]{1,0:T(8,128)} %refs_5_.1, ...), custom_call_target="tpu_custom_call" | custom-call | tf_op jit(solution)/shard_map/slots/pallas_call | solution.py:542
  3.7 5.0 %all-to-all-start = ((f32[8,24,128]{2,1,0:T(8,128)}), f32[8,24,128]{2,1,0:T(8,128)S(1)}, u32[]{:S(2)}, u32[]{:S(2)}) async-start(f32[8,24,128]{2,1,0:T(8,128)} %get-tuple-element.9), calls=%async_computation | async-start | bytes 196608 | tf_op jit(solution)/shard_map/all_to_all | solution.py:554
  8.7 2.0 %collective-permute-start = (f32[136,128]{1,0:T(8,128)S(1)}, f32[136,128]{1,0:T(8,128)S(1)}, u32[]{:S(2)}, u32[]{:S(2)}) collective-permute-start(f32[136,128]{1,0:T(8,128)S(1)} %copy-done.1), channel_id=1, source_target_pairs={{0,1},{1,2},{2,3},{3,4},{4,5},{5,6},{6,7},{8,9},{9,10},{10,11},{11... | collective-permute-start | bytes 208904 | tf_op jit(solution)/shard_map/ppermute | solution.py:555
  10.7 3.5 %collective-permute-start.1 = (f32[136,128]{1,0:T(8,128)S(1)}, f32[136,128]{1,0:T(8,128)S(1)}, u32[]{:S(2)}, u32[]{:S(2)}) collective-permute-start(f32[136,128]{1,0:T(8,128)S(1)} %copy-done.1), channel_id=1, source_target_pairs={{1,0},{2,1},{3,2},{4,3},{5,4},{6,5},{7,6},{9,8},{10,9},{11,10},{12... | collective-permute-start | bytes 208904 | tf_op jit(solution)/shard_map/ppermute | solution.py:556
  14.2 0.0 all-to-all-done.skels
  14.3 0.6 %top.1.top_message = f32[128,128]{1,0:T(8,128)} custom-call(f32[8,24,128]{2,1,0:T(8,128)S(1)} %all-to-all-done.skels), custom_call_target="tpu_custom_call" | custom-call | tf_op jit(solution)/shard_map/top/pallas_call | solution.py:558
  14.9 17.9 %all-to-all-start.1 = ((f32[64,2,128]{2,1,0:T(2,128)}), f32[64,2,128]{2,1,0:T(2,128)S(1)}, u32[]{:S(2)}, u32[]{:S(2)}) async-start(f32[64,2,128]{2,1,0:T(2,128)} %bitcast.4), calls=%async_computation.1 | async-start | bytes 131072 | tf_op jit(solution)/shard_map/all_to_all | solution.py:565
  32.8 0.0 collective-permute-done.from_down
  32.8 0.0 collective-permute-done.1.from_up
  32.9 0.9 %strip.1 = f32[408,128]{1,0:T(8,128)S(1)} custom-call(f32[8,24,128]{2,1,0:T(8,128)S(1)} %all-to-all-done.skels, f32[136,128]{1,0:T(8,128)S(1)} %collective-permute-done.from_down, f32[136,128]{1,0:T(8,128)S(1)} %copy-done.1, f32[136,128]{1,0:T(8,128)S(1)} %collective-permute-done.1.from_up, f32[128,128]{1,0:T(8,128)} %top.1.top_message), custom_call_target="tpu_custom_call" | custom-call | tf_op jit(solution)/shard_map/strip/pallas_call | solution.py:567
  33.7 3.4 %collective-permute-start.2 = (f32[408,128]{1,0:T(8,128)S(1)}, f32[408,128]{1,0:T(8,128)S(1)}, u32[]{:S(2)}, u32[]{:S(2)}) collective-permute-start(f32[408,128]{1,0:T(8,128)S(1)} %strip.1), channel_id=1, source_target_pairs={{0,8},{8,16},{16,24},{24,32},{32,40},{40,48},{48,56},{56,64},{64,7... | collective-permute-start | bytes 626696 | tf_op jit(solution)/shard_map/ppermute | solution.py:574
  37.1 4.6 %collective-permute-start.3 = (f32[408,128]{1,0:T(8,128)S(1)}, f32[408,128]{1,0:T(8,128)S(1)}, u32[]{:S(2)}, u32[]{:S(2)}) collective-permute-start(f32[408,128]{1,0:T(8,128)S(1)} %strip.1), channel_id=1, source_target_pairs={{8,0},{16,8},{24,16},{32,24},{40,32},{48,40},{56,48},{64,56},{72,6... | collective-permute-start | bytes 626696 | tf_op jit(solution)/shard_map/ppermute | solution.py:575
  42.4 0.1 pad_add_fusion.place
  42.4 5.2 %inner.1 = (bf16[16,256,48]{2,1,0:T(8,128)(2,1)S(1)}, f32[32,128]{1,0:T(8,128)S(1)}) custom-call(s32[2]{0:T(128)S(1)} %pad_add_fusion.place, f32[408,128]{1,0:T(8,128)S(1)} %strip.1), custom_call_target="tpu_custom_call" | custom-call | tf_op jit(solution)/shard_map/inner/pallas_call | solution.py:586
  47.7 0.0 collective-permute-done.2.before
  47.7 0.0 collective-permute-done.3.after
  47.7 0.0 copy-start
  47.7 0.0 copy-start.2
  47.7 0.0 copy-start.3
  47.7 6.0 %outer.1.near = f32[32,128]{1,0:T(8,128)S(1)} custom-call(s32[2]{0:T(128)S(1)} %pad_add_fusion.place, f32[408,128]{1,0:T(8,128)S(1)} %collective-permute-done.2.before, f32[408,128]{1,0:T(8,128)S(1)} %strip.1, f32[408,128]{1,0:T(8,128)S(1)} %collective-permute-done.3.after, bf16[16,256,48]{2,1,0:T(8,128)(2,1)S(1)} %get-tuple-element.11.lhs, ...), custom_call_target="tpu_custom_call" | custom-call | tf_op jit(solution)/shard_map/outer/pallas_call | solution.py:596
  53.7 0.0 all-to-all-done.1
  53.7 0.0 copy-done
  53.8 0.0 copy-done.2
  53.8 2.5 %far.1 = f32[32,128]{1,0:T(8,128)} custom-call(s32[2]{0:T(128)S(1)} %pad_add_fusion.place, s32[1]{0:T(128)S(6)} %copy.14.far_count, f32[408,128]{1,0:T(8,128)S(1)} %collective-permute-done.2.before, f32[408,128]{1,0:T(8,128)S(1)} %strip.1, f32[408,128]{1,0:T(8,128)S(1)} %collective-permute-done.3.after, f32[128,128]{1,0:T(8,128)S(1)} %bitcast.7, ...), custom_call_target="tpu_custom_call" | custom-call | tf_op jit(solution)/shard_map/far/pallas_call | solution.py:605
  (3 shorter events, 0.0 us)
Async XLA Ops:
  3.7 5.0 %copy-start.1 = (f32[136,128]{1,0:T(8,128)S(1)}, f32[136,128]{1,0:T(8,128)}, u32[]{:S(2)}) copy-start(f32[136,128]{1,0:T(8,128)} %get-tuple-element.10.own) | copy-start | bytes 208900
  3.7 10.5 %all-to-all-start = ((f32[8,24,128]{2,1,0:T(8,128)}), f32[8,24,128]{2,1,0:T(8,128)S(1)}, u32[]{:S(2)}, u32[]{:S(2)}) async-start(f32[8,24,128]{2,1,0:T(8,128)} %get-tuple-element.9), calls=%async_computation | async-start | bytes 196608 | tf_op jit(solution)/shard_map/all_to_all | solution.py:554
  8.7 24.2 %collective-permute-start = (f32[136,128]{1,0:T(8,128)S(1)}, f32[136,128]{1,0:T(8,128)S(1)}, u32[]{:S(2)}, u32[]{:S(2)}) collective-permute-start(f32[136,128]{1,0:T(8,128)S(1)} %copy-done.1), channel_id=1, source_target_pairs={{0,1},{1,2},{2,3},{3,4},{4,5},{5,6},{6,7},{8,9},{9,10},{10,11},{11... | collective-permute-start | bytes 208904 | tf_op jit(solution)/shard_map/ppermute | solution.py:555
  10.7 22.1 %collective-permute-start.1 = (f32[136,128]{1,0:T(8,128)S(1)}, f32[136,128]{1,0:T(8,128)S(1)}, u32[]{:S(2)}, u32[]{:S(2)}) collective-permute-start(f32[136,128]{1,0:T(8,128)S(1)} %copy-done.1), channel_id=1, source_target_pairs={{1,0},{2,1},{3,2},{4,3},{5,4},{6,5},{7,6},{9,8},{10,9},{11,10},{12... | collective-permute-start | bytes 208904 | tf_op jit(solution)/shard_map/ppermute | solution.py:556
  14.9 38.8 %all-to-all-start.1 = ((f32[64,2,128]{2,1,0:T(2,128)}), f32[64,2,128]{2,1,0:T(2,128)S(1)}, u32[]{:S(2)}, u32[]{:S(2)}) async-start(f32[64,2,128]{2,1,0:T(2,128)} %bitcast.4), calls=%async_computation.1 | async-start | bytes 131072 | tf_op jit(solution)/shard_map/all_to_all | solution.py:565
  33.7 13.9 %collective-permute-start.2 = (f32[408,128]{1,0:T(8,128)S(1)}, f32[408,128]{1,0:T(8,128)S(1)}, u32[]{:S(2)}, u32[]{:S(2)}) collective-permute-start(f32[408,128]{1,0:T(8,128)S(1)} %strip.1), channel_id=1, source_target_pairs={{0,8},{8,16},{16,24},{24,32},{32,40},{40,48},{48,56},{56,64},{64,7... | collective-permute-start | bytes 626696 | tf_op jit(solution)/shard_map/ppermute | solution.py:574
  37.1 10.5 %collective-permute-start.3 = (f32[408,128]{1,0:T(8,128)S(1)}, f32[408,128]{1,0:T(8,128)S(1)}, u32[]{:S(2)}, u32[]{:S(2)}) collective-permute-start(f32[408,128]{1,0:T(8,128)S(1)} %strip.1), channel_id=1, source_target_pairs={{8,0},{16,8},{24,16},{32,24},{40,32},{48,40},{56,48},{64,56},{72,6... | collective-permute-start | bytes 626696 | tf_op jit(solution)/shard_map/ppermute | solution.py:575
  47.7 6.1 %copy-start = (f32[32,4096]{1,0:T(8,128)S(1)}, f32[32,4096]{1,0:T(8,128)}, u32[]{:S(2)}) copy-start(f32[32,4096]{1,0:T(8,128)} %target_basis.1) | copy-start | bytes 1572868
  47.7 6.1 %copy-start.2 = (s32[4096]{0:T(1024)S(1)}, s32[4096]{0:T(1024)}, u32[]{:S(2)}) copy-start(s32[4096]{0:T(1024)} %param.14) | copy-start | bytes 49156
  47.7 6.1 %copy-start.3 = (s32[3,128]{1,0:T(4,128)S(1)}, s32[3,128]{1,0:T(4,128)}, u32[]{:S(2)}) copy-start(s32[3,128]{1,0:T(4,128)} %far_pairs.1) | copy-start | bytes 4612

commit v7 on v6

--- a/solution.py
+++ b/solution.py
@@ -67,7 +67,8 @@
     ]
     for copy in copies:
         copy.start()
-    order, points, charges, near_pairs, source_basis, transfer, skeleton_points, top_points = held
+    order, points, charges, near_pairs = held[:4]
+    source_basis, transfer, skeleton_points, top_points = held[4:]
     for copy in copies[:4]:
         copy.wait()
     low = order[...] & (LANES - 1)
@@ -226,10 +227,10 @@
 
 
 def list_entries(place, own_rows, other_rows, inner, out):
-    wide_index = place[0]
-    narrow_index = place[1]
+    wide_index = place[0:1, 0:1].astype(f32)
+    narrow_index = place[0:1, 1:2].astype(f32)
     count_rows = len(own_rows)
-    base = (wide_index * GROUP + narrow_index * CLUSTERS + 1).astype(f32)
+    base = wide_index * GROUP + narrow_index * CLUSTERS + 1.0
     nothing = [jnp.zeros((16 - count_rows, LANES), f32)]
     own_ids = jnp.concatenate(own_rows + nothing, axis=0)
     other_ids = jnp.concatenate(other_rows + nothing, axis=0)
@@ -239,14 +240,16 @@
     rest = other - GROUP * group
     depth = jnp.floor(rest * (1.0 / WIDTH))
     column = rest - WIDTH * depth
-    group_step = group - (wide_index - 1).astype(f32)
-    depth_step = depth - (2 * narrow_index - 1).astype(f32)
+    group_step = group - (wide_index - 1.0)
+    depth_step = depth - (2.0 * narrow_index - 1.0)
     slot = depth_step * WIDTH + column
     if inner:
         wanted = group_step == 1.0
     else:
         wanted = group_step != 1.0
-        slot = jnp.where(group_step > 1.0, slot + STRIP_CLUSTERS, slot)
+        odd = wide_index - 2.0 * jnp.floor(0.5 * wide_index)
+        second = jnp.where(group_step > 1.0, 1.0 - odd, odd)
+        slot = slot + STRIP_CLUSTERS * second
     used = wanted & (local >= 0.0) & (local < CLUSTERS) & (own_ids > 0.0)
     count = used.astype(f32)
     upto = as_bf16(iota((LANES, LANES), 0) <= iota((LANES, LANES), 1))
@@ -379,9 +382,9 @@
 
 def outer_kernel(
     place,
-    before,
+    first_strip,
     strip,
-    after,
+    second_strip,
     lhs,
     inner,
     near,
@@ -392,7 +395,7 @@
     semaphore,
     *sums,
 ):
-    targets, sources = pair_rows((before, after))
+    targets, sources = pair_rows((first_strip, second_strip))
     own_targets, own_sources = pair_rows((strip,))
     list_entries(
         place, sources + [own_targets[1]], targets + [own_sources[1]], False, listed
@@ -404,7 +407,7 @@
     origin = own_origin(strip, 64)
 
     def window_step(block, carry):
-        for part, ref in enumerate((before, after)):
+        for part, ref in enumerate((first_strip, second_strip)):
             for odd in range(2):
                 slot = part * STRIP_CLUSTERS + 2 * block + odd
                 put_source(features, charge, slot, cluster_halves(ref, block, odd), origin)
@@ -422,11 +425,11 @@
 
 
 def far_kernel(
+    far_count,
     place,
-    far_count,
-    before,
+    first_strip,
     strip,
-    after,
+    second_strip,
     top,
     far_pairs,
     near,
@@ -435,24 +438,24 @@
     potential,
     total,
 ):
-    wide_index = place[0]
-    narrow_index = place[1]
-    first = wide_index * GROUP + narrow_index * CLUSTERS
-    target = far_pairs[0:1, :] - first
+    group_first = place[0:1, 0:1] * GROUP
+    target = far_pairs[0:1, :] - group_first
     source = far_pairs[1:2, :]
     is_leaf = far_pairs[2:3, :] == 0
     live = iota((1, LANES), 1) < far_count[0]
-    index = jnp.where(is_leaf, source - (wide_index - 1) * GROUP, source + 3 * GROUP)
+    sign = 1 - 2 * (place[0:1, 0:1] & 1)
+    offset = source - group_first
+    leaf = (1 + sign * (offset >> 7)) * GROUP + (offset & (GROUP - 1))
+    index = jnp.where(is_leaf, leaf, source + 3 * GROUP)
     skel = slice(SKEL_ROW, SKEL_ROW + GROUP)
     tops = top[pl.ds(0, top.shape[0] // TOP_ROWS, stride=TOP_ROWS), :]
-    table = jnp.concatenate([before[skel, :], strip[skel, :], after[skel, :], tops], axis=0)
+    table = jnp.concatenate([first_strip[skel, :], strip[skel, :], second_strip[skel, :], tops], axis=0)
     chosen = as_bf16(iota((table.shape[0], LANES), 0) == index)
     over_rows = ((0,), (0,))
     sources = parts_dot(table, chosen, over_rows)
-    own_start = pl.multiple_of(SKEL_ROW + narrow_index * CLUSTERS, 8)
-    own_skel = strip[pl.ds(own_start, CLUSTERS), :]
-    own_chosen = as_bf16(iota((CLUSTERS, LANES), 0) == target)
-    targets = parts_dot(own_skel, own_chosen, over_rows)
+    own_chosen = as_bf16(iota((GROUP, LANES), 0) == target)
+    targets = parts_dot(strip[skel, :], own_chosen, over_rows)
+    target = target - place[0:1, 1:2] * CLUSTERS
     rows = []
     for a in range(R):
         square = soft_square
@@ -525,7 +528,7 @@
 ):
     wide_size = lax.axis_size("wide")
     narrow_size = lax.axis_size("narrow")
-    place = jnp.stack([lax.axis_index("wide"), lax.axis_index("narrow")]).astype(i32)
+    place = jnp.stack([lax.axis_index("wide"), lax.axis_index("narrow")]).astype(i32).reshape(1, 2)
     order = order.reshape(ROWS, LANES)
     shape = jax.ShapeDtypeStruct
     inputs = (
@@ -571,8 +574,10 @@
             out_specs=vmem(),
             compiler_params=params,
         )(skels, from_down, own, from_up, top_message)
-    before = lax.ppermute(strip, "wide", [(i, i + 1) for i in range(wide_size - 1)])
-    after = lax.ppermute(strip, "wide", [(i + 1, i) for i in range(wide_size - 1)])
+    odd_even = [(i, i + 1) for i in range(1, wide_size - 1, 2)]
+    even_odd = [(i, i + 1) for i in range(0, wide_size - 1, 2)]
+    first_strip = lax.ppermute(strip, "wide", odd_even + [(j, i) for i, j in odd_even])
+    second_strip = lax.ppermute(strip, "wide", even_odd + [(j, i) for i, j in even_odd])
     def near_scratch(slots):
         return [
             pltpu.VMEM((slots, DEPTH, C), bf16),
@@ -586,7 +591,7 @@
         lhs, inner = pl.pallas_call(
             inner_kernel,
             out_shape=(shape((CLUSTERS, C, DEPTH), bf16), shape((ROWS, LANES), f32)),
-            in_specs=[smem(), vmem()],
+            in_specs=[vmem()] * 2,
             out_specs=[vmem()] * 2,
             scratch_shapes=near_scratch(SELF + CLUSTERS)
             + [pltpu.VMEM((CLUSTERS, DEPTH, C), bf16)],
@@ -596,20 +601,20 @@
         near = pl.pallas_call(
             outer_kernel,
             out_shape=shape((ROWS, LANES), f32),
-            in_specs=[smem()] + [vmem()] * 5,
+            in_specs=[vmem()] * 6,
             out_specs=vmem(),
             scratch_shapes=near_scratch(OUTER + 1),
             compiler_params=params,
-        )(place, before, strip, after, lhs, inner)
+        )(place, first_strip, strip, second_strip, lhs, inner)
     with jax.named_scope("far"):
         potential = pl.pallas_call(
             far_kernel,
             out_shape=shape((ROWS, LANES), f32),
-            in_specs=[smem(), smem()] + [vmem()] * 8,
+            in_specs=[smem()] + [vmem()] * 9,
             out_specs=vmem(),
             scratch_shapes=[pltpu.VMEM((ROWS, LANES), f32)],
             compiler_params=params,
-        )(place, far_count, before, strip, after, tops, far_pairs, near, order, target_basis)
+        )(far_count, place, first_strip, strip, second_strip, tops, far_pairs, near, order, target_basis)
     return potential.reshape(-1)
 
 

time: 56.7 us -> 54.3 us (0.958)
  the two profiles are of different devices: /device:TPU:66 before, /device:TPU:2 now
where the time goes in v7:
time: 54.3 us; the launch traced here: 53.8 us
  starting transfers between devices  36.1 us (66%)
  Pallas kernels  16.1 us (30%)
  between operations  1.47 us (3%)
    all_to_all x1, starting transfers between devices, local(): tops = lax.all_to_all(top_message, 'wide', 0, 0, tiled=True)  14.4 us
    all_to_all x1, starting transfers between devices, local(): skels = lax.all_to_all(skel, 'narrow', 0, 0, tiled=True)  9.32 us
    ppermute x1, starting transfers between devices, local(): lax.ppermute(strip, 'wide', even_odd + [(j, i) for i, j in even_odd])  6.18 us
    pallas_call x1, Pallas kernels, local(): pl.pallas_call(inner_kernel, out_shape=(shape((CLUSTERS, C, DEPTH), bf16)...  5.08 us
    pallas_call x1, Pallas kernels, local(): pl.pallas_call(outer_kernel, out_shape=shape((ROWS, LANES), f32), in_spec...  4.49 us
    ppermute x1, starting transfers between devices, local(): lax.ppermute(own, 'narrow', [(i + 1, i) for i in range(narrow_size - 1)])  3.51 us
    pallas_call x1, Pallas kernels, local(): pl.pallas_call(slots_kernel, out_shape=(shape((136, LANES), f32), shape((...  3.03 us
    ppermute x1, starting transfers between devices, local(): lax.ppermute(own, 'narrow', [(i, i + 1) for i in range(narrow_size - 1)])  2.05 us
  transfers between devices with their start and end apart: 6, of which 0 were waited for; matrix products, arithmetic and copies ran while one was open for 0% of the time, Pallas kernels for 21%

profile of v7, /device:TPU:2, one launch (start us, length us, event | category | flops | bytes accessed | tf_op | source)
XLA Modules:
  0.0 53.8 jit_solution(2262615806894484671)
XLA Ops:
  0.7 3.0 %slots.1 = (f32[136,128]{1,0:T(8,128)}, f32[8,24,128]{2,1,0:T(8,128)}) custom-call(s32[1]{0:T(128)S(6)} %copy.13.near_count, s32[32,128]{1,0:T(8,128)} %bitcast.10, f32[3,4096]{1,0:T(4,128)} %refs_1_.1, f32[32,128]{1,0:T(8,128)} %bitcast.12, s32[2,64]{1,0:T(2,128)} %refs_3_.1, f32[32,4096]{1,0:T(8,128)} %refs_4_.1, f32[32,512]{1,0:T(8,128)} %refs_5_.1, ...), custom_call_target="tpu_custom_call" | custom-call | tf_op jit(solution)/shard_map/slots/pallas_call | solution.py:545
  3.7 0.0 copy-start.1
  3.7 9.3 %all-to-all-start = ((f32[8,24,128]{2,1,0:T(8,128)}), f32[8,24,128]{2,1,0:T(8,128)S(1)}, u32[]{:S(2)}, u32[]{:S(2)}) async-start(f32[8,24,128]{2,1,0:T(8,128)} %get-tuple-element.9), calls=%async_computation | async-start | bytes 196608 | tf_op jit(solution)/shard_map/all_to_all | solution.py:557
  13.0 0.0 copy-done.1
  13.0 2.0 %collective-permute-start = (f32[136,128]{1,0:T(8,128)S(1)}, f32[136,128]{1,0:T(8,128)S(1)}, u32[]{:S(2)}, u32[]{:S(2)}) collective-permute-start(f32[136,128]{1,0:T(8,128)S(1)} %copy-done.1), channel_id=1, source_target_pairs={{0,1},{1,2},{2,3},{3,4},{4,5},{5,6},{6,7},{8,9},{9,10},{10,11},{11... | collective-permute-start | bytes 208904 | tf_op jit(solution)/shard_map/ppermute | solution.py:558
  15.1 3.5 %collective-permute-start.1 = (f32[136,128]{1,0:T(8,128)S(1)}, f32[136,128]{1,0:T(8,128)S(1)}, u32[]{:S(2)}, u32[]{:S(2)}) collective-permute-start(f32[136,128]{1,0:T(8,128)S(1)} %copy-done.1), channel_id=1, source_target_pairs={{1,0},{2,1},{3,2},{4,3},{5,4},{6,5},{7,6},{9,8},{10,9},{11,10},{12... | collective-permute-start | bytes 208904 | tf_op jit(solution)/shard_map/ppermute | solution.py:559
  18.6 0.0 all-to-all-done.skels
  18.6 0.6 %top.1.top_message = f32[128,128]{1,0:T(8,128)} custom-call(f32[8,24,128]{2,1,0:T(8,128)S(1)} %all-to-all-done.skels), custom_call_target="tpu_custom_call" | custom-call | tf_op jit(solution)/shard_map/top/pallas_call | solution.py:561
  19.2 14.4 %all-to-all-start.1 = ((f32[64,2,128]{2,1,0:T(2,128)}), f32[64,2,128]{2,1,0:T(2,128)S(1)}, u32[]{:S(2)}, u32[]{:S(2)}) async-start(f32[64,2,128]{2,1,0:T(2,128)} %bitcast.5), calls=%async_computation.1 | async-start | bytes 131072 | tf_op jit(solution)/shard_map/all_to_all | solution.py:568
  33.6 0.0 collective-permute-done.from_down
  33.6 0.0 collective-permute-done.1.from_up
  33.7 0.9 %strip.1 = f32[408,128]{1,0:T(8,128)S(1)} custom-call(f32[8,24,128]{2,1,0:T(8,128)S(1)} %all-to-all-done.skels, f32[136,128]{1,0:T(8,128)S(1)} %collective-permute-done.from_down, f32[136,128]{1,0:T(8,128)S(1)} %copy-done.1, f32[136,128]{1,0:T(8,128)S(1)} %collective-permute-done.1.from_up, f32[128,128]{1,0:T(8,128)} %top.1.top_message), custom_call_target="tpu_custom_call" | custom-call | tf_op jit(solution)/shard_map/strip/pallas_call | solution.py:570
  34.5 0.7 %collective-permute-start.2 = (f32[408,128]{1,0:T(8,128)S(1)}, f32[408,128]{1,0:T(8,128)S(1)}, u32[]{:S(2)}, u32[]{:S(2)}) collective-permute-start(f32[408,128]{1,0:T(8,128)S(1)} %strip.1), channel_id=1, source_target_pairs={{8,16},{24,32},{40,48},{56,64},{72,80},{88,96},{104,112},{120,128}... | collective-permute-start | bytes 626696 | tf_op jit(solution)/shard_map/ppermute | solution.py:579
  35.2 6.2 %collective-permute-start.3 = (f32[408,128]{1,0:T(8,128)S(1)}, f32[408,128]{1,0:T(8,128)S(1)}, u32[]{:S(2)}, u32[]{:S(2)}) collective-permute-start(f32[408,128]{1,0:T(8,128)S(1)} %strip.1), channel_id=1, source_target_pairs={{0,8},{16,24},{32,40},{48,56},{64,72},{80,88},{96,104},{112,120},{... | collective-permute-start | bytes 626696 | tf_op jit(solution)/shard_map/ppermute | solution.py:580
  42.1 0.1 add_bitcast_fusion.place
  42.1 5.1 %inner.1 = (bf16[16,256,48]{2,1,0:T(8,128)(2,1)S(1)}, f32[32,128]{1,0:T(8,128)S(1)}) custom-call(s32[1,2]{1,0:T(1,128)S(1)} %add_bitcast_fusion.place, f32[408,128]{1,0:T(8,128)S(1)} %strip.1), custom_call_target="tpu_custom_call" | custom-call | tf_op jit(solution)/shard_map/inner/pallas_call | solution.py:591
  47.2 0.0 collective-permute-done.2.first_strip
  47.2 0.0 collective-permute-done.3.second_strip
  47.2 0.0 copy-start
  47.3 0.0 copy-start.2
  47.3 0.0 copy-start.3
  47.3 4.5 %outer.1.near = f32[32,128]{1,0:T(8,128)S(1)} custom-call(s32[1,2]{1,0:T(1,128)S(1)} %add_bitcast_fusion.place, f32[408,128]{1,0:T(8,128)S(1)} %collective-permute-done.2.first_strip, f32[408,128]{1,0:T(8,128)S(1)} %strip.1, f32[408,128]{1,0:T(8,128)S(1)} %collective-permute-done.3.second_strip, bf16[16,256,48]{2,1,0:T(8,128)(2,1)S(1)} %get-tuple-element.11.lhs, ...), custom_call_target="tpu_custom_call" | custom-call | tf_op jit(solution)/shard_map/outer/pallas_call | solution.py:601
  51.8 0.0 all-to-all-done.1
  51.8 2.0 %far.1 = f32[32,128]{1,0:T(8,128)} custom-call(s32[1]{0:T(128)S(6)} %copy.14.far_count, s32[1,2]{1,0:T(1,128)S(1)} %add_bitcast_fusion.place, f32[408,128]{1,0:T(8,128)S(1)} %collective-permute-done.2.first_strip, f32[408,128]{1,0:T(8,128)S(1)} %strip.1, f32[408,128]{1,0:T(8,128)S(1)} %collective-permute-done.3.second_strip, f32[128,128]{1,0:T(8,128)S(1)} %bitcast.9, ...), custom_call_target="tpu_custom_call" | custom-call | tf_op jit(solution)/shard_map/far/pallas_call | solution.py:610
  (3 shorter events, 0.0 us)
Async XLA Ops:
  3.7 9.3 %copy-start.1 = (f32[136,128]{1,0:T(8,128)S(1)}, f32[136,128]{1,0:T(8,128)}, u32[]{:S(2)}) copy-start(f32[136,128]{1,0:T(8,128)} %get-tuple-element.10.own) | copy-start | bytes 208900
  3.7 14.9 %all-to-all-start = ((f32[8,24,128]{2,1,0:T(8,128)}), f32[8,24,128]{2,1,0:T(8,128)S(1)}, u32[]{:S(2)}, u32[]{:S(2)}) async-start(f32[8,24,128]{2,1,0:T(8,128)} %get-tuple-element.9), calls=%async_computation | async-start | bytes 196608 | tf_op jit(solution)/shard_map/all_to_all | solution.py:557
  13.0 20.6 %collective-permute-start = (f32[136,128]{1,0:T(8,128)S(1)}, f32[136,128]{1,0:T(8,128)S(1)}, u32[]{:S(2)}, u32[]{:S(2)}) collective-permute-start(f32[136,128]{1,0:T(8,128)S(1)} %copy-done.1), channel_id=1, source_target_pairs={{0,1},{1,2},{2,3},{3,4},{4,5},{5,6},{6,7},{8,9},{9,10},{10,11},{11... | collective-permute-start | bytes 208904 | tf_op jit(solution)/shard_map/ppermute | solution.py:558
  15.1 18.6 %collective-permute-start.1 = (f32[136,128]{1,0:T(8,128)S(1)}, f32[136,128]{1,0:T(8,128)S(1)}, u32[]{:S(2)}, u32[]{:S(2)}) collective-permute-start(f32[136,128]{1,0:T(8,128)S(1)} %copy-done.1), channel_id=1, source_target_pairs={{1,0},{2,1},{3,2},{4,3},{5,4},{6,5},{7,6},{9,8},{10,9},{11,10},{12... | collective-permute-start | bytes 208904 | tf_op jit(solution)/shard_map/ppermute | solution.py:559
  19.2 32.5 %all-to-all-start.1 = ((f32[64,2,128]{2,1,0:T(2,128)}), f32[64,2,128]{2,1,0:T(2,128)S(1)}, u32[]{:S(2)}, u32[]{:S(2)}) async-start(f32[64,2,128]{2,1,0:T(2,128)} %bitcast.5), calls=%async_computation.1 | async-start | bytes 131072 | tf_op jit(solution)/shard_map/all_to_all | solution.py:568
  34.5 12.7 %collective-permute-start.2 = (f32[408,128]{1,0:T(8,128)S(1)}, f32[408,128]{1,0:T(8,128)S(1)}, u32[]{:S(2)}, u32[]{:S(2)}) collective-permute-start(f32[408,128]{1,0:T(8,128)S(1)} %strip.1), channel_id=1, source_target_pairs={{8,16},{24,32},{40,48},{56,64},{72,80},{88,96},{104,112},{120,128}... | collective-permute-start | bytes 626696 | tf_op jit(solution)/shard_map/ppermute | solution.py:579
  35.2 12.0 %collective-permute-start.3 = (f32[408,128]{1,0:T(8,128)S(1)}, f32[408,128]{1,0:T(8,128)S(1)}, u32[]{:S(2)}, u32[]{:S(2)}) collective-permute-start(f32[408,128]{1,0:T(8,128)S(1)} %strip.1), channel_id=1, source_target_pairs={{0,8},{16,24},{32,40},{48,56},{64,72},{80,88},{96,104},{112,120},{... | collective-permute-start | bytes 626696 | tf_op jit(solution)/shard_map/ppermute | solution.py:580
  47.2 4.5 %copy-start = (f32[32,4096]{1,0:T(8,128)S(1)}, f32[32,4096]{1,0:T(8,128)}, u32[]{:S(2)}) copy-start(f32[32,4096]{1,0:T(8,128)} %target_basis.1) | copy-start | bytes 1572868
  47.3 4.5 %copy-start.2 = (s32[4096]{0:T(1024)S(1)}, s32[4096]{0:T(1024)}, u32[]{:S(2)}) copy-start(s32[4096]{0:T(1024)} %param.14) | copy-start | bytes 49156
  47.3 4.5 %copy-start.3 = (s32[3,128]{1,0:T(4,128)S(1)}, s32[3,128]{1,0:T(4,128)}, u32[]{:S(2)}) copy-start(s32[3,128]{1,0:T(4,128)} %far_pairs.1) | copy-start | bytes 4612

commit v8 on v7

--- a/solution.py
+++ b/solution.py
@@ -380,64 +380,9 @@
             near[row : row + 1, :] = summed_row((first_sum, second_sum), cluster, half)
 
 
-def outer_kernel(
-    place,
-    first_strip,
-    strip,
-    second_strip,
-    lhs,
-    inner,
-    near,
-    features,
-    charge,
-    listed,
-    entries,
-    semaphore,
-    *sums,
-):
-    targets, sources = pair_rows((first_strip, second_strip))
-    own_targets, own_sources = pair_rows((strip,))
-    list_entries(
-        place, sources + [own_targets[1]], targets + [own_sources[1]], False, listed
-    )
-    copy = pltpu.make_async_copy(listed, entries, semaphore)
-    copy.start()
-    for total in sums:
-        total[...] = jnp.zeros(total.shape, f32)
-    origin = own_origin(strip, 64)
-
-    def window_step(block, carry):
-        for part, ref in enumerate((first_strip, second_strip)):
-            for odd in range(2):
-                slot = part * STRIP_CLUSTERS + 2 * block + odd
-                put_source(features, charge, slot, cluster_halves(ref, block, odd), origin)
-        return carry
-
-    lax.fori_loop(0, STRIP_CLUSTERS // 2, window_step, 0, unroll=2)
-    features[OUTER] = jnp.zeros((DEPTH, C), bf16)
-    charge[OUTER] = jnp.zeros((8, C), f32)
-    copy.wait()
-    add_pairs(entries, lhs, features, charge, OUTER, sums)
-    for cluster in range(CLUSTERS):
-        for half in range(2):
-            row = 2 * cluster + half
-            near[row : row + 1, :] = inner[row : row + 1, :] + summed_row(sums, cluster, half)
-
-
-def far_kernel(
-    far_count,
-    place,
-    first_strip,
-    strip,
-    second_strip,
-    top,
-    far_pairs,
-    near,
-    order,
-    target_basis,
-    potential,
-    total,
-):
+def far_rows(far_count, place, strips, top, far_pairs, target_basis, inner, total):
+    first_strip, strip, second_strip = strips
+    tops = top[pl.ds(0, top.shape[0] // TOP_ROWS, stride=TOP_ROWS), :]
     group_first = place[0:1, 0:1] * GROUP
     target = far_pairs[0:1, :] - group_first
     source = far_pairs[1:2, :]
@@ -446,9 +391,9 @@
     sign = 1 - 2 * (place[0:1, 0:1] & 1)
     offset = source - group_first
     leaf = (1 + sign * (offset >> 7)) * GROUP + (offset & (GROUP - 1))
-    index = jnp.where(is_leaf, leaf, source + 3 * GROUP)
+    groups = tops.shape[0]
+    index = jnp.where(is_leaf, leaf, ((source + groups // 2) & (groups - 1)) + 3 * GROUP)
     skel = slice(SKEL_ROW, SKEL_ROW + GROUP)
-    tops = top[pl.ds(0, top.shape[0] // TOP_ROWS, stride=TOP_ROWS), :]
     table = jnp.concatenate([first_strip[skel, :], strip[skel, :], second_strip[skel, :], tops], axis=0)
     chosen = as_bf16(iota((table.shape[0], LANES), 0) == index)
     over_rows = ((0,), (0,))
@@ -473,8 +418,11 @@
         for half in range(2):
             row = 2 * cluster + half
             total[row : row + 1, :] = (
-                near[row : row + 1, :] + spread[:, half * LANES : (half + 1) * LANES]
+                inner[row : row + 1, :] + spread[:, half * LANES : (half + 1) * LANES]
             )
+
+
+def arrival_order(total, order):
     low = order[...] & (LANES - 1)
     high = order[...] >> 7
     tall = iota((LANES, LANES), 0)
@@ -493,7 +441,60 @@
         preferred_element_type=f32,
     )
     out = placed[:ROWS] + placed[ROWS : 2 * ROWS] + placed[2 * ROWS :]
-    potential[...] = out
+    return out
+
+
+def outer_kernel(
+    far_count,
+    place,
+    second_strip,
+    strip,
+    first_strip,
+    lhs,
+    inner,
+    top,
+    far_pairs,
+    order,
+    target_basis,
+    potential,
+    features,
+    charge,
+    listed,
+    entries,
+    semaphore,
+    *rest,
+):
+    *sums, total = rest
+    targets, sources = pair_rows((first_strip, second_strip))
+    own_targets, own_sources = pair_rows((strip,))
+    list_entries(
+        place, sources + [own_targets[1]], targets + [own_sources[1]], False, listed
+    )
+    copy = pltpu.make_async_copy(listed, entries, semaphore)
+    copy.start()
+    for part in sums:
+        part[...] = jnp.zeros(part.shape, f32)
+    strips = (first_strip, strip, second_strip)
+    far_rows(far_count, place, strips, top, far_pairs, target_basis, inner, total)
+    origin = own_origin(strip, 64)
+
+    def window_step(block, carry):
+        for part, ref in enumerate((first_strip, second_strip)):
+            for odd in range(2):
+                slot = part * STRIP_CLUSTERS + 2 * block + odd
+                put_source(features, charge, slot, cluster_halves(ref, block, odd), origin)
+        return carry
+
+    lax.fori_loop(0, STRIP_CLUSTERS // 2, window_step, 0, unroll=2)
+    features[OUTER] = jnp.zeros((DEPTH, C), bf16)
+    charge[OUTER] = jnp.zeros((8, C), f32)
+    copy.wait()
+    add_pairs(entries, lhs, features, charge, OUTER, sums)
+    for cluster in range(CLUSTERS):
+        for half in range(2):
+            row = 2 * cluster + half
+            total[row : row + 1, :] += summed_row(sums, cluster, half)
+    potential[...] = arrival_order(total, order)
 
 
 def smem():
@@ -565,7 +566,10 @@
             out_specs=vmem(),
             compiler_params=params,
         )(skels)
-    tops = lax.all_to_all(top_message, "wide", 0, 0, tiled=True)
+    members = [(i + wide_size // 2) % wide_size for i in range(wide_size)]
+    tops = lax.all_to_all(
+        top_message, "wide", 0, 0, tiled=True, axis_index_groups=[members]
+    )
     with jax.named_scope("strip"):
         strip = pl.pallas_call(
             strip_kernel,
@@ -598,23 +602,26 @@
             compiler_params=params,
         )(place, strip)
     with jax.named_scope("outer"):
-        near = pl.pallas_call(
+        potential = pl.pallas_call(
             outer_kernel,
             out_shape=shape((ROWS, LANES), f32),
-            in_specs=[vmem()] * 6,
+            in_specs=[smem()] + [vmem()] * 10,
             out_specs=vmem(),
-            scratch_shapes=near_scratch(OUTER + 1),
+            scratch_shapes=near_scratch(OUTER + 1) + [pltpu.VMEM((ROWS, LANES), f32)],
             compiler_params=params,
-        )(place, first_strip, strip, second_strip, lhs, inner)
-    with jax.named_scope("far"):
-        potential = pl.pallas_call(
-            far_kernel,
-            out_shape=shape((ROWS, LANES), f32),
-            in_specs=[smem()] + [vmem()] * 9,
-            out_specs=vmem(),
-            scratch_shapes=[pltpu.VMEM((ROWS, LANES), f32)],
-            compiler_params=params,
-        )(far_count, place, first_strip, strip, second_strip, tops, far_pairs, near, order, target_basis)
+        )(
+            far_count,
+            place,
+            second_strip,
+            strip,
+            first_strip,
+            lhs,
+            inner,
+            tops,
+            far_pairs,
+            order,
+            target_basis,
+        )
     return potential.reshape(-1)
 
 

time: 54.3 us -> 57.3 us (1.055)
  the two profiles are of different devices: /device:TPU:2 before, /device:TPU:13 now
where the time goes in v8:
time: 57.3 us; the launch traced here: 56.9 us
  starting transfers between devices  37.4 us (65%)
  Pallas kernels  15.5 us (27%)
  waiting for transfers between devices  1.72 us (3%)
  between operations  1.42 us (2%)
  local copies, waits for them, and re-layouts  0.68 us (1%)
    all_to_all x1, starting transfers between devices, local(): lax.all_to_all(top_message, 'wide', 0, 0, tiled=True, axis_index_groups=[...  21.5 us
    pallas_call x1, Pallas kernels, local(): pl.pallas_call(outer_kernel, out_shape=shape((ROWS, LANES), f32), in_spec...  6.64 us
    all_to_all x1, starting transfers between devices, local(): skels = lax.all_to_all(skel, 'narrow', 0, 0, tiled=True)  5.26 us
    pallas_call x1, Pallas kernels, local(): pl.pallas_call(inner_kernel, out_shape=(shape((CLUSTERS, C, DEPTH), bf16)...  4.35 us
    ppermute x1, starting transfers between devices, local(): lax.ppermute(own, 'narrow', [(i, i + 1) for i in range(narrow_size - 1)])  3.29 us
    ppermute x1, starting transfers between devices, local(): lax.ppermute(strip, 'wide', odd_even + [(j, i) for i, j in odd_even])  3.1 us
    pallas_call x1, Pallas kernels, local(): pl.pallas_call(slots_kernel, out_shape=(shape((136, LANES), f32), shape((...  3.03 us
    ppermute x1, starting transfers between devices, local(): lax.ppermute(own, 'narrow', [(i + 1, i) for i in range(narrow_size - 1)])  2.4 us
  transfers between devices with their start and end apart: 6, of which 1 were waited for; matrix products, arithmetic and copies ran while one was open for 0% of the time, Pallas kernels for 10%

profile of v8, /device:TPU:13, one launch (start us, length us, event | category | flops | bytes accessed | tf_op | source)
XLA Modules:
  0.0 56.9 jit_solution(10735443143666001025)
XLA Ops:
  0.7 3.0 %slots.1 = (f32[136,128]{1,0:T(8,128)}, f32[8,24,128]{2,1,0:T(8,128)}) custom-call(s32[1]{0:T(128)S(6)} %copy.13.near_count, s32[32,128]{1,0:T(8,128)} %bitcast.10, f32[3,4096]{1,0:T(4,128)} %refs_1_.1, f32[32,128]{1,0:T(8,128)} %bitcast.12, s32[2,64]{1,0:T(2,128)} %refs_3_.1, f32[32,4096]{1,0:T(8,128)} %refs_4_.1, f32[32,512]{1,0:T(8,128)} %refs_5_.1, ...), custom_call_target="tpu_custom_call" | custom-call | tf_op jit(solution)/shard_map/slots/pallas_call | solution.py:546
  3.7 0.0 copy-start.1
  3.7 5.3 %all-to-all-start = ((f32[8,24,128]{2,1,0:T(8,128)}), f32[8,24,128]{2,1,0:T(8,128)S(1)}, u32[]{:S(2)}, u32[]{:S(2)}) async-start(f32[8,24,128]{2,1,0:T(8,128)} %get-tuple-element.9), calls=%async_computation | async-start | bytes 196608 | tf_op jit(solution)/shard_map/all_to_all | solution.py:558
  9.0 0.0 copy-done.1
  9.0 0.0 copy-start
  9.0 2.4 %collective-permute-start.1 = (f32[136,128]{1,0:T(8,128)S(1)}, f32[136,128]{1,0:T(8,128)S(1)}, u32[]{:S(2)}, u32[]{:S(2)}) collective-permute-start(f32[136,128]{1,0:T(8,128)S(1)} %copy-done.1), channel_id=1, source_target_pairs={{1,0},{2,1},{3,2},{4,3},{5,4},{6,5},{7,6},{9,8},{10,9},{11,10},{12... | collective-permute-start | bytes 208904 | tf_op jit(solution)/shard_map/ppermute | solution.py:560
  11.4 3.3 %collective-permute-start = (f32[136,128]{1,0:T(8,128)S(1)}, f32[136,128]{1,0:T(8,128)S(1)}, u32[]{:S(2)}, u32[]{:S(2)}) collective-permute-start(f32[136,128]{1,0:T(8,128)S(1)} %copy-done.1), channel_id=1, source_target_pairs={{0,1},{1,2},{2,3},{3,4},{4,5},{5,6},{6,7},{8,9},{9,10},{10,11},{11... | collective-permute-start | bytes 208904 | tf_op jit(solution)/shard_map/ppermute | solution.py:559
  14.7 0.0 all-to-all-done.skels
  14.7 0.6 %top.1.top_message = f32[128,128]{1,0:T(8,128)} custom-call(f32[8,24,128]{2,1,0:T(8,128)S(1)} %all-to-all-done.skels), custom_call_target="tpu_custom_call" | custom-call | tf_op jit(solution)/shard_map/top/pallas_call | solution.py:562
  15.3 21.5 %all-to-all-start.1 = ((f32[64,2,128]{2,1,0:T(2,128)}), f32[64,2,128]{2,1,0:T(2,128)S(1)}, u32[]{:S(2)}, u32[]{:S(2)}) async-start(f32[64,2,128]{2,1,0:T(2,128)} %bitcast.5), calls=%async_computation.1 | async-start | bytes 131072 | tf_op jit(solution)/shard_map/all_to_all | solution.py:570
  36.8 0.0 collective-permute-done.1.from_up
  36.8 0.0 collective-permute-done.from_down
  36.8 0.9 %strip.1 = f32[408,128]{1,0:T(8,128)S(1)} custom-call(f32[8,24,128]{2,1,0:T(8,128)S(1)} %all-to-all-done.skels, f32[136,128]{1,0:T(8,128)S(1)} %collective-permute-done.from_down, f32[136,128]{1,0:T(8,128)S(1)} %copy-done.1, f32[136,128]{1,0:T(8,128)S(1)} %collective-permute-done.1.from_up, f32[128,128]{1,0:T(8,128)} %top.1.top_message), custom_call_target="tpu_custom_call" | custom-call | tf_op jit(solution)/shard_map/strip/pallas_call | solution.py:574
  37.7 3.1 %collective-permute-start.3 = (f32[408,128]{1,0:T(8,128)S(1)}, f32[408,128]{1,0:T(8,128)S(1)}, u32[]{:S(2)}, u32[]{:S(2)}) collective-permute-start(f32[408,128]{1,0:T(8,128)S(1)} %strip.1), channel_id=1, source_target_pairs={{8,16},{24,32},{40,48},{56,64},{72,80},{88,96},{104,112},{120,128}... | collective-permute-start | bytes 626696 | tf_op jit(solution)/shard_map/ppermute | solution.py:583
  40.8 1.9 %collective-permute-start.2 = (f32[408,128]{1,0:T(8,128)S(1)}, f32[408,128]{1,0:T(8,128)S(1)}, u32[]{:S(2)}, u32[]{:S(2)}) collective-permute-start(f32[408,128]{1,0:T(8,128)S(1)} %strip.1), channel_id=1, source_target_pairs={{0,8},{16,24},{32,40},{48,56},{64,72},{80,88},{96,104},{112,120},{... | collective-permute-start | bytes 626696 | tf_op jit(solution)/shard_map/ppermute | solution.py:584
  43.4 0.1 add_bitcast_fusion.place
  43.5 4.3 %inner.1 = (bf16[16,256,48]{2,1,0:T(8,128)(2,1)S(1)}, f32[32,128]{1,0:T(8,128)S(1)}) custom-call(s32[1,2]{1,0:T(1,128)S(1)} %add_bitcast_fusion.place, f32[408,128]{1,0:T(8,128)S(1)} %strip.1), custom_call_target="tpu_custom_call" | custom-call | tf_op jit(solution)/shard_map/inner/pallas_call | solution.py:595
  47.8 0.0 collective-permute-done.3.first_strip
  47.8 1.7 %collective-permute-done.2.second_strip = f32[408,128]{1,0:T(8,128)S(1)} collective-permute-done((f32[408,128]{1,0:T(8,128)S(1)}, f32[408,128]{1,0:T(8,128)S(1)}, u32[]{:S(2)}, u32[]{:S(2)}) %collective-permute-start.2) | collective-permute-done | bytes 208928 | tf_op jit(solution)/shard_map/ppermute | solution.py:584
  49.5 0.0 all-to-all-done.1
  49.5 0.0 copy-done
  49.5 0.0 copy-done.2
  49.6 0.7 %copy-done.3 = s32[3,128]{1,0:T(4,128)S(1)} copy-done((s32[3,128]{1,0:T(4,128)S(1)}, s32[3,128]{1,0:T(4,128)}, u32[]{:S(2)}) %copy-start.3) | copy-done | bytes 1560
  50.2 6.6 %outer.1 = f32[32,128]{1,0:T(8,128)} custom-call(s32[1]{0:T(128)S(6)} %copy.14.far_count, s32[1,2]{1,0:T(1,128)S(1)} %add_bitcast_fusion.place, f32[408,128]{1,0:T(8,128)S(1)} %collective-permute-done.2.second_strip, f32[408,128]{1,0:T(8,128)S(1)} %strip.1, f32[408,128]{1,0:T(8,128)S(1)} %collective-permute-done.3.first_strip, ...), custom_call_target="tpu_custom_call" | custom-call | tf_op jit(solution)/shard_map/outer/pallas_call | solution.py:605
  (2 shorter events, 0.0 us)
Async XLA Ops:
  3.7 5.3 %copy-start.1 = (f32[136,128]{1,0:T(8,128)S(1)}, f32[136,128]{1,0:T(8,128)}, u32[]{:S(2)}) copy-start(f32[136,128]{1,0:T(8,128)} %get-tuple-element.10.own) | copy-start | bytes 208900
  3.7 11.0 %all-to-all-start = ((f32[8,24,128]{2,1,0:T(8,128)}), f32[8,24,128]{2,1,0:T(8,128)S(1)}, u32[]{:S(2)}, u32[]{:S(2)}) async-start(f32[8,24,128]{2,1,0:T(8,128)} %get-tuple-element.9), calls=%async_computation | async-start | bytes 196608 | tf_op jit(solution)/shard_map/all_to_all | solution.py:558
  9.0 40.6 %copy-start = (f32[32,4096]{1,0:T(8,128)S(1)}, f32[32,4096]{1,0:T(8,128)}, u32[]{:S(2)}) copy-start(f32[32,4096]{1,0:T(8,128)} %target_basis.1) | copy-start | bytes 1572868
  9.0 27.8 %collective-permute-start.1 = (f32[136,128]{1,0:T(8,128)S(1)}, f32[136,128]{1,0:T(8,128)S(1)}, u32[]{:S(2)}, u32[]{:S(2)}) collective-permute-start(f32[136,128]{1,0:T(8,128)S(1)} %copy-done.1), channel_id=1, source_target_pairs={{1,0},{2,1},{3,2},{4,3},{5,4},{6,5},{7,6},{9,8},{10,9},{11,10},{12... | collective-permute-start | bytes 208904 | tf_op jit(solution)/shard_map/ppermute | solution.py:560
  11.4 25.4 %collective-permute-start = (f32[136,128]{1,0:T(8,128)S(1)}, f32[136,128]{1,0:T(8,128)S(1)}, u32[]{:S(2)}, u32[]{:S(2)}) collective-permute-start(f32[136,128]{1,0:T(8,128)S(1)} %copy-done.1), channel_id=1, source_target_pairs={{0,1},{1,2},{2,3},{3,4},{4,5},{5,6},{6,7},{8,9},{9,10},{10,11},{11... | collective-permute-start | bytes 208904 | tf_op jit(solution)/shard_map/ppermute | solution.py:559
  15.3 34.2 %all-to-all-start.1 = ((f32[64,2,128]{2,1,0:T(2,128)}), f32[64,2,128]{2,1,0:T(2,128)S(1)}, u32[]{:S(2)}, u32[]{:S(2)}) async-start(f32[64,2,128]{2,1,0:T(2,128)} %bitcast.5), calls=%async_computation.1 | async-start | bytes 131072 | tf_op jit(solution)/shard_map/all_to_all | solution.py:570
  37.7 10.1 %collective-permute-start.3 = (f32[408,128]{1,0:T(8,128)S(1)}, f32[408,128]{1,0:T(8,128)S(1)}, u32[]{:S(2)}, u32[]{:S(2)}) collective-permute-start(f32[408,128]{1,0:T(8,128)S(1)} %strip.1), channel_id=1, source_target_pairs={{8,16},{24,32},{40,48},{56,64},{72,80},{88,96},{104,112},{120,128}... | collective-permute-start | bytes 626696 | tf_op jit(solution)/shard_map/ppermute | solution.py:583
  40.8 8.7 %collective-permute-start.2 = (f32[408,128]{1,0:T(8,128)S(1)}, f32[408,128]{1,0:T(8,128)S(1)}, u32[]{:S(2)}, u32[]{:S(2)}) collective-permute-start(f32[408,128]{1,0:T(8,128)S(1)} %strip.1), channel_id=1, source_target_pairs={{0,8},{16,24},{32,40},{48,56},{64,72},{80,88},{96,104},{112,120},{... | collective-permute-start | bytes 626696 | tf_op jit(solution)/shard_map/ppermute | solution.py:584
  43.5 6.1 %copy-start.2 = (s32[4096]{0:T(1024)S(1)}, s32[4096]{0:T(1024)}, u32[]{:S(2)}) copy-start(s32[4096]{0:T(1024)} %param.14) | copy-start | bytes 49156
  49.5 0.7 %copy-start.3 = (s32[3,128]{1,0:T(4,128)S(1)}, s32[3,128]{1,0:T(4,128)}, u32[]{:S(2)}) copy-start(s32[3,128]{1,0:T(4,128)} %far_pairs.1) | copy-start | bytes 4612

commit v9 on v8

--- a/solution.py
+++ b/solution.py
@@ -58,7 +58,7 @@
 
 
 def slots_kernel(near_count, *refs):
-    count = 8
+    count = 9
     own, skel_out = refs[count : count + 2]
     held = refs[count + 2 : 2 * count + 2]
     semaphores = refs[2 * count + 2]
@@ -67,9 +67,9 @@
     ]
     for copy in copies:
         copy.start()
-    order, points, charges, near_pairs = held[:4]
-    source_basis, transfer, skeleton_points, top_points = held[4:]
-    for copy in copies[:4]:
+    order, points, charges, near_pairs, far_pairs = held[:5]
+    source_basis, transfer, skeleton_points, top_points = held[5:]
+    for copy in copies[:5]:
         copy.wait()
     low = order[...] & (LANES - 1)
     high = order[...] >> 7
@@ -92,9 +92,10 @@
         tiles.append(values)
 
     pairs = jnp.where(iota((2, 64), 1) < near_count[0], near_pairs[...] + 1, 0).astype(f32)
-    own[128:136, :] = jnp.zeros((8, LANES), f32)
+    own[128:144, :] = jnp.zeros((16, LANES), f32)
     own[128:130, 0:64] = pairs
-    for copy in copies[4:]:
+    own[136:139, :] = far_pairs[...].astype(f32)
+    for copy in copies[5:]:
         copy.wait()
 
     lane = iota((R, LANES), 1)
@@ -384,6 +385,7 @@
     first_strip, strip, second_strip = strips
     tops = top[pl.ds(0, top.shape[0] // TOP_ROWS, stride=TOP_ROWS), :]
     group_first = place[0:1, 0:1] * GROUP
+    far_pairs = far_pairs.astype(i32)
     target = far_pairs[0:1, :] - group_first
     source = far_pairs[1:2, :]
     is_leaf = far_pairs[2:3, :] == 0
@@ -391,8 +393,7 @@
     sign = 1 - 2 * (place[0:1, 0:1] & 1)
     offset = source - group_first
     leaf = (1 + sign * (offset >> 7)) * GROUP + (offset & (GROUP - 1))
-    groups = tops.shape[0]
-    index = jnp.where(is_leaf, leaf, ((source + groups // 2) & (groups - 1)) + 3 * GROUP)
+    index = jnp.where(is_leaf, leaf, source + 3 * GROUP)
     skel = slice(SKEL_ROW, SKEL_ROW + GROUP)
     table = jnp.concatenate([first_strip[skel, :], strip[skel, :], second_strip[skel, :], tops], axis=0)
     chosen = as_bf16(iota((table.shape[0], LANES), 0) == index)
@@ -453,7 +454,7 @@
     lhs,
     inner,
     top,
-    far_pairs,
+    own,
     order,
     target_basis,
     potential,
@@ -475,7 +476,7 @@
     for part in sums:
         part[...] = jnp.zeros(part.shape, f32)
     strips = (first_strip, strip, second_strip)
-    far_rows(far_count, place, strips, top, far_pairs, target_basis, inner, total)
+    far_rows(far_count, place, strips, top, own[136:139, :], target_basis, inner, total)
     origin = own_origin(strip, 64)
 
     def window_step(block, carry):
@@ -537,6 +538,7 @@
         points,
         charges.reshape(ROWS, LANES),
         near_pairs,
+        far_pairs,
         source_basis,
         transfer,
         skeleton_points,
@@ -546,7 +548,7 @@
         own, skel = pl.pallas_call(
             slots_kernel,
             out_shape=(
-                shape((136, LANES), f32),
+                shape((144, LANES), f32),
                 shape((NARROW, SKEL_REC, LANES), f32),
             ),
             in_specs=[smem()] + [in_hbm()] * len(inputs),
@@ -566,10 +568,7 @@
             out_specs=vmem(),
             compiler_params=params,
         )(skels)
-    members = [(i + wide_size // 2) % wide_size for i in range(wide_size)]
-    tops = lax.all_to_all(
-        top_message, "wide", 0, 0, tiled=True, axis_index_groups=[members]
-    )
+    tops = lax.all_to_all(top_message, "wide", 0, 0, tiled=True)
     with jax.named_scope("strip"):
         strip = pl.pallas_call(
             strip_kernel,
@@ -618,7 +617,7 @@
             lhs,
             inner,
             tops,
-            far_pairs,
+            own,
             order,
             target_basis,
         )

time: 57.3 us -> 55.5 us (0.969)
  the two profiles are of different devices: /device:TPU:13 before, /device:TPU:37 now
where the time goes in v9:
time: 55.5 us; the launch traced here: 55.1 us
  starting transfers between devices  35 us (63%)
  Pallas kernels  16 us (29%)
  waiting for transfers between devices  2.54 us (5%)
  between operations  1.4 us (3%)
    all_to_all x1, starting transfers between devices, local(): tops = lax.all_to_all(top_message, 'wide', 0, 0, tiled=True)  17.8 us
    pallas_call x1, Pallas kernels, local(): pl.pallas_call(outer_kernel, out_shape=shape((ROWS, LANES), f32), in_spec...  7.38 us
    all_to_all x1, starting transfers between devices, local(): skels = lax.all_to_all(skel, 'narrow', 0, 0, tiled=True)  5.26 us
    ppermute x1, starting transfers between devices, local(): lax.ppermute(strip, 'wide', odd_even + [(j, i) for i, j in odd_even])  4.3 us
    pallas_call x1, Pallas kernels, local(): pl.pallas_call(inner_kernel, out_shape=(shape((CLUSTERS, C, DEPTH), bf16)...  4.07 us
    ppermute x1, starting transfers between devices, local(): lax.ppermute(own, 'narrow', [(i, i + 1) for i in range(narrow_size - 1)])  3.29 us
    pallas_call x1, Pallas kernels, local(): pl.pallas_call(slots_kernel, out_shape=(shape((144, LANES), f32), shape((...  3.05 us
    ppermute x1, starting transfers between devices, local(): lax.ppermute(own, 'narrow', [(i + 1, i) for i in range(narrow_size - 1)])  2.4 us
  transfers between devices with their start and end apart: 6, of which 3 were waited for; matrix products, arithmetic and copies ran while one was open for 0% of the time, Pallas kernels for 10%

profile of v9, /device:TPU:37, one launch (start us, length us, event | category | flops | bytes accessed | tf_op | source)
XLA Modules:
  0.0 55.1 jit_solution(12287388250843321027)
XLA Ops:
  0.7 3.1 %slots.1 = (f32[144,128]{1,0:T(8,128)}, f32[8,24,128]{2,1,0:T(8,128)}) custom-call(s32[1]{0:T(128)S(6)} %copy.13.near_count, s32[32,128]{1,0:T(8,128)} %bitcast.10, f32[3,4096]{1,0:T(4,128)} %refs_1_.1, f32[32,128]{1,0:T(8,128)} %bitcast.12, s32[2,64]{1,0:T(2,128)} %refs_3_.1, s32[3,128]{1,0:T(4,128)} %refs_4_.1, f32[32,4096]{1,0:T(8,128)} %refs_5_.1, ...), custom_call_target="tpu_custom_call" | custom-call | tf_op jit(solution)/shard_map/slots/pallas_call | solution.py:548
  3.7 0.0 copy-start.1
  3.7 5.3 %all-to-all-start = ((f32[8,24,128]{2,1,0:T(8,128)}), f32[8,24,128]{2,1,0:T(8,128)S(1)}, u32[]{:S(2)}, u32[]{:S(2)}) async-start(f32[8,24,128]{2,1,0:T(8,128)} %get-tuple-element.9), calls=%async_computation | async-start | bytes 196608 | tf_op jit(solution)/shard_map/all_to_all | solution.py:560
  9.0 0.0 copy-done.1
  9.0 0.0 copy-start
  9.0 2.4 %collective-permute-start.1 = (f32[144,128]{1,0:T(8,128)S(1)}, f32[144,128]{1,0:T(8,128)S(1)}, u32[]{:S(2)}, u32[]{:S(2)}) collective-permute-start(f32[144,128]{1,0:T(8,128)S(1)} %copy-done.1), channel_id=1, source_target_pairs={{1,0},{2,1},{3,2},{4,3},{5,4},{6,5},{7,6},{9,8},{10,9},{11,10},{12... | collective-permute-start | bytes 221192 | tf_op jit(solution)/shard_map/ppermute | solution.py:562
  11.4 3.3 %collective-permute-start = (f32[144,128]{1,0:T(8,128)S(1)}, f32[144,128]{1,0:T(8,128)S(1)}, u32[]{:S(2)}, u32[]{:S(2)}) collective-permute-start(f32[144,128]{1,0:T(8,128)S(1)} %copy-done.1), channel_id=1, source_target_pairs={{0,1},{1,2},{2,3},{3,4},{4,5},{5,6},{6,7},{8,9},{9,10},{10,11},{11... | collective-permute-start | bytes 221192 | tf_op jit(solution)/shard_map/ppermute | solution.py:561
  14.7 0.0 all-to-all-done.skels
  14.7 0.6 %top.1.top_message = f32[128,128]{1,0:T(8,128)} custom-call(f32[8,24,128]{2,1,0:T(8,128)S(1)} %all-to-all-done.skels), custom_call_target="tpu_custom_call" | custom-call | tf_op jit(solution)/shard_map/top/pallas_call | solution.py:564
  15.3 17.8 %all-to-all-start.1 = ((f32[64,2,128]{2,1,0:T(2,128)}), f32[64,2,128]{2,1,0:T(2,128)S(1)}, u32[]{:S(2)}, u32[]{:S(2)}) async-start(f32[64,2,128]{2,1,0:T(2,128)} %bitcast.5), calls=%async_computation.1 | async-start | bytes 131072 | tf_op jit(solution)/shard_map/all_to_all | solution.py:571
  33.2 0.0 collective-permute-done.1.from_up
  33.2 0.0 collective-permute-done.from_down
  33.2 0.9 %strip.1 = f32[408,128]{1,0:T(8,128)S(1)} custom-call(f32[8,24,128]{2,1,0:T(8,128)S(1)} %all-to-all-done.skels, f32[144,128]{1,0:T(8,128)S(1)} %collective-permute-done.from_down, f32[144,128]{1,0:T(8,128)S(1)} %copy-done.1, f32[144,128]{1,0:T(8,128)S(1)} %collective-permute-done.1.from_up, f32[128,128]{1,0:T(8,128)} %top.1.top_message), custom_call_target="tpu_custom_call" | custom-call | tf_op jit(solution)/shard_map/strip/pallas_call | solution.py:573
  34.1 4.3 %collective-permute-start.3 = (f32[408,128]{1,0:T(8,128)S(1)}, f32[408,128]{1,0:T(8,128)S(1)}, u32[]{:S(2)}, u32[]{:S(2)}) collective-permute-start(f32[408,128]{1,0:T(8,128)S(1)} %strip.1), channel_id=1, source_target_pairs={{8,16},{24,32},{40,48},{56,64},{72,80},{88,96},{104,112},{120,128}... | collective-permute-start | bytes 626696 | tf_op jit(solution)/shard_map/ppermute | solution.py:582
  38.4 1.9 %collective-permute-start.2 = (f32[408,128]{1,0:T(8,128)S(1)}, f32[408,128]{1,0:T(8,128)S(1)}, u32[]{:S(2)}, u32[]{:S(2)}) collective-permute-start(f32[408,128]{1,0:T(8,128)S(1)} %strip.1), channel_id=1, source_target_pairs={{0,8},{16,24},{32,40},{48,56},{64,72},{80,88},{96,104},{112,120},{... | collective-permute-start | bytes 626696 | tf_op jit(solution)/shard_map/ppermute | solution.py:583
  41.0 0.1 add_bitcast_fusion.place
  41.1 0.0 copy-start.2
  41.1 4.1 %inner.1 = (bf16[16,256,48]{2,1,0:T(8,128)(2,1)S(1)}, f32[32,128]{1,0:T(8,128)S(1)}) custom-call(s32[1,2]{1,0:T(1,128)S(1)} %add_bitcast_fusion.place, f32[408,128]{1,0:T(8,128)S(1)} %strip.1), custom_call_target="tpu_custom_call" | custom-call | tf_op jit(solution)/shard_map/inner/pallas_call | solution.py:594
  45.1 1.0 %collective-permute-done.3.first_strip = f32[408,128]{1,0:T(8,128)S(1)} collective-permute-done((f32[408,128]{1,0:T(8,128)S(1)}, f32[408,128]{1,0:T(8,128)S(1)}, u32[]{:S(2)}, u32[]{:S(2)}) %collective-permute-start.3) | collective-permute-done | bytes 208928 | tf_op jit(solution)/shard_map/ppermute | solution.py:582
  46.2 1.1 %collective-permute-done.2.second_strip = f32[408,128]{1,0:T(8,128)S(1)} collective-permute-done((f32[408,128]{1,0:T(8,128)S(1)}, f32[408,128]{1,0:T(8,128)S(1)}, u32[]{:S(2)}, u32[]{:S(2)}) %collective-permute-start.2) | collective-permute-done | bytes 208928 | tf_op jit(solution)/shard_map/ppermute | solution.py:583
  47.3 0.4 all-to-all-done.1
  47.7 0.0 copy-done
  47.7 0.0 copy-done.2
  47.7 7.4 %outer.1 = f32[32,128]{1,0:T(8,128)} custom-call(s32[1]{0:T(128)S(6)} %copy.14.far_count, s32[1,2]{1,0:T(1,128)S(1)} %add_bitcast_fusion.place, f32[408,128]{1,0:T(8,128)S(1)} %collective-permute-done.2.second_strip, f32[408,128]{1,0:T(8,128)S(1)} %strip.1, f32[408,128]{1,0:T(8,128)S(1)} %collective-permute-done.3.first_strip, ...), custom_call_target="tpu_custom_call" | custom-call | tf_op jit(solution)/shard_map/outer/pallas_call | solution.py:604
Async XLA Ops:
  3.7 5.3 %copy-start.1 = (f32[144,128]{1,0:T(8,128)S(1)}, f32[144,128]{1,0:T(8,128)}, u32[]{:S(2)}) copy-start(f32[144,128]{1,0:T(8,128)} %get-tuple-element.10.own) | copy-start | bytes 221188
  3.7 11.0 %all-to-all-start = ((f32[8,24,128]{2,1,0:T(8,128)}), f32[8,24,128]{2,1,0:T(8,128)S(1)}, u32[]{:S(2)}, u32[]{:S(2)}) async-start(f32[8,24,128]{2,1,0:T(8,128)} %get-tuple-element.9), calls=%async_computation | async-start | bytes 196608 | tf_op jit(solution)/shard_map/all_to_all | solution.py:560
  9.0 38.7 %copy-start = (f32[32,4096]{1,0:T(8,128)S(1)}, f32[32,4096]{1,0:T(8,128)}, u32[]{:S(2)}) copy-start(f32[32,4096]{1,0:T(8,128)} %target_basis.1) | copy-start | bytes 1572868
  9.0 24.2 %collective-permute-start.1 = (f32[144,128]{1,0:T(8,128)S(1)}, f32[144,128]{1,0:T(8,128)S(1)}, u32[]{:S(2)}, u32[]{:S(2)}) collective-permute-start(f32[144,128]{1,0:T(8,128)S(1)} %copy-done.1), channel_id=1, source_target_pairs={{1,0},{2,1},{3,2},{4,3},{5,4},{6,5},{7,6},{9,8},{10,9},{11,10},{12... | collective-permute-start | bytes 221192 | tf_op jit(solution)/shard_map/ppermute | solution.py:562
  11.4 21.8 %collective-permute-start = (f32[144,128]{1,0:T(8,128)S(1)}, f32[144,128]{1,0:T(8,128)S(1)}, u32[]{:S(2)}, u32[]{:S(2)}) collective-permute-start(f32[144,128]{1,0:T(8,128)S(1)} %copy-done.1), channel_id=1, source_target_pairs={{0,1},{1,2},{2,3},{3,4},{4,5},{5,6},{6,7},{8,9},{9,10},{10,11},{11... | collective-permute-start | bytes 221192 | tf_op jit(solution)/shard_map/ppermute | solution.py:561
  15.3 32.3 %all-to-all-start.1 = ((f32[64,2,128]{2,1,0:T(2,128)}), f32[64,2,128]{2,1,0:T(2,128)S(1)}, u32[]{:S(2)}, u32[]{:S(2)}) async-start(f32[64,2,128]{2,1,0:T(2,128)} %bitcast.5), calls=%async_computation.1 | async-start | bytes 131072 | tf_op jit(solution)/shard_map/all_to_all | solution.py:571
  34.1 12.1 %collective-permute-start.3 = (f32[408,128]{1,0:T(8,128)S(1)}, f32[408,128]{1,0:T(8,128)S(1)}, u32[]{:S(2)}, u32[]{:S(2)}) collective-permute-start(f32[408,128]{1,0:T(8,128)S(1)} %strip.1), channel_id=1, source_target_pairs={{8,16},{24,32},{40,48},{56,64},{72,80},{88,96},{104,112},{120,128}... | collective-permute-start | bytes 626696 | tf_op jit(solution)/shard_map/ppermute | solution.py:582
  38.4 8.9 %collective-permute-start.2 = (f32[408,128]{1,0:T(8,128)S(1)}, f32[408,128]{1,0:T(8,128)S(1)}, u32[]{:S(2)}, u32[]{:S(2)}) collective-permute-start(f32[408,128]{1,0:T(8,128)S(1)} %strip.1), channel_id=1, source_target_pairs={{0,8},{16,24},{32,40},{48,56},{64,72},{80,88},{96,104},{112,120},{... | collective-permute-start | bytes 626696 | tf_op jit(solution)/shard_map/ppermute | solution.py:583
  41.1 6.6 %copy-start.2 = (s32[4096]{0:T(1024)S(1)}, s32[4096]{0:T(1024)}, u32[]{:S(2)}) copy-start(s32[4096]{0:T(1024)} %param.14) | copy-start | bytes 49156

commit v10 on v7

--- a/solution.py
+++ b/solution.py
@@ -15,7 +15,7 @@
 WIDTH = 8
 STRIP_CLUSTERS = 32
 PAIR_ROW = 8 * STRIP_CLUSTERS
-SKEL_ROW = PAIR_ROW + 24
+SKEL_ROW = PAIR_ROW + 8
 STRIP_ROWS = SKEL_ROW + GROUP
 SKEL_REC = 24
 TOP_ROWS = 2
@@ -142,14 +142,15 @@
     top_message[...] = jnp.broadcast_to(row, top_message.shape)
 
 
-def strip_kernel(skels, from_down, own, from_up, top_message, strip):
+def strip_kernel(place, skels, chip_own, own, next_own, top_message, strip):
     del top_message
-    strip[0:64, :] = from_down[64:128, :]
+    odd = (place[0:1, 1:2] & 1) == 1
+    strip[0:64, :] = jnp.where(odd, chip_own[64:128, :], next_own[64:128, :])
     strip[64:192, :] = own[0:128, :]
-    strip[192:256, :] = from_up[0:64, :]
-    strip[PAIR_ROW : PAIR_ROW + 8, :] = from_down[128:136, :]
-    strip[PAIR_ROW + 8 : PAIR_ROW + 16, :] = own[128:136, :]
-    strip[PAIR_ROW + 16 : PAIR_ROW + 24, :] = from_up[128:136, :]
+    strip[192:256, :] = jnp.where(odd, next_own[0:64, :], chip_own[0:64, :])
+    pairs = [ref[128:130, :] for ref in (chip_own, own, next_own)]
+    pairs.append(jnp.zeros((2, LANES), f32))
+    strip[PAIR_ROW : PAIR_ROW + 8, :] = jnp.concatenate(pairs, axis=0)
     for device in range(NARROW):
         start = SKEL_ROW + device * CLUSTERS
         strip[start : start + CLUSTERS, :] = skels[device, :CLUSTERS, :]
@@ -220,7 +221,7 @@
     targets, sources = [], []
     for ref in refs:
         for block in range(3):
-            start = PAIR_ROW + 8 * block
+            start = PAIR_ROW + 2 * block
             targets.append(ref[start : start + 1, :])
             sources.append(ref[start + 1 : start + 2, :])
     return targets, sources
@@ -555,8 +556,10 @@
             compiler_params=first_params,
         )(near_count, *inputs)
     skels = lax.all_to_all(skel, "narrow", 0, 0, tiled=True)
-    from_down = lax.ppermute(own, "narrow", [(i, i + 1) for i in range(narrow_size - 1)])
-    from_up = lax.ppermute(own, "narrow", [(i + 1, i) for i in range(narrow_size - 1)])
+    in_chip = [(i, i + 1) for i in range(0, narrow_size - 1, 2)]
+    next_chip = [(i, i + 1) for i in range(1, narrow_size - 1, 2)]
+    chip_own = lax.ppermute(own, "narrow", in_chip + [(j, i) for i, j in in_chip])
+    next_own = lax.ppermute(own, "narrow", next_chip + [(j, i) for i, j in next_chip])
     with jax.named_scope("top"):
         top_message = pl.pallas_call(
             top_kernel,
@@ -570,10 +573,10 @@
         strip = pl.pallas_call(
             strip_kernel,
             out_shape=shape((STRIP_ROWS, LANES), f32),
-            in_specs=[vmem()] * 5,
+            in_specs=[vmem()] * 6,
             out_specs=vmem(),
             compiler_params=params,
-        )(skels, from_down, own, from_up, top_message)
+        )(place, skels, chip_own, own, next_own, top_message)
     odd_even = [(i, i + 1) for i in range(1, wide_size - 1, 2)]
     even_odd = [(i, i + 1) for i in range(0, wide_size - 1, 2)]
     first_strip = lax.ppermute(strip, "wide", odd_even + [(j, i) for i, j in odd_even])

time: 54.3 us -> 54.5 us (level)
  the two profiles are of different devices: /device:TPU:2 before, /device:TPU:32 now
where the time goes in v10:
time: 54.5 us; the launch traced here: 53.8 us
  starting transfers between devices  32.6 us (60%)
  Pallas kernels  16.1 us (30%)
  waiting for transfers between devices  3.55 us (7%)
  between operations  1.42 us (3%)
    all_to_all x1, starting transfers between devices, local(): tops = lax.all_to_all(top_message, 'wide', 0, 0, tiled=True)  18.4 us
    pallas_call x1, Pallas kernels, local(): pl.pallas_call(inner_kernel, out_shape=(shape((CLUSTERS, C, DEPTH), bf16)...  4.79 us
    pallas_call x1, Pallas kernels, local(): pl.pallas_call(outer_kernel, out_shape=shape((ROWS, LANES), f32), in_spec...  4.78 us
    ppermute x1, starting transfers between devices, local(): lax.ppermute(strip, 'wide', odd_even + [(j, i) for i, j in odd_even])  4.57 us
    all_to_all x1, starting transfers between devices, local(): skels = lax.all_to_all(skel, 'narrow', 0, 0, tiled=True)  4.44 us
    pallas_call x1, Pallas kernels, local(): pl.pallas_call(slots_kernel, out_shape=(shape((136, LANES), f32), shape((...  3.03 us
    all_to_all x1, waiting for transfers between devices, local(): skels = lax.all_to_all(skel, 'narrow', 0, 0, tiled=True)  2.71 us
    ppermute x1, starting transfers between devices, local(): lax.ppermute(own, 'narrow', in_chip + [(j, i) for i, j in in_chip])  2.4 us
  transfers between devices with their start and end apart: 6, of which 2 were waited for; matrix products, arithmetic and copies ran while one was open for 0% of the time, Pallas kernels for 21%

profile of v10, /device:TPU:32, one launch (start us, length us, event | category | flops | bytes accessed | tf_op | source)
XLA Modules:
  0.0 53.8 jit_solution(3327023417757002896)
XLA Ops:
  0.7 3.0 %slots.1 = (f32[136,128]{1,0:T(8,128)}, f32[8,24,128]{2,1,0:T(8,128)}) custom-call(s32[1]{0:T(128)S(6)} %copy.13.near_count, s32[32,128]{1,0:T(8,128)} %bitcast.10, f32[3,4096]{1,0:T(4,128)} %refs_1_.1, f32[32,128]{1,0:T(8,128)} %bitcast.12, s32[2,64]{1,0:T(2,128)} %refs_3_.1, f32[32,4096]{1,0:T(8,128)} %refs_4_.1, f32[32,512]{1,0:T(8,128)} %refs_5_.1, ...), custom_call_target="tpu_custom_call" | custom-call | tf_op jit(solution)/shard_map/slots/pallas_call | solution.py:546
  3.7 0.0 copy-start.1
  3.7 4.4 %all-to-all-start = ((f32[8,24,128]{2,1,0:T(8,128)}), f32[8,24,128]{2,1,0:T(8,128)S(1)}, u32[]{:S(2)}, u32[]{:S(2)}) async-start(f32[8,24,128]{2,1,0:T(8,128)} %get-tuple-element.9), calls=%async_computation | async-start | bytes 196608 | tf_op jit(solution)/shard_map/all_to_all | solution.py:558
  8.1 0.0 copy-done.1
  8.2 2.4 %collective-permute-start = (f32[136,128]{1,0:T(8,128)S(1)}, f32[136,128]{1,0:T(8,128)S(1)}, u32[]{:S(2)}, u32[]{:S(2)}) collective-permute-start(f32[136,128]{1,0:T(8,128)S(1)} %copy-done.1), channel_id=1, source_target_pairs={{0,1},{2,3},{4,5},{6,7},{1,0},{3,2},{5,4},{7,6},{8,9},{10,11},{12,... | collective-permute-start | bytes 208904 | tf_op jit(solution)/shard_map/ppermute | solution.py:561
  10.6 0.7 %collective-permute-start.1 = (f32[136,128]{1,0:T(8,128)S(1)}, f32[136,128]{1,0:T(8,128)S(1)}, u32[]{:S(2)}, u32[]{:S(2)}) collective-permute-start(f32[136,128]{1,0:T(8,128)S(1)} %copy-done.1), channel_id=1, source_target_pairs={{1,2},{3,4},{5,6},{2,1},{4,3},{6,5},{9,10},{11,12},{13,14},{10,9},... | collective-permute-start | bytes 208904 | tf_op jit(solution)/shard_map/ppermute | solution.py:562
  11.2 2.7 %all-to-all-done.skels = f32[8,24,128]{2,1,0:T(8,128)S(1)} async-done(((f32[8,24,128]{2,1,0:T(8,128)}), f32[8,24,128]{2,1,0:T(8,128)S(1)}, u32[]{:S(2)}, u32[]{:S(2)}) %all-to-all-start) | async-done | bytes 98336 | tf_op jit(solution)/shard_map/all_to_all | solution.py:558
  13.9 0.6 %top.1.top_message = f32[128,128]{1,0:T(8,128)} custom-call(f32[8,24,128]{2,1,0:T(8,128)S(1)} %all-to-all-done.skels), custom_call_target="tpu_custom_call" | custom-call | tf_op jit(solution)/shard_map/top/pallas_call | solution.py:564
  14.6 18.4 %all-to-all-start.1 = ((f32[64,2,128]{2,1,0:T(2,128)}), f32[64,2,128]{2,1,0:T(2,128)S(1)}, u32[]{:S(2)}, u32[]{:S(2)}) async-start(f32[64,2,128]{2,1,0:T(2,128)} %bitcast.5), calls=%async_computation.1 | async-start | bytes 131072 | tf_op jit(solution)/shard_map/all_to_all | solution.py:571
  33.0 0.1 add_bitcast_fusion.place
  33.1 0.0 collective-permute-done.chip_own
  33.1 0.0 collective-permute-done.1.next_own
  33.1 0.9 %strip.1 = f32[392,128]{1,0:T(8,128)S(1)} custom-call(s32[1,2]{1,0:T(1,128)S(1)} %add_bitcast_fusion.place, f32[8,24,128]{2,1,0:T(8,128)S(1)} %all-to-all-done.skels, f32[136,128]{1,0:T(8,128)S(1)} %collective-permute-done.chip_own, f32[136,128]{1,0:T(8,128)S(1)} %copy-done.1, f32[136,128]{1,0:T(8,128)S(1)} %collective-permute-done.1.next_own, ...), custom_call_target="tpu_custom_call" | custom-call | tf_op jit(solution)/shard_map/strip/pallas_call | solution.py:573
  34.0 4.6 %collective-permute-start.2 = (f32[392,128]{1,0:T(8,128)S(1)}, f32[392,128]{1,0:T(8,128)S(1)}, u32[]{:S(2)}, u32[]{:S(2)}) collective-permute-start(f32[392,128]{1,0:T(8,128)S(1)} %strip.1), channel_id=1, source_target_pairs={{8,16},{24,32},{40,48},{56,64},{72,80},{88,96},{104,112},{120,128}... | collective-permute-start | bytes 602120 | tf_op jit(solution)/shard_map/ppermute | solution.py:582
  38.6 2.2 %collective-permute-start.3 = (f32[392,128]{1,0:T(8,128)S(1)}, f32[392,128]{1,0:T(8,128)S(1)}, u32[]{:S(2)}, u32[]{:S(2)}) collective-permute-start(f32[392,128]{1,0:T(8,128)S(1)} %strip.1), channel_id=1, source_target_pairs={{0,8},{16,24},{32,40},{48,56},{64,72},{80,88},{96,104},{112,120},{... | collective-permute-start | bytes 602120 | tf_op jit(solution)/shard_map/ppermute | solution.py:583
  41.4 4.8 %inner.1 = (bf16[16,256,48]{2,1,0:T(8,128)(2,1)S(1)}, f32[32,128]{1,0:T(8,128)S(1)}) custom-call(s32[1,2]{1,0:T(1,128)S(1)} %add_bitcast_fusion.place, f32[392,128]{1,0:T(8,128)S(1)} %strip.1), custom_call_target="tpu_custom_call" | custom-call | tf_op jit(solution)/shard_map/inner/pallas_call | solution.py:594
  46.2 0.0 collective-permute-done.2.first_strip
  46.2 0.8 %collective-permute-done.3.second_strip = f32[392,128]{1,0:T(8,128)S(1)} collective-permute-done((f32[392,128]{1,0:T(8,128)S(1)}, f32[392,128]{1,0:T(8,128)S(1)}, u32[]{:S(2)}, u32[]{:S(2)}) %collective-permute-start.3) | collective-permute-done | bytes 200736 | tf_op jit(solution)/shard_map/ppermute | solution.py:583
  47.0 4.8 %outer.1.near = f32[32,128]{1,0:T(8,128)S(1)} custom-call(s32[1,2]{1,0:T(1,128)S(1)} %add_bitcast_fusion.place, f32[392,128]{1,0:T(8,128)S(1)} %collective-permute-done.2.first_strip, f32[392,128]{1,0:T(8,128)S(1)} %strip.1, f32[392,128]{1,0:T(8,128)S(1)} %collective-permute-done.3.second_strip, bf16[16,256,48]{2,1,0:T(8,128)(2,1)S(1)} %get-tuple-element.11.lhs, ...), custom_call_target="tpu_custom_call" | custom-call | tf_op jit(solution)/shard_map/outer/pallas_call | solution.py:604
  51.8 0.0 all-to-all-done.1
  51.8 0.0 copy-done
  51.8 0.0 copy-done.2
  51.8 0.0 copy-done.3
  51.9 2.0 %far.1 = f32[32,128]{1,0:T(8,128)} custom-call(s32[1]{0:T(128)S(6)} %copy.14.far_count, s32[1,2]{1,0:T(1,128)S(1)} %add_bitcast_fusion.place, f32[392,128]{1,0:T(8,128)S(1)} %collective-permute-done.2.first_strip, f32[392,128]{1,0:T(8,128)S(1)} %strip.1, f32[392,128]{1,0:T(8,128)S(1)} %collective-permute-done.3.second_strip, f32[128,128]{1,0:T(8,128)S(1)} %bitcast.9, ...), custom_call_target="tpu_custom_call" | custom-call | tf_op jit(solution)/shard_map/far/pallas_call | solution.py:613
  (3 shorter events, 0.0 us)
Async XLA Ops:
  3.7 4.5 %copy-start.1 = (f32[136,128]{1,0:T(8,128)S(1)}, f32[136,128]{1,0:T(8,128)}, u32[]{:S(2)}) copy-start(f32[136,128]{1,0:T(8,128)} %get-tuple-element.10.own) | copy-start | bytes 208900
  3.7 10.2 %all-to-all-start = ((f32[8,24,128]{2,1,0:T(8,128)}), f32[8,24,128]{2,1,0:T(8,128)S(1)}, u32[]{:S(2)}, u32[]{:S(2)}) async-start(f32[8,24,128]{2,1,0:T(8,128)} %get-tuple-element.9), calls=%async_computation | async-start | bytes 196608 | tf_op jit(solution)/shard_map/all_to_all | solution.py:558
  8.2 24.9 %collective-permute-start = (f32[136,128]{1,0:T(8,128)S(1)}, f32[136,128]{1,0:T(8,128)S(1)}, u32[]{:S(2)}, u32[]{:S(2)}) collective-permute-start(f32[136,128]{1,0:T(8,128)S(1)} %copy-done.1), channel_id=1, source_target_pairs={{0,1},{2,3},{4,5},{6,7},{1,0},{3,2},{5,4},{7,6},{8,9},{10,11},{12,... | collective-permute-start | bytes 208904 | tf_op jit(solution)/shard_map/ppermute | solution.py:561
  10.6 22.5 %collective-permute-start.1 = (f32[136,128]{1,0:T(8,128)S(1)}, f32[136,128]{1,0:T(8,128)S(1)}, u32[]{:S(2)}, u32[]{:S(2)}) collective-permute-start(f32[136,128]{1,0:T(8,128)S(1)} %copy-done.1), channel_id=1, source_target_pairs={{1,2},{3,4},{5,6},{2,1},{4,3},{6,5},{9,10},{11,12},{13,14},{10,9},... | collective-permute-start | bytes 208904 | tf_op jit(solution)/shard_map/ppermute | solution.py:562
  14.6 37.2 %all-to-all-start.1 = ((f32[64,2,128]{2,1,0:T(2,128)}), f32[64,2,128]{2,1,0:T(2,128)S(1)}, u32[]{:S(2)}, u32[]{:S(2)}) async-start(f32[64,2,128]{2,1,0:T(2,128)} %bitcast.5), calls=%async_computation.1 | async-start | bytes 131072 | tf_op jit(solution)/shard_map/all_to_all | solution.py:571
  34.0 12.2 %collective-permute-start.2 = (f32[392,128]{1,0:T(8,128)S(1)}, f32[392,128]{1,0:T(8,128)S(1)}, u32[]{:S(2)}, u32[]{:S(2)}) collective-permute-start(f32[392,128]{1,0:T(8,128)S(1)} %strip.1), channel_id=1, source_target_pairs={{8,16},{24,32},{40,48},{56,64},{72,80},{88,96},{104,112},{120,128}... | collective-permute-start | bytes 602120 | tf_op jit(solution)/shard_map/ppermute | solution.py:582
  38.6 8.5 %collective-permute-start.3 = (f32[392,128]{1,0:T(8,128)S(1)}, f32[392,128]{1,0:T(8,128)S(1)}, u32[]{:S(2)}, u32[]{:S(2)}) collective-permute-start(f32[392,128]{1,0:T(8,128)S(1)} %strip.1), channel_id=1, source_target_pairs={{0,8},{16,24},{32,40},{48,56},{64,72},{80,88},{96,104},{112,120},{... | collective-permute-start | bytes 602120 | tf_op jit(solution)/shard_map/ppermute | solution.py:583
  47.0 4.8 %copy-start = (f32[32,4096]{1,0:T(8,128)S(1)}, f32[32,4096]{1,0:T(8,128)}, u32[]{:S(2)}) copy-start(f32[32,4096]{1,0:T(8,128)} %target_basis.1) | copy-start | bytes 1572868
  47.0 4.8 %copy-start.2 = (s32[4096]{0:T(1024)S(1)}, s32[4096]{0:T(1024)}, u32[]{:S(2)}) copy-start(s32[4096]{0:T(1024)} %param.14) | copy-start | bytes 49156
  47.0 4.8 %copy-start.3 = (s32[3,128]{1,0:T(4,128)S(1)}, s32[3,128]{1,0:T(4,128)}, u32[]{:S(2)}) copy-start(s32[3,128]{1,0:T(4,128)} %far_pairs.1) | copy-start | bytes 4612
